TPU v7x, 128 devices: a whole 4x4x4 slice. The times are simulated.
128 devices in a mesh: chan: 32 (over y, z, core), freq: 4 (over x).
Axes of the slice: x: 4, y: 4, z: 4, core: 2. Of those that a mesh axis runs over, the one named last changes fastest.
Arguments:
- records: bfloat16 [32768, 2, 8192], P('chan', None, 'freq'), may hold values from -400 to 400
- chan_pos: int32 [32768], replicated, may hold values from 0 to 511
- bin_row: int32 [512], replicated, may hold values from 0 to 511, each once
- pair_mask: int32 [32, 2], P('chan'), may hold values from 0 to 1, as said below
Outputs:
- traces: float32 [512, 1024], P('chan', 'freq')
Inputs may be any that keep to these rules, and one draw needn't show every extreme that they name: `pair_mask`: 1 pairs receiver block i with virtual-source block i - j - 1; entries whose source block would be negative are ignored; the last receiver block pairs with all 2 of its sources.
All inputs are finite; a program needn't handle non-finite values.
Results may differ from a plain program's by a relative error of at most 0.0041.
Values may be sent and summed in bfloat16 or wider, within the bound.
No kernel may reach another device: no remote copies, remote signals or barrier semaphores. Data moves between devices by JAX's collectives and lax.ppermute only.
A program may use at most 192 MiB of HBM per device.

v0:
```python
import math

import jax
import jax.numpy as jnp
from jax import lax
from jax.sharding import PartitionSpec as P

NF = 8192
LAGS = 1024


water = 0.5
tiny = 1e-06


def passed_along(block, axis, distance):
    devices = range(lax.axis_size(axis))
    route = [(i - distance, i) for i in devices if i - distance in devices]
    return lax.ppermute(block, axis, route)


def lag_table(first, count, lag_count, full):
    freqs = first + jnp.arange(count, dtype=jnp.int32)
    lagvec = jnp.arange(lag_count, dtype=jnp.int32) - lag_count // 2
    phase = jnp.mod(freqs[:, None] * lagvec[None, :], 2 * full)
    theta = 2.0 * math.pi / (2 * full) * phase.astype(jnp.float32)
    scale = 1.0 / math.sqrt(full)
    return jnp.concatenate([jnp.cos(theta) * scale, -jnp.sin(theta) * scale], axis=0)


def shards(records, chan_pos, bin_row, pair_mask):
    here = lax.axis_index("chan")
    width = records.shape[0]
    band = records.shape[2]
    reach = pair_mask.shape[1]
    bins = bin_row.shape[0]
    rec = records.astype(jnp.float32)
    power = rec[:, 0] * rec[:, 0] + rec[:, 1] * rec[:, 1]
    total = lax.psum(jnp.sum(power, axis=1), "freq")
    level = water * total / NF + tiny
    whitened = (rec / (power + level[:, None])[:, None, :]).astype(jnp.bfloat16)
    own_pos = lax.dynamic_slice_in_dim(chan_pos, here * width, width)
    bin_ids = jnp.arange(bins, dtype=jnp.int32)
    stack = jnp.zeros((bins, 2 * band), jnp.float32)
    current = whitened
    for step in range(reach):
        current = passed_along(current, "chan", 1)
        source = here - step - 1
        src_pos = lax.dynamic_slice_in_dim(chan_pos, jnp.maximum(source, 0) * width, width)
        offset = jnp.abs(own_pos - src_pos)
        usable = (source >= 0) & (pair_mask[0, step] > 0)
        target = jnp.sum(
            jnp.where(offset[:, None] == bin_ids[None, :], bin_row[None, :], 0), axis=1
        )
        onehot = ((bin_ids[:, None] == target[None, :]) & usable).astype(jnp.bfloat16)
        wsrc = current.astype(jnp.float32)
        prod_re = rec[:, 0] * wsrc[:, 0] + rec[:, 1] * wsrc[:, 1]
        prod_im = rec[:, 1] * wsrc[:, 0] - rec[:, 0] * wsrc[:, 1]
        prods = jnp.stack([prod_re, prod_im], axis=1).astype(jnp.bfloat16).reshape(width, 2 * band)
        stack = stack + jnp.dot(onehot, prods, preferred_element_type=jnp.float32)
    table = lag_table(lax.axis_index("freq") * band, band, LAGS, NF)
    lagged = jnp.dot(stack, table, precision=lax.Precision.HIGHEST)
    partial_lags = lax.psum_scatter(lagged, "freq", scatter_dimension=1, tiled=True)
    traces = lax.psum_scatter(partial_lags, "chan", scatter_dimension=0, tiled=True)
    return traces


def solution(mesh):
    placed = (P("chan", None, "freq"), P(), P(), P("chan", None))
    return jax.shard_map(
        shards, mesh=mesh, in_specs=placed, out_specs=P("chan", "freq"), check_vma=False
    )
```

profile of v0, /device:TPU:0, one launch (start us, length us, event | category | flops | bytes accessed | tf_op | source)
XLA Modules:
  0.0 488.1 jit_solution(12670345803102726703)
XLA Ops:
  6.5 0.0 reduce-scatter.3.cloned.1.call-start
  6.5 13.3 %copy_convert_fusion = f32[1024,2,2048]{2,0,1:T(8,128)} fusion(bf16[1024,2,2048]{2,1,0:T(2,128)(2,1)} %param.4), kind=kLoop, calls=%fused_computation.15 | loop fusion | flops 4194304 | bytes 25165824 | tf_op jit(solution)/shard_map/convert_element_type | solution.py:37
  19.8 6.5 %fusion.14 = f32[1024]{0:T(1024)S(1)} fusion(f32[1024,2,2048]{2,0,1:T(8,128)} %copy_convert_fusion), kind=kLoop, calls=%fused_computation.35 | loop fusion | flops 8387584 | bytes 16781312 | tf_op jit(solution)/shard_map/reduce_sum | solution.py:39
  26.3 10.6 %psum.7 = f32[1024]{0:T(1024)S(1)} all-reduce(f32[1024]{0:T(1024)S(1)} %fusion.14), channel_id=1, replica_groups=mesh['chan'=32,'freq'=4] {'freq'}, use_global_device_ids=true, to_apply=%region_2.3 | all-reduce | flops 1024 | bytes 8192 | tf_op jit(solution)/shard_map/psum | solution.py:39
  36.9 6.6 %add_bitcast_fusion = f32[1024,2048]{1,0:T(8,128)S(1)} fusion(f32[1024]{0:T(1024)S(1)} %multiply_add_fusion.1, f32[1024,2,2048]{2,0,1:T(8,128)} %copy_convert_fusion), kind=kLoop, calls=%fused_computation.23 | loop fusion | flops 8388608 | bytes 25169920 | tf_op jit(solution)/shard_map/div | solution.py:41
  43.5 0.0 copy-start.1
  43.5 0.0 copy-start
  43.5 6.8 %divide_convert_fusion = bf16[1024,2,2048]{2,0,1:T(8,128)(2,1)S(1)} fusion(f32[1024,2048]{1,0:T(8,128)S(1)} %add_bitcast_fusion, bf16[1024,2,2048]{2,1,0:T(2,128)(2,1)} %param.4), kind=kLoop, calls=%fused_computation.4 | loop fusion | flops 12582912 | bytes 25165824 | tf_op jit(solution)/shard_map/convert_element_type | solution.py:41
  50.4 4.5 collective-permute-start
  54.9 9.7 %collective-permute-done = bf16[1024,2,2048]{2,0,1:T(8,128)(2,1)} collective-permute-done((bf16[1024,2,2048]{2,0,1:T(8,128)(2,1)S(1)}, bf16[1024,2,2048]{2,0,1:T(8,128)(2,1)}, u32[]{:S(2)}, u32[]{:S(2)}) %collective-permute-start) | collective-permute-done | bytes 8388640 | tf_op jit(solution)/shard_map/ppermute | solution.py:19
  64.6 85.2 %collective-permute-start.1 = (bf16[1024,2,2048]{2,0,1:T(8,128)(2,1)}, bf16[1024,2,2048]{2,0,1:T(8,128)(2,1)}, u32[]{:S(2)}, u32[]{:S(2)}) collective-permute-start(bf16[1024,2,2048]{2,0,1:T(8,128)(2,1)} %collective-permute-done), channel_id=1, source_target_pairs={{0,4},{4,8},{8,12},{12,16},{16,20},{20,24},{24,28},{28,32},{32,36}... | collective-permute-start | bytes 25165832 | tf_op jit(solution)/shard_map/ppermute | solution.py:19
  149.8 0.0 copy-done.1
  149.8 0.6 fusion.20
  151.6 0.8 subtract_abs_fusion.1
  152.5 1.1 select_reduce_fusion
  153.6 35.7 %cosine_multiply_fusion = (f32[2048,1024]{1,0:T(8,128)}, f32[2048,1024]{1,0:T(8,128)}) fusion(s32[1024]{0:T(1024)S(1)} %iota_add_fusion.1, s32[2048]{0:T(1024)S(1)} %iota_add_fusion), kind=kLoop, calls=%fused_computation.17 | loop fusion | flops 35651584 | bytes 16789504 | tf_op jit(solution)/shard_map/mul | solution.py:28
  189.3 11.2 %convert_element_type.29 = f32[1024,2,2048]{2,0,1:T(8,128)} convert(bf16[1024,2,2048]{2,0,1:T(8,128)(2,1)} %collective-permute-done) | non-fusion elementwise | flops 4194304 | bytes 25165824 | tf_op jit(solution)/shard_map/convert_element_type | solution.py:56
  200.5 0.0 collective-permute-done.1
  200.5 11.2 %convert_element_type.31 = f32[1024,2,2048]{2,0,1:T(8,128)} convert(bf16[1024,2,2048]{2,0,1:T(8,128)(2,1)} %collective-permute-done.1) | non-fusion elementwise | flops 4194304 | bytes 25165824 | tf_op jit(solution)/shard_map/convert_element_type | solution.py:56
  211.7 23.1 %add_convert_fusion = (bf16[1024,1,2048]{2,0,1:T(8,128)(2,1)S(1)}, bf16[1024,1,2048]{2,0,1:T(8,128)(2,1)}, bf16[1024,1,2048]{2,0,1:T(8,128)(2,1)}, bf16[1024,1,2048]{2,0,1:T(8,128)(2,1)}) fusion(f32[1024,2,2048]{2,0,1:T(8,128)} %convert_element_type.31, f32[1024,2,2048]{2,0,1:T(8,128)} %copy_convert_fusion, f32[1024,2,2048]{2,0,1:T(8,128)} %convert_element_type.29), kind=kLoop, calls=%fused_computation.20 | loop fusion | flops 33554432 | bytes 67108864 | tf_op jit(solution)/shard_map/convert
  234.8 10.5 %pad_maximum_fusion = (bf16[1024,2,2048]{2,0,1:T(8,128)(2,1)}, bf16[1024,2,2048]{2,0,1:T(8,128)(2,1)}) fusion(bf16[1024,1,2048]{2,0,1:T(8,128)(2,1)} %get-tuple-element.11, bf16[1024,1,2048]{2,0,1:T(8,128)(2,1)} %get-tuple-element.12, bf16[1024,1,2048]{2,0,1:T(8,128)(2,1)} %get-tuple-element.8, bf16[1024,1,2048]{2,0,1:T(8,128)(2,1)S(1)} %get-tuple-element.7), kind=kLoop, calls=%fused_computation.13 | loop fusion | flops 8388608 | bytes 33554432 | tf_op jit(solution)/shard_map/stack | solution.py:59
  245.3 11.9 %copy.11 = bf16[1024,2,2048]{0,2,1:T(8,128)(2,1)} copy(bf16[1024,2,2048]{2,0,1:T(8,128)(2,1)} %get-tuple-element.20) | data formatting | bytes 16777216 | tf_op jit(solution)/shard_map/stack | solution.py:59
  257.2 11.9 %copy.10 = bf16[1024,2,2048]{0,2,1:T(8,128)(2,1)} copy(bf16[1024,2,2048]{2,0,1:T(8,128)(2,1)} %get-tuple-element.19) | data formatting | bytes 16777216 | tf_op jit(solution)/shard_map/stack | solution.py:59
  269.1 10.5 %fusion.12 = f32[512,4096]{1,0:T(8,128)} fusion(bf16[1024,4096]{0,1:T(8,128)(2,1)} %bitcast.13, s32[1024]{0:T(1024)S(1)} %get-tuple-element.5, pred[]{:T(512)S(6)} %and.28), kind=kOutput, calls=%fused_computation.34 | convolution fusion | flops 4296015872 | bytes 16781312 | tf_op jit(solution)/shard_map/dot_general | solution.py:60
  279.6 10.2 %fusion.9 = f32[512,4096]{1,0:T(8,128)} fusion(bf16[1024,4096]{0,1:T(8,128)(2,1)} %bitcast.12, s32[1024]{0:T(1024)S(1)} %get-tuple-element.6, pred[]{:T(512)S(6)} %and.25), kind=kOutput, calls=%fused_computation.32 | convolution fusion | flops 4296015872 | bytes 16781312 | tf_op jit(solution)/shard_map/dot_general | solution.py:60
  289.8 0.0 slice-done
  289.9 40.1 %fusion = f32[512,1024]{1,0:T(8,128)} fusion(f32[2048,1024]{1,0:T(8,128)S(1)} %bitcast.11, f32[2048,1024]{1,0:T(8,128)S(1)} %bitcast.9, f32[512,4096]{1,0:T(8,128)} %fusion.9, f32[512,4096]{1,0:T(8,128)} %fusion.12), kind=kOutput, calls=%fused_computation | convolution fusion | flops 25776095232 | bytes 35651584 | tf_op jit(solution)/shard_map/dot_general | solution.py:62
  329.9 0.0 reduce-scatter.3.cloned.1.call-update
  330.0 0.0 reduce-scatter.5.cloned.1.call-start
  330.0 70.5 %reduce-scatter.3.cloned.1.call-done = f32[512,256]{1,0:T(8,128)} async-done(((f32[512,1024]{1,0:T(8,128)}), f32[512,256]{1,0:T(8,128)}) %reduce-scatter.3.cloned.1.call-update) | async-done | bytes 524304 | tf_op jit(solution)/shard_map/reduce_scatter | solution.py:63
  400.5 0.0 reduce-scatter.5.cloned.1.call-update
  400.6 80.7 %reduce-scatter.5.cloned.1.call-done = f32[16,256]{1,0:T(8,128)} async-done(((f32[512,256]{1,0:T(8,128)}), f32[16,256]{1,0:T(8,128)}) %reduce-scatter.5.cloned.1.call-update) | async-done | bytes 16400 | tf_op jit(solution)/shard_map/reduce_scatter | solution.py:64
  (13 shorter events, 0.0 us)
Async XLA Ops:
  6.5 394.0 %reduce-scatter.3.cloned.1.call-start = ((), (), s32[]{:S(2)}) async-start(), calls=%async_computation.2 | async-start | bytes 2621440 | tf_op jit(solution)/shard_map/reduce_scatter | solution.py:63
  43.5 106.3 %copy-start.1 = (s32[1,2]{1,0:T(1,128)S(1)}, s32[1,2]{1,0:T(1,128)}, u32[]{:S(2)}) copy-start(s32[1,2]{1,0:T(1,128)} %param.7) | copy-start | bytes 28
  43.5 108.9 %copy-start = (s32[512]{0:T(512)S(1)}, s32[512]{0:T(512)}, u32[]{:S(2)}) copy-start(s32[512]{0:T(512)} %param.6) | copy-start | bytes 6148
  50.4 14.2 %collective-permute-start = (bf16[1024,2,2048]{2,0,1:T(8,128)(2,1)S(1)}, bf16[1024,2,2048]{2,0,1:T(8,128)(2,1)}, u32[]{:S(2)}, u32[]{:S(2)}) collective-permute-start(bf16[1024,2,2048]{2,0,1:T(8,128)(2,1)S(1)} %divide_convert_fusion), channel_id=1, source_target_pairs={{0,4},{4,8},{8,12},{12,16},{16,20},{20,24},{24,28},{28,32},{32,36}... | collective-permute-start | bytes 25165832 | tf_op jit(solution)/shard_map/ppermute | solution.py:19
  64.6 135.9 %collective-permute-start.1 = (bf16[1024,2,2048]{2,0,1:T(8,128)(2,1)}, bf16[1024,2,2048]{2,0,1:T(8,128)(2,1)}, u32[]{:S(2)}, u32[]{:S(2)}) collective-permute-start(bf16[1024,2,2048]{2,0,1:T(8,128)(2,1)} %collective-permute-done), channel_id=1, source_target_pairs={{0,4},{4,8},{8,12},{12,16},{16,20},{20,24},{24,28},{28,32},{32,36}... | collective-permute-start | bytes 25165832 | tf_op jit(solution)/shard_map/ppermute | solution.py:19
  269.1 20.7 %slice-start = ((s8[8388608]{0:T(1024)(128)(4,1)}), s8[4194304]{0:T(1024)(128)(4,1)S(1)}, s32[]{:S(2)}) async-start(s8[8388608]{0:T(1024)(128)(4,1)} %bitcast.8), calls=%async_computation.4 | async-start | bytes 8388608
  269.1 20.7 %slice-start.2 = ((s8[8388608]{0:T(1024)(128)(4,1)}), s8[4194304]{0:T(1024)(128)(4,1)S(1)}, s32[]{:S(2)}) async-start(s8[8388608]{0:T(1024)(128)(4,1)} %bitcast.10), calls=%async_computation.6 | async-start | bytes 8388608
  279.6 10.2 %slice-start.1 = ((s8[8388608]{0:T(1024)(128)(4,1)}), s8[4194304]{0:T(1024)(128)(4,1)S(1)}, s32[]{:S(2)}) async-start(s8[8388608]{0:T(1024)(128)(4,1)} %bitcast.8), calls=%async_computation.5 | async-start | bytes 8388608
  279.6 10.2 %slice-start.3 = ((s8[8388608]{0:T(1024)(128)(4,1)}), s8[4194304]{0:T(1024)(128)(4,1)S(1)}, s32[]{:S(2)}) async-start(s8[8388608]{0:T(1024)(128)(4,1)} %bitcast.10), calls=%async_computation.7 | async-start | bytes 8388608
  330.0 151.3 %reduce-scatter.5.cloned.1.call-start = ((), (), s32[]{:S(2)}) async-start(), calls=%async_computation.3 | async-start | bytes 540672 | tf_op jit(solution)/shard_map/reduce_scatter | solution.py:64
Sparse Core Ops, SparseCore 0:
  330.1 70.4 reduce-scatter.2
  404.4 76.8 reduce-scatter.4
where the time goes:
time: 489 us; the launch traced here: 488 us
  waiting for transfers between devices  161 us (33%)
  other arithmetic  127 us (26%)
  starting transfers between devices  89.8 us (18%)
  matrix products  60.8 us (12%)
  local copies, waits for them, and re-layouts  24.4 us (5%)
  between operations  14.7 us (3%)
  blocking collectives  10.6 us (2%)
    ppermute x2, starting transfers between devices, passed_along(): return lax.ppermute(block, axis, route)  89.8 us
    reduce_scatter x1, waiting for transfers between devices, shards(): lax.psum_scatter(partial_lags, 'chan', scatter_dimension=0, tiled=True)  80.7 us
    reduce_scatter x1, waiting for transfers between devices, shards(): lax.psum_scatter(lagged, 'freq', scatter_dimension=1, tiled=True)  70.5 us
    dot_general x1, matrix products, shards(): lagged = jnp.dot(stack, table, precision=lax.Precision.HIGHEST)  40.1 us
    mul x1, other arithmetic, lag_table(): jnp.cos(theta) * scale  35.7 us
    another operation x2, local copies, waits for them, and re-layouts, shards(): jnp.stack([prod_re, prod_im], axis=1).astype(jnp.bfloat16)  23.8 us
    another operation x1, other arithmetic  23.1 us
    convert_element_type x2, other arithmetic, shards(): wsrc = current.astype(jnp.float32)  22.4 us
  transfers between devices with their start and end apart: 4, of which 3 were waited for; matrix products, arithmetic and copies ran while one was open for 10% of the time, Pallas kernels for 0%

commit v1 on v0

v1 whole, which is shorter than its diff:
```python
import functools
import math

import jax
import jax.numpy as jnp
import numpy as np
from jax import lax
from jax.experimental import pallas as pl
from jax.experimental.pallas import tpu as pltpu
from jax.sharding import PartitionSpec as P

NF = 8192
LAGS = 1024

water = 0.5
tiny = 1e-06

TILE = 256
SLAB = 16
FINE = 16
CUTS = (1024, 512, 512)
VMEM = 40 * 1024 * 1024


def chips_along(block, distance):
    devices = range(lax.axis_size("chan"))
    route = [(i, i + 2 * distance) for i in devices if i + 2 * distance in devices]
    return lax.ppermute(block, "chan", route)


def to_sibling(block):
    return lax.ppermute(block, "chan", [(i, i ^ 1) for i in range(lax.axis_size("chan"))])


def phases(freqs, scale):
    lagvec = jnp.arange(LAGS, dtype=jnp.int32) - LAGS // 2
    phase = jnp.mod(freqs[:, None] * lagvec[None, :], 2 * NF)
    theta = 2.0 * math.pi / (2 * NF) * phase.astype(jnp.float32)
    return jnp.cos(theta) * scale, jnp.sin(theta) * scale


def split(value):
    high = value.astype(jnp.bfloat16)
    return high, (value - high.astype(jnp.float32)).astype(jnp.bfloat16)


def table_kernel(c1_ref, s1_ref, c2_ref, s2_ref, hi_ref, lo_ref):
    for a in range(TILE // FINE):
        c1, s1 = c1_ref[a : a + 1, :], s1_ref[a : a + 1, :]
        c2, s2 = c2_ref[...], s2_ref[...]
        for part, value in ((0, c1 * c2 - s1 * s2), (1, -(s1 * c2 + c1 * s2))):
            rows = pl.ds(part * TILE + a * FINE, FINE)
            hi_ref[0, rows, :], lo_ref[0, rows, :] = split(value)


def lag_tables(first, band):
    tiles = band // TILE
    coarse = first + FINE * jnp.arange(band // FINE, dtype=jnp.int32)
    c1, s1 = phases(coarse, 1.0 / math.sqrt(NF))
    c2, s2 = phases(jnp.arange(FINE, dtype=jnp.int32), 1.0)
    rows = pl.BlockSpec((TILE // FINE, LAGS), lambda t: (t, 0))
    fixed = pl.BlockSpec((FINE, LAGS), lambda t: (0, 0))
    out = pl.BlockSpec((1, 2 * TILE, LAGS), lambda t: (t, 0, 0))
    shape = jax.ShapeDtypeStruct((tiles, 2 * TILE, LAGS), jnp.bfloat16)
    return pl.pallas_call(
        table_kernel,
        grid=(tiles,),
        in_specs=[rows, rows, fixed, fixed],
        out_specs=[out, out],
        out_shape=[shape, shape],
        compiler_params=pltpu.CompilerParams(vmem_limit_bytes=VMEM),
        cost_estimate=pl.CostEstimate(
            flops=8 * band * LAGS, bytes_accessed=8 * band * LAGS, transcendentals=0
        ),
        name="lag_tables",
    )(c1, s1, c2, s2)


def load(ref, rows):
    return ref[0, rows, :].astype(jnp.float32), ref[1, rows, :].astype(jnp.float32)


def whiten(spectrum, level):
    re, im = spectrum
    inverse = 1.0 / (re * re + im * im + level)
    return (
        (re * inverse).astype(jnp.bfloat16).astype(jnp.float32),
        (im * inverse).astype(jnp.bfloat16).astype(jnp.float32),
    )


def put_product(prods, row, receiver, source):
    rre, rim = receiver
    wre, wim = source
    rows = pl.ds(row, SLAB)
    prods[rows, :TILE] = (rre * wre + rim * wim).astype(jnp.bfloat16)
    prods[rows, TILE:] = (rim * wre - rre * wim).astype(jnp.bfloat16)


def fill_onehot(onehot, target_ref):
    bins, pairs = onehot.shape
    for k in range(0, pairs, 256):
        row = lax.broadcasted_iota(jnp.int32, (bins, 256), 0)
        hit = row == target_ref[:, k : k + 256]
        onehot[:, k : k + 256] = jnp.where(hit, 1.0, 0.0).astype(jnp.bfloat16)


def local_kernel(role, target_ref, own, sib, own_level, sib_level, out_ref, onehot, prods):
    width = own.shape[1]

    @pl.when(pl.program_id(0) == 0)
    def _():
        fill_onehot(onehot, target_ref)

    def pairs(receiver, source, level):
        @pl.loop(0, width // SLAB)
        def _(s):
            row = pl.multiple_of(s * SLAB, SLAB)
            rows = pl.ds(row, SLAB)
            white = whiten(load(source, rows), level[rows, :])
            put_product(prods, row, load(receiver, rows), white)

    pl.when(role[0] == 0)(lambda: pairs(sib, own, own_level))
    pl.when(role[0] != 0)(lambda: pairs(own, sib, sib_level))
    out_ref[0] = jnp.dot(onehot[...], prods[...], preferred_element_type=jnp.float32)


def add_pairs(role, target_ref, prev, nxt, own, sib, prev_level, own_level, sib_level, onehot, prods):
    quarter = prev.shape[1]

    @pl.when(pl.program_id(0) == 0)
    def _():
        fill_onehot(onehot, target_ref)

    def pairs(l0, l1, l0_level, l1_level, odd):
        @pl.loop(0, quarter // SLAB)
        def _(s):
            row = pl.multiple_of(s * SLAB, SLAB)
            front = pl.ds(row, SLAB)
            back = pl.ds(quarter + row, SLAB)
            white = whiten(load(prev, front), prev_level[front, :])
            put_product(prods, row, load(l0, front), white)
            if odd:
                put_product(prods, 2 * quarter + row, load(l1, front), white)
            receiver = load(nxt, front)
            white = whiten(load(l1, back), l1_level[back, :])
            put_product(prods, quarter + row, receiver, white)
            if not odd:
                white = whiten(load(l0, back), l0_level[back, :])
                put_product(prods, 2 * quarter + row, receiver, white)

    for core in (0, 1):
        for odd in (0, 1):
            blocks = (own, sib, own_level, sib_level)
            if core:
                blocks = (sib, own, sib_level, own_level)
            run = functools.partial(pairs, *blocks, odd)
            pl.when((role[0] == core) & (role[1] == odd))(run)
    return jnp.dot(onehot[...], prods[...], preferred_element_type=jnp.float32)


def first_kernel(*refs):
    *ins, base, out_ref, onehot, prods = refs
    out_ref[0] = base[0] + add_pairs(*ins, onehot, prods)


def second_kernel(is_first, is_last, *refs):
    refs = list(refs)
    ins, refs = refs[:9], refs[9:]
    base, hi_ref, lo_ref, *refs = refs
    total_in = None if is_first else refs.pop(0)
    out_ref, onehot, prods, *refs = refs
    total = refs[0] if is_last else out_ref
    step = pl.program_id(0)
    stack = base[0] + add_pairs(*ins, onehot, prods)
    high, low = split(stack)
    lagged = jnp.dot(high, hi_ref[0], preferred_element_type=jnp.float32)
    lagged += jnp.dot(low, hi_ref[0], preferred_element_type=jnp.float32)
    lagged += jnp.dot(high, lo_ref[0], preferred_element_type=jnp.float32)

    @pl.when(step == 0)
    def _():
        total[...] = lagged if is_first else total_in[...] + lagged

    @pl.when(step > 0)
    def _():
        total[...] += lagged

    if is_last:
        parts, rows, lags = out_ref.shape
        bands = total.shape[1] // lags

        @pl.when(step == pl.num_programs(0) - 1)
        def _():
            for part in range(parts):
                r, f = part // bands * rows, part % bands * lags
                out_ref[part] = total[r : r + rows, f : f + lags].astype(jnp.bfloat16)


def shards(records, chan_pos, bin_row, pair_mask):
    here = lax.axis_index("chan")
    core, chip = here % 2, here // 2
    width, _, band = records.shape
    half, quarter = width // 2, width // 4
    bins = bin_row.shape[0]
    tiles = band // TILE
    devices = lax.axis_size("chan") * lax.axis_size("freq")

    def piece(array, first, count):
        return lax.dynamic_slice_in_dim(array, first, count).transpose(1, 0, 2)

    own_front = piece(records, core * half, quarter)
    own_back = piece(records, core * half + quarter, quarter)
    prev_own = chips_along(own_front, 1)
    next_own = chips_along(own_back, -1)
    rest, _, _ = lax.optimization_barrier((records, own_front, own_back))
    sib = to_sibling(piece(rest, (1 - core) * half, half))
    own = jnp.concatenate([own_front, own_back], axis=1)

    prev_sib, next_sib = [], []
    start = 0
    for cut in CUTS:
        prev_sib.append(chips_along(sib[:, :quarter, start : start + cut], 1))
        next_sib.append(chips_along(sib[:, quarter:, start : start + cut], -1))
        start += cut

    masks = lax.all_gather(pair_mask, "chan", tiled=True)

    def power(block):
        rec = block.astype(jnp.float32)
        return jnp.sum(rec[0] * rec[0] + rec[1] * rec[1], axis=1)

    totals = lax.psum(jnp.stack([power(own), power(sib)]), "freq")
    prev_totals = chips_along(totals[:, :quarter], 1)

    def level(total):
        return (water * total / NF + tiny)[:, None]

    own_level, sib_level = level(totals[0]), level(totals[1])

    def positions(block, offset):
        block = jnp.clip(block, 0, lax.axis_size("chan") - 1)
        return lax.dynamic_slice_in_dim(
            chan_pos, block * width + core * half + offset, quarter
        )

    def target(receiver, source, offset):
        apart = jnp.abs(positions(receiver, offset) - positions(source, offset))
        row = jnp.clip(receiver, 0, lax.axis_size("chan") - 1)
        used = jnp.where(receiver - source == 1, masks[row, 0], masks[row, 1])
        valid = (source >= 0) & (receiver < lax.axis_size("chan")) & (used > 0)
        return apart, jnp.broadcast_to(valid, apart.shape)

    l0, l1 = 2 * chip, 2 * chip + 1

    def slots(odd):
        before, after = l0 - 2 + odd, l0 + 2 + odd
        third_receiver = jnp.where(odd == 1, l1, after)
        third_source = jnp.where(odd == 1, before, l0)
        third_offset = jnp.where(odd == 1, 0, quarter)
        return [
            target(l0, before, 0),
            target(after, l1, quarter),
            target(third_receiver, third_source, third_offset),
        ]

    wanted = [target(l1, l0, 0), target(l1, l0, quarter)] + slots(core) + slots(1 - core)
    apart = jnp.concatenate([w[0] for w in wanted])
    valid = jnp.concatenate([w[1] for w in wanted])
    bin_ids = jnp.arange(bins, dtype=jnp.int32)
    row = jnp.sum(jnp.where(apart[:, None] == bin_ids[None, :], bin_row[None, :], 0), axis=1)
    row = jnp.where(valid, row, -1)[None, :]
    n = 3 * quarter
    local_row, own_row, sib_row = row[:, :half], row[:, half : half + n], row[:, half + n :]

    hi, lo = lag_tables(lax.axis_index("freq") * band, band)

    smem = pl.BlockSpec(memory_space=pltpu.SMEM)

    def whole(array):
        return pl.BlockSpec(array.shape, lambda t: (0,) * array.ndim)

    def columns(array, first=0):
        return pl.BlockSpec((2, array.shape[1], TILE), lambda t: (0, 0, t + first))

    def tile(array, first=0):
        return pl.BlockSpec((1, *array.shape[1:]), lambda t: (t + first, 0, 0))

    def params():
        return pltpu.CompilerParams(vmem_limit_bytes=VMEM)

    def scratch(count):
        return [
            pltpu.VMEM((bins, count), jnp.bfloat16),
            pltpu.VMEM((count, 2 * TILE), jnp.bfloat16),
        ]

    def cost(count, steps, lag=False):
        flops = steps * 2 * bins * 2 * TILE * (count + (3 * LAGS if lag else 0))
        return pl.CostEstimate(
            flops=flops, bytes_accessed=steps * 8 * bins * 2 * TILE, transcendentals=0
        )

    stack_shape = jax.ShapeDtypeStruct((tiles, bins, 2 * TILE), jnp.float32)
    roles = jnp.stack([core, core]).astype(jnp.int32)
    stack = pl.pallas_call(
        local_kernel,
        grid=(tiles,),
        in_specs=[smem, whole(local_row), columns(own), columns(sib)]
        + [whole(own_level), whole(sib_level)],
        out_specs=tile(stack_shape),
        out_shape=stack_shape,
        scratch_shapes=scratch(half),
        compiler_params=params(),
        cost_estimate=cost(half, tiles),
        name="local_pairs",
    )(roles, local_row, own, sib, own_level, sib_level)

    prev_level = level(prev_totals[0])
    stack = pl.pallas_call(
        first_kernel,
        grid=(tiles,),
        in_specs=[smem, whole(own_row), columns(prev_own), columns(next_own)]
        + [columns(own), columns(sib), whole(prev_level), whole(own_level)]
        + [whole(sib_level), tile(stack)],
        out_specs=tile(stack_shape),
        out_shape=stack_shape,
        scratch_shapes=scratch(n),
        compiler_params=params(),
        cost_estimate=cost(n, tiles),
        name="first_pairs",
    )(roles, own_row, prev_own, next_own, own, sib, prev_level, own_level, sib_level, stack)

    prev_level = level(prev_totals[1])
    roles = jnp.stack([core, 1 - core]).astype(jnp.int32)
    total = None
    start = 0
    for k, cut in enumerate(CUTS):
        is_first, is_last = k == 0, k == len(CUTS) - 1
        first, steps = start // TILE, cut // TILE
        ins = [roles, sib_row, prev_sib[k], next_sib[k], own, sib]
        ins += [prev_level, own_level, sib_level, stack, hi, lo]
        specs = [smem, whole(sib_row), columns(prev_sib[k]), columns(next_sib[k])]
        specs += [columns(own, first), columns(sib, first), whole(prev_level)]
        specs += [whole(own_level), whole(sib_level)]
        specs += [tile(stack, first), tile(hi, first), tile(lo, first)]
        if not is_first:
            ins.append(total)
            specs.append(whole(total))
        shape = jax.ShapeDtypeStruct((bins, LAGS), jnp.float32)
        extra = []
        if is_last:
            extra = [pltpu.VMEM(shape.shape, jnp.float32)]
            rows = bins // lax.axis_size("chan")
            lags = LAGS // lax.axis_size("freq")
            shape = jax.ShapeDtypeStruct((devices, rows, lags), jnp.bfloat16)
        total = pl.pallas_call(
            functools.partial(second_kernel, is_first, is_last),
            grid=(steps,),
            in_specs=specs,
            out_specs=whole(shape),
            out_shape=shape,
            scratch_shapes=scratch(n) + extra,
            compiler_params=params(),
            cost_estimate=cost(n, steps, True),
            name="second_pairs",
        )(*ins)
        start += cut

    parts = lax.all_to_all(total, ("chan", "freq"), 0, 0, tiled=True)
    return jnp.sum(parts.astype(jnp.float32), axis=0)


def solution(mesh):
    placed = (P("chan", None, "freq"), P(), P(), P("chan", None))
    return jax.shard_map(
        shards, mesh=mesh, in_specs=placed, out_specs=P("chan", "freq"), check_vma=False
    )
```

time: 489 us -> 283 us (0.58)
  waiting for transfers between devices: 161 us -> 0.03 us
  other arithmetic: 127 us -> 22.6 us
  Pallas kernels: 0 us -> 98.3 us
  blocking collectives: 10.6 us -> 88.3 us
  starting transfers between devices: 89.8 us -> 26.5 us
  matrix products: 60.8 us -> 0 us
  local copies, waits for them, and re-layouts: 24.4 us -> 36.6 us
  between operations: 14.7 us -> 8.86 us
    reduce_scatter x2 -> x0, waiting for transfers between devices: 151 us -> none  [the longest x1 80.7 us: shards(): lax.psum_scatter(partial_lags, 'chan', scatter_dimension=0, tiled=True)]
    pallas_call x0 -> x6, Pallas kernels: none -> 98.3 us  [the longest x3 40.6 us: shards(): pl.pallas_call(functools.partial(second_kernel, is_first, is_last), grid=...]
    ppermute x2 -> x10, starting transfers between devices: 89.8 us -> 26.5 us  [the longest x9 26.5 us: chips_along(): return lax.ppermute(block, 'chan', route)]
    dot_general x3 -> x0, matrix products: 60.8 us -> none  [the longest x1 40.1 us: shards(): lagged = jnp.dot(stack, table, precision=lax.Precision.HIGHEST)]
    all_gather x0 -> x1, blocking collectives: none -> 49.4 us  [shards(): masks = lax.all_gather(pair_mask, 'chan', tiled=True)]
    mul x1, other arithmetic: 35.7 us -> 2.14 us  [phases(): return (jnp.cos(theta) * scale, jnp.sin(theta) * scale)]
    another operation x2, other arithmetic: 33.6 us -> 0.09 us  [the longest x1 0.08 us: shards(): roles = jnp.stack([core, 1 - core]).astype(jnp.int32)]
    convert_element_type x4 -> x2, other arithmetic: 42.5 us -> 10.6 us  [power(): rec = block.astype(jnp.float32)]
  transfers between devices with their start and end apart: 4 -> 10, of which waited for: 3 -> 0; matrix products, arithmetic and copies ran while one was open for 10% -> 17% of each run, Pallas kernels for 0% -> 31%
where the time goes in v1:
time: 283 us; the launch traced here: 281 us
  Pallas kernels  98.3 us (35%)
  blocking collectives  88.3 us (31%)
  local copies, waits for them, and re-layouts  36.6 us (13%)
  starting transfers between devices  26.5 us (9%)
  other arithmetic  22.6 us (8%)
  between operations  8.86 us (3%)
    all_gather x1, blocking collectives, shards(): masks = lax.all_gather(pair_mask, 'chan', tiled=True)  49.4 us
    pallas_call x3, Pallas kernels, shards(): pl.pallas_call(functools.partial(second_kernel, is_first, is_last), grid=...  40.6 us
    pallas_call x1, Pallas kernels, shards(): pl.pallas_call(local_kernel, grid=(tiles,), in_specs=[smem, whole(local_r...  28.6 us
    all_to_all x1, blocking collectives, shards(): parts = lax.all_to_all(total, ('chan', 'freq'), 0, 0, tiled=True)  28.4 us
    ppermute x9, starting transfers between devices, chips_along(): return lax.ppermute(block, 'chan', route)  26.5 us
    pallas_call x1, Pallas kernels, shards(): pl.pallas_call(first_kernel, grid=(tiles,), in_specs=[smem, whole(own_row...  22.3 us
    convert_element_type x2, other arithmetic, power(): rec = block.astype(jnp.float32)  10.6 us
    optimization_barrier x1, local copies, waits for them, and re-layouts, shards(): rest, _, _ = lax.optimization_barrier((records, own_front, own_back))  10.5 us
  transfers between devices with their start and end apart: 10, of which 0 were waited for; matrix products, arithmetic and copies ran while one was open for 17% of the time, Pallas kernels for 31%

profile of v1, /device:TPU:0, one launch (start us, length us, event | category | flops | bytes accessed | tf_op | source)
XLA Modules:
  0.0 281.2 jit_solution(14466555234002717371)
XLA Ops:
  0.0 5.1 %constant_dynamic-slice_fusion.5 = (bf16[256,2,2048]{2,1,0:T(2,128)(2,1)S(1)}, bf16[256,2,2048]{2,1,0:T(2,128)(2,1)S(1)}) fusion(bf16[1024,2,2048]{2,1,0:T(2,128)(2,1)} %param.4, s32[]{:T(128)S(6)} %select_n.173, s32[]{:T(128)S(6)} %select_n.172), kind=kLoop, calls=%fused_computation.60 | loop fusion | bytes 8388616 | tf_op jit(solution)/shard_map/dynamic_slice | solution.py:210
  5.1 2.2 copy.64
  7.3 4.0 %collective-permute-start.4 = (bf16[2,256,2048]{2,1,0:T(8,128)(2,1)}, bf16[2,256,2048]{2,1,0:T(8,128)(2,1)S(1)}, u32[]{:S(2)}, u32[]{:S(2)}) collective-permute-start(bf16[2,256,2048]{2,1,0:T(8,128)(2,1)} %bitcast.32), channel_id=1, source_target_pairs={{0,8},{4,12},{8,16},{12,20},{16,24},{20,28},{24,32},{28,36},{32,40... | collective-permute-start | bytes 6291464 | tf_op jit(solution)/shard_map/ppermute | solution.py:28
  11.4 2.2 copy.63
  13.6 1.3 collective-permute-start.5
  14.9 10.5 %copy.44 = bf16[1024,2,2048]{2,0,1:T(8,128)(2,1)} copy(bf16[1024,2,2048]{2,1,0:T(2,128)(2,1)} %param.4) | data formatting | bytes 16777216 | tf_op jit(solution)/shard_map/optimization_barrier | solution.py:216
  25.4 4.8 %dynamic-slice_bitcast_fusion = bf16[2,512,2048]{2,1,0:T(8,128)(2,1)} fusion(bf16[1024,2,2048]{2,0,1:T(8,128)(2,1)} %copy.44, s32[]{:T(128)S(6)} %select_n.174), kind=kLoop, calls=%fused_computation.9 | loop fusion | bytes 8388612 | tf_op jit(solution)/shard_map/transpose | solution.py:210
  30.2 49.4 %all-gather = s32[32,1,2]{2,1,0:T(1,128)S(1)} all-gather(s32[1,1,2]{2,1,0:T(1,128)S(1)} %bitcast.36), channel_id=1, replica_groups=mesh['chan'=32,'freq'=4] {'chan'}, dimensions={0}, use_global_device_ids=true | all-gather | bytes 264 | tf_op jit(solution)/shard_map/all_gather | solution.py:227
  90.4 0.8 constant_dynamic-update-slice_fusion.14
  95.4 0.9 select_reduce_fusion
  96.7 2.1 sine_multiply_fusion
  98.8 6.7 %lag_tables.1 = (bf16[8,512,1024]{2,1,0:T(8,128)(2,1)S(1)}, bf16[8,512,1024]{2,1,0:T(8,128)(2,1)}) custom-call(f32[128,1024]{1,0:T(8,128)S(1)} %get-tuple-element.35.c1_ref, f32[128,1024]{1,0:T(8,128)S(1)} %get-tuple-element.34.s1_ref, f32[16,1024]{1,0:T(8,128)S(1)} %get-tuple-element.37.c2_ref, f32[16,1024]{1,0:T(8,128)S(1)} %get-tuple-element.36.s2_ref), custom_call_target="tpu_custom_call" | custom-call | flops 16777216 | bytes 16777216 | tf_op jit(solution)/shard_map/lag_tables/pallas_call | solution.py:65
  105.6 7.4 %fusion.23 = (f32[2,512,2048]{2,1,0:T(8,128)S(1)}, bf16[2,512,2048]{2,1,0:T(8,128)(2,1)}) fusion(bf16[2,256,2048]{2,1,0:T(8,128)(2,1)} %bitcast.31, bf16[2,256,2048]{2,1,0:T(8,128)(2,1)} %bitcast.32), kind=kLoop, calls=%fused_computation.83 | loop fusion | flops 10485760 | bytes 16777216 | tf_op jit(solution)/shard_map/convert_element_type | solution.py:230
  113.6 3.1 %fusion.24 = (bf16[2,256,1024]{2,1,0:T(8,128)(2,1)}, bf16[2,256,1024]{2,1,0:T(8,128)(2,1)}) fusion(bf16[2,512,2048]{2,1,0:T(8,128)(2,1)} %collective-permute-done.sib.refs_5_), kind=kLoop, calls=%fused_computation.84 | loop fusion | bytes 4194304 | tf_op jit(solution)/shard_map/slice | solution.py:224
  116.7 1.3 collective-permute-start.9
  118.0 5.5 %collective-permute-start.8 = (bf16[2,256,1024]{2,1,0:T(8,128)(2,1)}, bf16[2,256,1024]{2,1,0:T(8,128)(2,1)}, u32[]{:S(2)}, u32[]{:S(2)}) collective-permute-start(bf16[2,256,1024]{2,1,0:T(8,128)(2,1)} %get-tuple-element.14), channel_id=1, source_target_pairs={{0,8},{4,12},{8,16},{12,20},{16,24},{20,28},{24,32},{28,36},{32,40... | collective-permute-start | bytes 3145736 | tf_op jit(solution)/shard_map/ppermute | solution.py:28
  123.5 3.3 %convert_element_type.18 = f32[2,512,2048]{2,1,0:T(8,128)S(1)} convert(bf16[2,512,2048]{2,1,0:T(8,128)(2,1)} %collective-permute-done.sib.refs_5_) | non-fusion elementwise | flops 2097152 | bytes 12582912 | tf_op jit(solution)/shard_map/convert_element_type | solution.py:230
  127.4 10.5 %psum.7 = f32[2,512]{1,0:T(2,128)S(1)} all-reduce(f32[2,512]{1,0:T(2,128)S(1)} %pad_maximum_fusion.1), channel_id=1, replica_groups=mesh['chan'=32,'freq'=4] {'freq'}, use_global_device_ids=true, to_apply=%region_3.4 | all-reduce | flops 1024 | bytes 8192 | tf_op jit(solution)/shard_map/psum | solution.py:233
  137.9 2.5 collective-permute-start.3
  140.7 3.0 %fusion.25 = (bf16[2,256,512]{2,1,0:T(8,128)(2,1)}, bf16[2,256,512]{2,1,0:T(8,128)(2,1)}, bf16[2,256,512]{2,1,0:T(8,128)(2,1)}, bf16[2,256,512]{2,1,0:T(8,128)(2,1)}) fusion(bf16[2,512,2048]{2,1,0:T(8,128)(2,1)} %collective-permute-done.sib.refs_5_), kind=kLoop, calls=%fused_computation.85 | loop fusion | bytes 4194304 | tf_op jit(solution)/shard_map/slice | solution.py:224
  143.9 28.6 %local_pairs.1.refs_9_ = f32[8,512,512]{2,1,0:T(8,128)} custom-call(s32[2]{0:T(128)S(1)} %get-tuple-element.43.role.refs_0_, s32[1,512]{1,0:T(1,128)S(1)} %slice.89.target_ref, bf16[2,512,2048]{2,1,0:T(8,128)(2,1)S(1)} %copy-done, bf16[2,512,2048]{2,1,0:T(8,128)(2,1)} %collective-permute-done.sib.refs_5_, f32[512,1]{1,0:T(8,128)S(1)} %copy.57.own_level.refs_7_, ...), custom_call_target="tpu_custom_call" | custom-call | flops 2147483648 | bytes 16777216 | tf_op jit(solution)/shard_map/local_pairs/pallas_call | solution.py:306
  172.6 1.3 collective-permute-start.7
  174.2 4.6 %collective-permute-start.6 = (bf16[2,256,512]{2,1,0:T(8,128)(2,1)}, bf16[2,256,512]{2,1,0:T(8,128)(2,1)S(1)}, u32[]{:S(2)}, u32[]{:S(2)}) collective-permute-start(bf16[2,256,512]{2,1,0:T(8,128)(2,1)} %get-tuple-element.16), channel_id=1, source_target_pairs={{0,8},{4,12},{8,16},{12,20},{16,24},{20,28},{24,32},{28,36},{32,40... | collective-permute-start | bytes 1572872 | tf_op jit(solution)/shard_map/ppermute | solution.py:28
  178.7 1.3 collective-permute-start.2
  180.1 2.2 copy-done.1
  182.2 22.3 %first_pairs.1.refs_9_ = f32[8,512,512]{2,1,0:T(8,128)} custom-call(s32[2]{0:T(128)S(1)} %get-tuple-element.43.role.refs_0_, s32[1,768]{1,0:T(1,128)S(1)} %get-tuple-element.32.refs_1_, bf16[2,256,2048]{2,1,0:T(8,128)(2,1)S(1)} %collective-permute-done.4.refs_2_, bf16[2,256,2048]{2,1,0:T(8,128)(2,1)} %collective-permute-done.5.refs_3_, ...), custom_call_target="tpu_custom_call" | custom-call | flops 3221225472 | bytes 16777216 | tf_op jit(solution)/shard_map/first_pairs/pallas_call | solution.py:320
  204.6 4.8 %collective-permute-start.1 = (bf16[2,256,512]{2,1,0:T(8,128)(2,1)S(1)}, bf16[2,256,512]{2,1,0:T(8,128)(2,1)S(1)}, u32[]{:S(2)}, u32[]{:S(2)}) collective-permute-start(bf16[2,256,512]{2,1,0:T(8,128)(2,1)S(1)} %copy-done.6), channel_id=1, source_target_pairs={{0,8},{4,12},{8,16},{12,20},{16,24},{20,28},{24,32},{28,36},{32,40... | collective-permute-start | bytes 1572872 | tf_op jit(solution)/shard_map/ppermute | solution.py:28
  209.4 19.2 %second_pairs.3.refs_12_ = f32[512,1024]{1,0:T(8,128)S(1)} custom-call(s32[2]{0:T(128)S(1)} %get-tuple-element.42.refs_0_, s32[1,768]{1,0:T(1,128)S(1)} %get-tuple-element.33.refs_1_, bf16[2,256,1024]{2,1,0:T(8,128)(2,1)} %collective-permute-done.8.refs_2_, bf16[2,256,1024]{2,1,0:T(8,128)(2,1)} %collective-permute-done.9.refs_3_, ...), custom_call_target="tpu_custom_call" | custom-call | flops 8053063680 | bytes 8388608 | tf_op jit(solution)/shard_map/second_pairs/pallas_call | solution.py:357
  229.5 1.0 copy-done.5
  230.5 10.7 %second_pairs.4.refs_12_ = f32[512,1024]{1,0:T(8,128)S(1)} custom-call(s32[2]{0:T(128)S(1)} %get-tuple-element.42.refs_0_, s32[1,768]{1,0:T(1,128)S(1)} %get-tuple-element.33.refs_1_, bf16[2,256,512]{2,1,0:T(8,128)(2,1)S(1)} %copy-done.5, bf16[2,256,512]{2,1,0:T(8,128)(2,1)S(1)} %collective-permute-done.7.refs_3_, bf16[2,512,2048]{2,1,0:T(8,128)(2,1)S(1)} %copy-done.2, ...), custom_call_target="tpu_custom_call" | custom-call | flops 4026531840 | bytes 4194304 | tf_op jit(solution)/shard_map/second_pairs/pallas_call | solution.py:357
  241.2 10.8 %second_pairs.5 = bf16[128,16,256]{2,1,0:T(8,128)(2,1)S(1)} custom-call(s32[2]{0:T(128)S(1)} %get-tuple-element.42.refs_0_, s32[1,768]{1,0:T(1,128)S(1)} %get-tuple-element.33.refs_1_, bf16[2,256,512]{2,1,0:T(8,128)(2,1)S(1)} %collective-permute-done.1.refs_2_, bf16[2,256,512]{2,1,0:T(8,128)(2,1)S(1)} %collective-permute-done.2.refs_3_, ...), custom_call_target="tpu_custom_call" | custom-call | flops 4026531840 | bytes 4194304 | tf_op jit(solution)/shard_map/second_pairs/pallas_call | solution.py:357
  252.0 28.4 %all_to_all.5 = bf16[128,16,256]{2,1,0:T(8,128)(2,1)S(1)} all-to-all(bf16[128,16,256]{2,1,0:T(8,128)(2,1)S(1)} %second_pairs.5), channel_id=1, replica_groups=mesh['chan'=32,'freq'=4] {'chan','freq'}, dimensions={0} | all-to-all | bytes 2097152 | tf_op jit(solution)/shard_map/all_to_all | solution.py:370
  (62 shorter events, 10.4 us)
Async XLA Ops:
  7.3 166.8 %collective-permute-start.4 = (bf16[2,256,2048]{2,1,0:T(8,128)(2,1)}, bf16[2,256,2048]{2,1,0:T(8,128)(2,1)S(1)}, u32[]{:S(2)}, u32[]{:S(2)}) collective-permute-start(bf16[2,256,2048]{2,1,0:T(8,128)(2,1)} %bitcast.32), channel_id=1, source_target_pairs={{0,8},{4,12},{8,16},{12,20},{16,24},{20,28},{24,32},{28,36},{32,40... | collective-permute-start | bytes 6291464 | tf_op jit(solution)/shard_map/ppermute | solution.py:28
  13.6 165.1 %collective-permute-start.5 = (bf16[2,256,2048]{2,1,0:T(8,128)(2,1)}, bf16[2,256,2048]{2,1,0:T(8,128)(2,1)}, u32[]{:S(2)}, u32[]{:S(2)}) collective-permute-start(bf16[2,256,2048]{2,1,0:T(8,128)(2,1)} %bitcast.31), channel_id=1, source_target_pairs={{8,0},{12,4},{16,8},{20,12},{24,16},{28,20},{32,24},{36,28},{40,32... | collective-permute-start | bytes 6291464 | tf_op jit(solution)/shard_map/ppermute | solution.py:28
  25.4 4.8 %copy-start.8 = (s32[1,2]{1,0:T(1,128)S(1)}, s32[1,2]{1,0:T(1,128)}, u32[]{:S(2)}) copy-start(s32[1,2]{1,0:T(1,128)} %param.7) | copy-start | bytes 28
  25.4 69.9 %copy-start.7 = (s32[512]{0:T(512)S(1)}, s32[512]{0:T(512)}, u32[]{:S(2)}) copy-start(s32[512]{0:T(512)} %param.6) | copy-start | bytes 6148
  30.2 83.4 %collective-permute-start = (bf16[2,512,2048]{2,1,0:T(8,128)(2,1)}, bf16[2,512,2048]{2,1,0:T(8,128)(2,1)}, u32[]{:S(2)}, u32[]{:S(2)}) collective-permute-start(bf16[2,512,2048]{2,1,0:T(8,128)(2,1)} %dynamic-slice_bitcast_fusion), channel_id=1, source_target_pairs={{0,4},{4,0},{8,12},{12,8},{16,20},{20,16},{24,28},{28,24},{32,36},... | collective-permute-start | bytes 12582920 | tf_op jit(solution)/shard_map/ppermute | solution.py:32
  105.5 7.5 %copy-start.3 = (bf16[8,512,1024]{2,1,0:T(8,128)(2,1)}, bf16[8,512,1024]{2,1,0:T(8,128)(2,1)S(1)}, u32[]{:S(2)}) copy-start(bf16[8,512,1024]{2,1,0:T(8,128)(2,1)S(1)} %get-tuple-element.9.refs_10_) | copy-start | bytes 25165828
  116.7 87.9 %collective-permute-start.9 = (bf16[2,256,1024]{2,1,0:T(8,128)(2,1)}, bf16[2,256,1024]{2,1,0:T(8,128)(2,1)}, u32[]{:S(2)}, u32[]{:S(2)}) collective-permute-start(bf16[2,256,1024]{2,1,0:T(8,128)(2,1)} %get-tuple-element.13), channel_id=1, source_target_pairs={{8,0},{12,4},{16,8},{20,12},{24,16},{28,20},{32,24},{36,28},{40,32... | collective-permute-start | bytes 3145736 | tf_op jit(solution)/shard_map/ppermute | solution.py:28
  118.0 91.4 %collective-permute-start.8 = (bf16[2,256,1024]{2,1,0:T(8,128)(2,1)}, bf16[2,256,1024]{2,1,0:T(8,128)(2,1)}, u32[]{:S(2)}, u32[]{:S(2)}) collective-permute-start(bf16[2,256,1024]{2,1,0:T(8,128)(2,1)} %get-tuple-element.14), channel_id=1, source_target_pairs={{0,8},{4,12},{8,16},{12,20},{16,24},{20,28},{24,32},{28,36},{32,40... | collective-permute-start | bytes 3145736 | tf_op jit(solution)/shard_map/ppermute | solution.py:28
  137.9 34.7 %collective-permute-start.3 = (f32[2,256]{1,0:T(2,128)S(1)}, f32[2,256]{1,0:T(2,128)S(1)}, u32[]{:S(2)}, u32[]{:S(2)}) collective-permute-start(f32[2,256]{1,0:T(2,128)S(1)} %slice.83), channel_id=1, source_target_pairs={{0,8},{4,12},{8,16},{12,20},{16,24},{20,28},{24,32},{28,36},{32,40... | collective-permute-start | bytes 6152 | tf_op jit(solution)/shard_map/ppermute | solution.py:28
  140.7 3.2 %copy-start = (bf16[2,512,2048]{2,1,0:T(8,128)(2,1)S(1)}, bf16[2,512,2048]{2,1,0:T(8,128)(2,1)}, u32[]{:S(2)}) copy-start(bf16[2,512,2048]{2,1,0:T(8,128)(2,1)} %get-tuple-element.20.own.refs_4_) | copy-start | bytes 12582916
  172.6 56.1 %collective-permute-start.7 = (bf16[2,256,512]{2,1,0:T(8,128)(2,1)}, bf16[2,256,512]{2,1,0:T(8,128)(2,1)S(1)}, u32[]{:S(2)}, u32[]{:S(2)}) collective-permute-start(bf16[2,256,512]{2,1,0:T(8,128)(2,1)} %get-tuple-element.15), channel_id=1, source_target_pairs={{8,0},{12,4},{16,8},{20,12},{24,16},{28,20},{32,24},{36,28},{40,32... | collective-permute-start | bytes 1572872 | tf_op jit(solution)/shard_map/ppermute | solution.py:28
  174.2 54.5 %collective-permute-start.6 = (bf16[2,256,512]{2,1,0:T(8,128)(2,1)}, bf16[2,256,512]{2,1,0:T(8,128)(2,1)S(1)}, u32[]{:S(2)}, u32[]{:S(2)}) collective-permute-start(bf16[2,256,512]{2,1,0:T(8,128)(2,1)} %get-tuple-element.16), channel_id=1, source_target_pairs={{0,8},{4,12},{8,16},{12,20},{16,24},{20,28},{24,32},{28,36},{32,40... | collective-permute-start | bytes 1572872 | tf_op jit(solution)/shard_map/ppermute | solution.py:28
  178.7 62.4 %collective-permute-start.2 = (bf16[2,256,512]{2,1,0:T(8,128)(2,1)}, bf16[2,256,512]{2,1,0:T(8,128)(2,1)S(1)}, u32[]{:S(2)}, u32[]{:S(2)}) collective-permute-start(bf16[2,256,512]{2,1,0:T(8,128)(2,1)} %get-tuple-element.17), channel_id=1, source_target_pairs={{8,0},{12,4},{16,8},{20,12},{24,16},{28,20},{32,24},{36,28},{40,32... | collective-permute-start | bytes 1572872 | tf_op jit(solution)/shard_map/ppermute | solution.py:28
  180.0 2.2 copy-start.1
  182.2 22.4 %copy-start.6 = (bf16[2,256,512]{2,1,0:T(8,128)(2,1)S(1)}, bf16[2,256,512]{2,1,0:T(8,128)(2,1)}, u32[]{:S(2)}) copy-start(bf16[2,256,512]{2,1,0:T(8,128)(2,1)} %get-tuple-element.18) | copy-start | bytes 1572868
  182.2 27.2 %copy-start.2 = (bf16[2,512,2048]{2,1,0:T(8,128)(2,1)S(1)}, bf16[2,512,2048]{2,1,0:T(8,128)(2,1)}, u32[]{:S(2)}) copy-start(bf16[2,512,2048]{2,1,0:T(8,128)(2,1)} %get-tuple-element.20.own.refs_4_) | copy-start | bytes 12582916
  204.6 36.6 %collective-permute-start.1 = (bf16[2,256,512]{2,1,0:T(8,128)(2,1)S(1)}, bf16[2,256,512]{2,1,0:T(8,128)(2,1)S(1)}, u32[]{:S(2)}, u32[]{:S(2)}) collective-permute-start(bf16[2,256,512]{2,1,0:T(8,128)(2,1)S(1)} %copy-done.6), channel_id=1, source_target_pairs={{0,8},{4,12},{8,16},{12,20},{16,24},{20,28},{24,32},{28,36},{32,40... | collective-permute-start | bytes 1572872 | tf_op jit(solution)/shard_map/ppermute | solution.py:28
  228.6 0.8 copy-start.4
  229.5 1.0 copy-start.5

commit v2 on v0

v2 whole, which is shorter than its diff:
```python
import functools
import math

import jax
import jax.numpy as jnp
from jax import lax
from jax.experimental import pallas as pl
from jax.experimental.pallas import tpu as pltpu
from jax.sharding import PartitionSpec as P

NF = 8192
LAGS = 1024

water = 0.5
tiny = 1e-06

TILE = 256
SLAB = 16
FINE = 16
LANES = 128
PARTS = 4
CUTS = (768, 512, 512, 256)


def params(mebibytes=57):
    return pltpu.CompilerParams(vmem_limit_bytes=mebibytes * 1024 * 1024)


def cost():
    return pl.CostEstimate(flops=1, bytes_accessed=1, transcendentals=0)


def after(*arrays):
    return lax.optimization_barrier(arrays)


def to_sibling(block):
    return lax.ppermute(block, "chan", [(i, i ^ 1) for i in range(lax.axis_size("chan"))])


def to_chips(block, core_steps):
    devices = range(lax.axis_size("chan"))
    route = [(i, i + 2 * core_steps[i % 2]) for i in devices]
    return lax.ppermute(block, "chan", [(i, j) for i, j in route if j in devices])


def phases(first, tiles):
    tile = first + TILE * jnp.arange(tiles, dtype=jnp.int32)
    coarse = FINE * jnp.arange(TILE // FINE, dtype=jnp.int32)
    freqs = jnp.concatenate([tile, coarse, jnp.arange(FINE, dtype=jnp.int32)])
    lagvec = jnp.arange(LAGS, dtype=jnp.int32) - LAGS // 2
    phase = jnp.mod(freqs[:, None] * lagvec[None, :], 2 * NF)
    theta = 2.0 * math.pi / (2 * NF) * phase.astype(jnp.float32)
    scale = jnp.where(jnp.arange(len(freqs)) < tiles, 1.0 / math.sqrt(NF), 1.0)[:, None]
    return jnp.stack([jnp.cos(theta) * scale, -jnp.sin(theta) * scale], axis=1)


def turned(one, other):
    return one[0] * other[0] - one[1] * other[1], one[1] * other[0] + one[0] * other[1]


def planes_kernel(column, core_ref, *refs):
    count = (len(refs) - 4) // 2
    for n, records_ref in enumerate(refs[:2]):
        *planes_refs, power_ref = refs[2 + n * (count + 1) : 2 + (n + 1) * (count + 1)]
        channels, _, width = records_ref.shape
        width -= column
        for s in range(0, channels, SLAB):
            planes = jnp.swapaxes(records_ref[s : s + SLAB, :, column:], 0, 1)
            start = 0
            for ref in planes_refs:
                cut = ref.shape[2]
                ref[:, s : s + SLAB, :] = planes[:, :, start : start + cut]
                start += cut
            re, im = planes[0].astype(jnp.float32), planes[1].astype(jnp.float32)
            power = re * re + im * im
            total = power[:, :LANES]
            for f in range(LANES, width, LANES):
                total += power[:, f : f + LANES]
            power_ref[s : s + SLAB, :] = total


def planes(records, core, start, cuts):
    half = records.shape[0] // 2
    width = sum(cuts)
    loaded = width if start == 0 else records.shape[2]
    block = 128
    steps = half // block
    outs = [pl.BlockSpec((2, block, cut), lambda t, c: (0, t, 0)) for cut in cuts]
    outs += [pl.BlockSpec((block, LANES), lambda t, c: (t, 0))]
    shapes = [jax.ShapeDtypeStruct((2, half, cut), jnp.bfloat16) for cut in cuts]
    shapes += [jax.ShapeDtypeStruct((half, LANES), jnp.float32)]
    spec = pltpu.PrefetchScalarGridSpec(
        num_scalar_prefetch=1,
        grid=(steps,),
        in_specs=[
            pl.BlockSpec((block, 2, loaded), lambda t, c: (c[0] * steps + t, 0, 0)),
            pl.BlockSpec((block, 2, loaded), lambda t, c: ((1 - c[0]) * steps + t, 0, 0)),
        ],
        out_specs=outs * 2,
    )
    results = pl.pallas_call(
        functools.partial(planes_kernel, start),
        grid_spec=spec,
        out_shape=shapes * 2,
        compiler_params=params(),
        cost_estimate=cost(),
        name="planes",
    )(core, records, records)
    n = len(cuts)
    return list(results[:n]), results[n], list(results[n + 1 : -1]), results[-1]


def load(ref, rows):
    return ref[0, rows, :].astype(jnp.float32), ref[1, rows, :].astype(jnp.float32)


def whiten(spectrum, level):
    re, im = spectrum
    inverse = pltpu.reciprocal(re * re + im * im + level, approx=True)
    return (
        (re * inverse).astype(jnp.bfloat16).astype(jnp.float32),
        (im * inverse).astype(jnp.bfloat16).astype(jnp.float32),
    )


def pairs_kernel(is_first, is_last, core, row_ref, own, sib, from_own, from_sib, *refs):
    levels, tile_ref, coarse_ref, fine_ref, *refs = refs
    total_in = None if is_first else refs.pop(0)
    out_ref, onehot, table, *refs = refs
    total = refs.pop(0) if is_last else out_ref
    step = pl.program_id(0)
    count = own.shape[1] // len(refs)

    @pl.when(step == 0)
    def _():
        bins, pairs = onehot.shape
        for k in range(0, pairs, 256):
            bin_row = lax.broadcasted_iota(jnp.int32, (bins, 256), 0)
            hit = bin_row == row_ref[:, k : k + 256]
            onehot[:, k : k + 256] = jnp.where(hit, 1.0, 0.0).astype(jnp.bfloat16)

    def fill_table():
        coarse = turned(
            (tile_ref[0, 0:1, :], tile_ref[0, 1:2, :]), (coarse_ref[0], coarse_ref[1])
        )
        for a in range(TILE // FINE):
            rows = slice(a * FINE, (a + 1) * FINE)
            cos, sin = turned([part[a : a + 1, :] for part in coarse], (fine_ref[0], fine_ref[1]))
            table[rows, :] = cos.astype(jnp.bfloat16)
            table[TILE + a * FINE : TILE + (a + 1) * FINE, :] = sin.astype(jnp.bfloat16)

    def products(prods, start, even, odd, even_level, prev, after):
        for s in range(0, count, SLAB):
            rows = slice(start + s, start + s + SLAB)

            def put(slot, receiver, source):
                rre, rim = receiver
                wre, wim = source
                to = slice(slot * count + s, slot * count + s + SLAB)
                prods[to, :TILE] = (rre * wre + rim * wim).astype(jnp.bfloat16)
                prods[to, TILE:] = (rim * wre - rre * wim).astype(jnp.bfloat16)

            even_rec, odd_rec = load(even, rows), load(odd, rows)
            even_white = whiten(even_rec, levels[rows, even_level : even_level + 1])
            prev_white = whiten(load(prev, rows), levels[rows, 2:3])
            put(0, odd_rec, even_white)
            put(1, even_rec, prev_white)
            put(2, odd_rec, prev_white)
            put(3, load(after, rows), even_white)

    def run(*blocks):
        fill_table()
        stack = None
        for part, prods in enumerate(refs):
            products(prods, part * count, *blocks)
            pairs = slice(part * 4 * count, (part + 1) * 4 * count)
            sums = jnp.dot(onehot[:, pairs], prods[...], preferred_element_type=jnp.float32)
            stack = sums if stack is None else stack + sums
        high = stack.astype(jnp.bfloat16)
        low = (stack - high.astype(jnp.float32)).astype(jnp.bfloat16)
        lagged = jnp.dot(high, table[...], preferred_element_type=jnp.float32)
        lagged += jnp.dot(low, table[...], preferred_element_type=jnp.float32)

        @pl.when(step == 0)
        def _():
            total[...] = lagged if is_first else total_in[...] + lagged

        @pl.when(step > 0)
        def _():
            total[...] += lagged

    pl.when(core[0] == 0)(lambda: run(own, sib, 0, from_sib, from_own))
    pl.when(core[0] != 0)(lambda: run(sib, own, 1, from_own, from_sib))

    if is_last:
        parts, rows, lags = out_ref.shape
        bands = total.shape[1] // lags

        @pl.when(step == pl.num_programs(0) - 1)
        def _():
            for part in range(parts):
                r, f = part // bands * rows, part % bands * lags
                out_ref[part] = total[r : r + rows, f : f + lags].astype(jnp.bfloat16)


def add_pairs(first, core, row, own, sib, from_own, from_sib, levels, phase, total, out, bins):
    cut = own.shape[2]
    pairs = row.shape[1]
    by_tile, coarse, fine = phase

    def whole(array):
        return pl.BlockSpec(array.shape, lambda t: (0,) * array.ndim)

    def columns(array):
        return pl.BlockSpec((2, array.shape[1], TILE), lambda t: (0, 0, t))

    blocks = [own, sib, from_own, from_sib]
    ins = [core, row, *blocks, levels, by_tile, coarse, fine]
    specs = [pl.BlockSpec(memory_space=pltpu.SMEM), whole(row)]
    specs += [columns(b) for b in blocks] + [whole(levels)]
    specs += [pl.BlockSpec((1, 2, LAGS), lambda t: (t + first, 0, 0)), whole(coarse), whole(fine)]
    scratch = [pltpu.VMEM((bins, pairs), jnp.bfloat16), pltpu.VMEM((2 * TILE, LAGS), jnp.bfloat16)]
    if total is not None:
        ins.append(total)
        specs.append(whole(total))
    is_last = out is not None
    if is_last:
        scratch.append(pltpu.VMEM((bins, LAGS), jnp.float32))
    else:
        out = jax.ShapeDtypeStruct((bins, LAGS), jnp.float32)
    return pl.pallas_call(
        functools.partial(pairs_kernel, total is None, is_last),
        grid=(cut // TILE,),
        in_specs=specs,
        out_specs=whole(out),
        out_shape=out,
        scratch_shapes=scratch
        + [pltpu.VMEM((pairs // PARTS, 2 * TILE), jnp.bfloat16)] * PARTS,
        compiler_params=params(40),
        cost_estimate=cost(),
        name="add_pairs",
    )(*ins)


def shards(records, chan_pos, bin_row, pair_mask):
    here = lax.axis_index("chan")
    core, chip = here % 2, here // 2
    blocks, bands = lax.axis_size("chan"), lax.axis_size("freq")
    width, _, band = records.shape
    half = width // 2
    bins = bin_row.shape[0]

    core_ref = core.astype(jnp.int32)[None]
    own, own_power, give, give_power = planes(records, core_ref, 0, CUTS[:1])
    sib = [to_sibling(give[0])]
    moved = [to_chips(own[0], (-1, 1)), to_chips(sib[0], (1, -1))]
    records, sib[0] = after(records, sib[0])
    rest_own, more_own, rest, more_give = planes(records, core_ref, CUTS[0], CUTS[1:])
    own, own_power, give_power = own + rest_own, own_power + more_own, give_power + more_give

    totals = lax.psum(jnp.sum(jnp.stack([own_power, give_power]), axis=2), "freq")
    mask = pair_mask[0].astype(jnp.float32)
    own_info = jnp.concatenate([totals[0], mask])
    sib_info = to_sibling(jnp.concatenate([totals[1], mask]))
    own_info_moved = to_chips(own_info, (-1, 1))
    sib_info_moved = to_chips(sib_info, (1, -1))
    own[1], own_info_moved = after(own[1], own_info_moved)

    first, sib_info = after(lax.axis_index("freq") * band, sib_info)
    phase = phases(first, band // TILE)

    phase = phase[: band // TILE], *phase[band // TILE :].reshape(2, FINE, 2, LAGS).swapaxes(1, 2)

    sib += [to_sibling(block) for block in rest]
    sib[1], sib_info_moved, moved[1] = after(sib[1], sib_info_moved, moved[1])
    moved += [to_chips(own[1], (-1, 1)), to_chips(sib[1], (1, -1))]

    even_mask = jnp.where(core == 0, mask, sib_info[half:])
    odd_mask = jnp.where(core == 0, sib_info[half:], mask)
    prev_info = jnp.where(core == 0, sib_info_moved, own_info_moved)
    next_info = jnp.where(core == 0, own_info_moved, sib_info_moved)

    totals = jnp.stack([own_info[:half], sib_info[:half], prev_info[:half]], axis=1)
    levels = water * totals / NF + tiny

    places = jnp.pad(chan_pos.reshape(blocks, width), ((1, 1), (0, 0)))
    places = lax.dynamic_slice(places, (2 * chip, core * half), (4, half))
    prev_pos, even_pos, odd_pos, next_pos = places
    apart = jnp.abs(
        jnp.concatenate(
            [odd_pos - even_pos, even_pos - prev_pos, odd_pos - prev_pos, next_pos - even_pos]
        )
    )
    used = jnp.stack(
        [
            odd_mask[0] > 0,
            (even_mask[0] > 0) & (chip > 0),
            (odd_mask[1] > 0) & (chip > 0),
            (next_info[half + 1] > 0) & (chip < blocks // 2 - 1),
        ]
    )
    bin_ids = jnp.arange(bins, dtype=jnp.int32)
    row = jnp.sum(jnp.where(apart[:, None] == bin_ids[None, :], bin_row[None, :], 0), axis=1)
    row = jnp.where(jnp.repeat(used, half), row, -1)
    row = row.reshape(4, PARTS, half // PARTS).transpose(1, 0, 2).reshape(-1)

    out = jax.ShapeDtypeStruct((blocks * bands, bins // blocks, LAGS // bands), jnp.bfloat16)
    total, start = None, 0
    for k, cut in enumerate(CUTS):
        arrays = own[k], sib[k], moved[2 * k], moved[2 * k + 1]
        goal = out if k == len(CUTS) - 1 else None
        total = add_pairs(
            start // TILE, core_ref, row[None, :], *arrays, levels, phase, total, goal, bins
        )
        if k + 2 < len(CUTS):
            own[k + 2], sib[k + 2], total = after(own[k + 2], sib[k + 2], total)
            moved += [to_chips(own[k + 2], (-1, 1)), to_chips(sib[k + 2], (1, -1))]
        start += cut

    parts = lax.all_to_all(total, ("chan", "freq"), 0, 0, tiled=True)
    return jnp.sum(parts.astype(jnp.float32), axis=0)


def solution(mesh):
    placed = (P("chan", None, "freq"), P(), P(), P("chan", None))
    return jax.shard_map(
        shards, mesh=mesh, in_specs=placed, out_specs=P("chan", "freq"), check_vma=False
    )
```

time: 489 us -> 155 us (0.32)
  waiting for transfers between devices: 161 us -> 13.4 us
  other arithmetic: 127 us -> 9.98 us
  matrix products: 60.8 us -> 0 us
  starting transfers between devices: 89.8 us -> 32.9 us
  Pallas kernels: 0 us -> 46.6 us
  blocking collectives: 10.6 us -> 45.7 us
  local copies, waits for them, and re-layouts: 24.4 us -> 2.29 us
  between operations: 14.7 us -> 2.31 us
    reduce_scatter x2 -> x0, waiting for transfers between devices: 151 us -> none  [the longest x1 80.7 us: shards(): lax.psum_scatter(partial_lags, 'chan', scatter_dimension=0, tiled=True)]
    dot_general x3 -> x0, matrix products: 60.8 us -> none  [the longest x1 40.1 us: shards(): lagged = jnp.dot(stack, table, precision=lax.Precision.HIGHEST)]
    ppermute x2 -> x15, starting transfers between devices: 89.8 us -> 32.9 us  [the longest x10 30.9 us: to_chips(): lax.ppermute(block, 'chan', [(i, j) for i, j in route if j in devices])]
    pallas_call x0 -> x6, Pallas kernels: none -> 46.6 us  [the longest x4 33.4 us: add_pairs(): pl.pallas_call(functools.partial(pairs_kernel, total is None, is_last), g...]
    convert_element_type x4 -> x2, other arithmetic: 42.5 us -> 0.15 us  [the longest x1 0.14 us: phases(): theta = 2.0 * math.pi / (2 * NF) * phase.astype(jnp.float32)]
    all_to_all x0 -> x1, blocking collectives: none -> 34.9 us  [shards(): parts = lax.all_to_all(total, ('chan', 'freq'), 0, 0, tiled=True)]
    another operation x2 -> x3, other arithmetic: 33.6 us -> 1.43 us  [the longest x1 1.11 us: shards(): jnp.stack([own_power, give_power])]
    mul x1 -> x2, other arithmetic: 35.7 us -> 5 us  [the longest x1 4.99 us: phases(): return jnp.stack([jnp.cos(theta) * scale, -jnp.sin(theta) * scale], axis=1)]
  transfers between devices with their start and end apart: 4 -> 15, of which waited for: 3 -> 5; matrix products, arithmetic and copies ran while one was open for 10% -> 7% of each run, Pallas kernels for 0% -> 24%
where the time goes in v2:
time: 155 us; the launch traced here: 153 us
  Pallas kernels  46.6 us (30%)
  blocking collectives  45.7 us (29%)
  starting transfers between devices  32.9 us (21%)
  waiting for transfers between devices  13.4 us (9%)
  other arithmetic  9.98 us (6%)
  between operations  2.31 us (1%)
  local copies, waits for them, and re-layouts  2.29 us (1%)
    all_to_all x1, blocking collectives, shards(): parts = lax.all_to_all(total, ('chan', 'freq'), 0, 0, tiled=True)  34.9 us
    pallas_call x4, Pallas kernels, add_pairs(): pl.pallas_call(functools.partial(pairs_kernel, total is None, is_last), g...  33.4 us
    ppermute x10, starting transfers between devices, to_chips(): lax.ppermute(block, 'chan', [(i, j) for i, j in route if j in devices])  30.9 us
    pallas_call x2, Pallas kernels, planes(): pl.pallas_call(functools.partial(planes_kernel, start), grid_spec=spec, o...  13.2 us
    ppermute x10, waiting for transfers between devices, to_chips(): lax.ppermute(block, 'chan', [(i, j) for i, j in route if j in devices])  12.4 us
    psum x1, blocking collectives, shards(): lax.psum(jnp.sum(jnp.stack([own_power, give_power]), axis=2), 'freq')  10.8 us
    mul x1, other arithmetic, phases(): return jnp.stack([jnp.cos(theta) * scale, -jnp.sin(theta) * scale], axis=1)  4.99 us
  transfers between devices with their start and end apart: 15, of which 5 were waited for; matrix products, arithmetic and copies ran while one was open for 7% of the time, Pallas kernels for 24%

profile of v2, /device:TPU:0, one launch (start us, length us, event | category | flops | bytes accessed | tf_op | source)
XLA Modules:
  0.0 153.1 jit_solution(9582210700279150861)
XLA Ops:
  0.0 5.2 %planes.2 = (bf16[2,512,768]{2,1,0:T(8,128)(2,1)}, f32[512,128]{1,0:T(8,128)}, bf16[2,512,768]{2,1,0:T(8,128)(2,1)}, f32[512,128]{1,0:T(8,128)}) custom-call(s32[1]{0:T(128)} %bitcast.core_ref.core, bf16[1024,2,2048]{2,1,0:T(2,128)(2,1)} %refs_1_.2, bf16[1024,2,2048]{2,1,0:T(2,128)(2,1)} %refs_1_.2), custom_call_target="tpu_custom_call" | custom-call | flops 1 | bytes 1 | tf_op jit(solution)/shard_map/planes/pallas_call | solution.py:102
  5.2 1.3 collective-permute-start.10
  6.9 1.0 select_reduce_fusion
  7.9 1.0 collective-permute-done.sib
  8.9 7.9 %planes.3 = (bf16[2,512,512]{2,1,0:T(8,128)(2,1)}, bf16[2,512,512]{2,1,0:T(8,128)(2,1)}, bf16[2,512,256]{2,1,0:T(8,128)(2,1)}, f32[512,128]{1,0:T(8,128)}, bf16[...) custom-call(s32[1]{0:T(128)} %bitcast.core_ref.core, ...), custom_call_target="tpu_custom_call" | custom-call | flops 1 | bytes 1 | tf_op jit(solution)/shard_map/planes/pallas_call | solution.py:102
  16.8 1.1 add_bitcast_fusion
  18.1 10.8 %psum.7 = f32[2,512]{1,0:T(2,128)S(1)} all-reduce(f32[2,512]{1,0:T(2,128)S(1)} %maximum_reduce_fusion), channel_id=1, replica_groups=mesh['chan'=32,'freq'=4] {'freq'}, use_global_device_ids=true, to_apply=%region_1.2 | all-reduce | flops 1024 | bytes 8192 | tf_op jit(solution)/shard_map/psum | solution.py:262
  28.9 1.0 collective-permute-start.1
  30.0 4.1 %collective-permute-start.5 = (bf16[2,512,768]{2,1,0:T(8,128)(2,1)S(1)}, bf16[2,512,768]{2,1,0:T(8,128)(2,1)}, u32[]{:S(2)}, u32[]{:S(2)}) collective-permute-start(bf16[2,512,768]{2,1,0:T(8,128)(2,1)S(1)} %collective-permute-done.sib), channel_id=1, source_target_pairs={{0,8},{8,16},{12,4},{16,24},{20,12},{24,32},{28,20},{32,40},{36,28... | collective-permute-start | bytes 4718600 | tf_op jit(solution)/shard_map/ppermute | solution.py:44
  34.1 1.3 collective-permute-start.2
  36.2 5.0 %cosine_multiply_fusion = (f32[40,1,1024]{2,1,0:T(1,128)S(1)}, f32[40,1,1024]{2,1,0:T(1,128)S(1)}) fusion(f32[40]{0:T(128)S(1)} %compare_select_fusion, f32[40,1,1024]{2,0,1:T(8,128)S(1)} %fusion), kind=kLoop, calls=%fused_computation.21 | loop fusion | flops 163840 | bytes 491680 | tf_op jit(solution)/shard_map/mul | solution.py:55
  41.7 4.5 %collective-permute-start.4 = (f32[514]{0:T(1024)S(1)}, f32[514]{0:T(1024)S(1)}, u32[]{:S(2)}, u32[]{:S(2)}) collective-permute-start(f32[514]{0:T(1024)S(1)} %collective-permute-done.1), channel_id=1, source_target_pairs={{0,8},{8,16},{12,4},{16,24},{20,12},{24,32},{28,20},{32,40},{36,28... | collective-permute-start | bytes 6176 | tf_op jit(solution)/shard_map/ppermute | solution.py:44
  46.2 0.6 fusion.5
  48.1 2.9 %collective-permute-done.4 = f32[514]{0:T(1024)S(1)} collective-permute-done((f32[514]{0:T(1024)S(1)}, f32[514]{0:T(1024)S(1)}, u32[]{:S(2)}, u32[]{:S(2)}) %collective-permute-start.4) | collective-permute-done | bytes 2088 | tf_op jit(solution)/shard_map/ppermute | solution.py:44
  51.3 1.3 collective-permute-start.7
  52.6 0.9 copy.22
  53.5 0.6 slice.40
  54.7 5.7 %collective-permute-start.8 = (bf16[2,512,512]{2,1,0:T(8,128)(2,1)}, bf16[2,512,512]{2,1,0:T(8,128)(2,1)}, u32[]{:S(2)}, u32[]{:S(2)}) collective-permute-start(bf16[2,512,512]{2,1,0:T(8,128)(2,1)} %collective-permute-done.3.sib), channel_id=1, source_target_pairs={{0,8},{8,16},{12,4},{16,24},{20,12},{24,32},{28,20},{32,40},{36,28... | collective-permute-start | bytes 3145736 | tf_op jit(solution)/shard_map/ppermute | solution.py:44
  60.6 1.0 broadcast_add_fusion.refs_0_
  61.6 11.8 %add_pairs.4.refs_4_ = f32[512,1024]{1,0:T(8,128)S(1)} custom-call(s32[1]{0:T(128)} %bitcast.core_ref.core, s32[1,2048]{1,0:T(1,128)S(1)} %bitcast.40, bf16[2,512,768]{2,1,0:T(8,128)(2,1)S(1)} %copy-done, bf16[2,512,768]{2,1,0:T(8,128)(2,1)S(1)} %collective-permute-done.sib, bf16[2,512,768]{2,1,0:T(8,128)(2,1)} %collective-permute-done.10.from_own, ...), custom_call_target="tpu_custom_call" | custom-call | flops 1 | bytes 1 | tf_op jit(solution)/shard_map/add_pairs/pallas_call | solution.py:232
  73.5 1.4 collective-permute-start.13
  74.9 4.8 %collective-permute-start.14 = (bf16[2,512,512]{2,1,0:T(8,128)(2,1)}, bf16[2,512,512]{2,1,0:T(8,128)(2,1)S(1)}, u32[]{:S(2)}, u32[]{:S(2)}) collective-permute-start(bf16[2,512,512]{2,1,0:T(8,128)(2,1)} %collective-permute-done.9.sib), channel_id=1, source_target_pairs={{0,8},{8,16},{12,4},{16,24},{20,12},{24,32},{28,20},{32,40},{36,28... | collective-permute-start | bytes 3145736 | tf_op jit(solution)/shard_map/ppermute | solution.py:44
  79.8 8.5 %add_pairs.5.refs_4_ = f32[512,1024]{1,0:T(8,128)S(1)} custom-call(s32[1]{0:T(128)} %bitcast.core_ref.core, s32[1,2048]{1,0:T(1,128)S(1)} %bitcast.41, bf16[2,512,512]{2,1,0:T(8,128)(2,1)S(1)} %copy-done.2, bf16[2,512,512]{2,1,0:T(8,128)(2,1)} %collective-permute-done.3.sib, bf16[2,512,512]{2,1,0:T(8,128)(2,1)} %collective-permute-done.7.from_own, ...), custom_call_target="tpu_custom_call" | custom-call | flops 1 | bytes 1 | tf_op jit(solution)/shard_map/add_pairs/pallas_call | solution.py:232
  88.3 1.3 collective-permute-start.11
  89.6 5.1 %collective-permute-start.12 = (bf16[2,512,256]{2,1,0:T(8,128)(2,1)}, bf16[2,512,256]{2,1,0:T(8,128)(2,1)S(1)}, u32[]{:S(2)}, u32[]{:S(2)}) collective-permute-start(bf16[2,512,256]{2,1,0:T(8,128)(2,1)} %collective-permute-done.6.sib), channel_id=1, source_target_pairs={{0,8},{8,16},{12,4},{16,24},{20,12},{24,32},{28,20},{32,40},{36,28... | collective-permute-start | bytes 1572872 | tf_op jit(solution)/shard_map/ppermute | solution.py:44
  94.7 4.4 %collective-permute-done.13.from_own = bf16[2,512,512]{2,1,0:T(8,128)(2,1)S(1)} collective-permute-done((bf16[2,512,512]{2,1,0:T(8,128)(2,1)S(1)}, bf16[2,512,512]{2,1,0:T(8,128)(2,1)S(1)}, u32[]{:S(2)}, u32[]{:S(2)}) %collective-permute-start.13) | collective-permute-done | bytes 1048608 | tf_op jit(solution)/shard_map/ppermute | solution.py:44
  99.1 4.3 %collective-permute-done.14.from_sib = bf16[2,512,512]{2,1,0:T(8,128)(2,1)S(1)} collective-permute-done((bf16[2,512,512]{2,1,0:T(8,128)(2,1)}, bf16[2,512,512]{2,1,0:T(8,128)(2,1)S(1)}, u32[]{:S(2)}, u32[]{:S(2)}) %collective-permute-start.14) | collective-permute-done | bytes 1048608 | tf_op jit(solution)/shard_map/ppermute | solution.py:44
  103.4 8.2 %add_pairs.6.refs_4_ = f32[512,1024]{1,0:T(8,128)S(1)} custom-call(s32[1]{0:T(128)} %bitcast.core_ref.core, s32[1,2048]{1,0:T(1,128)S(1)} %bitcast.42, bf16[2,512,512]{2,1,0:T(8,128)(2,1)S(1)} %copy-done.1, bf16[2,512,512]{2,1,0:T(8,128)(2,1)} %collective-permute-done.9.sib, bf16[2,512,512]{2,1,0:T(8,128)(2,1)S(1)} %collective-permute-done.13.from_own, ...), custom_call_target="tpu_custom_call" | custom-call | flops 1 | bytes 1 | tf_op jit(solution)/shard_map/add_pairs/pallas_call | solution.py:232
  111.6 0.9 collective-permute-done.12.from_sib
  112.5 4.9 %add_pairs.7 = bf16[128,16,256]{2,1,0:T(8,128)(2,1)S(1)} custom-call(s32[1]{0:T(128)} %bitcast.core_ref.core, s32[1,2048]{1,0:T(1,128)S(1)} %bitcast.43, bf16[2,512,256]{2,1,0:T(8,128)(2,1)S(1)} %copy-done.3, bf16[2,512,256]{2,1,0:T(8,128)(2,1)} %collective-permute-done.6.sib, bf16[2,512,256]{2,1,0:T(8,128)(2,1)S(1)} %collective-permute-done.11.from_own, ...), custom_call_target="tpu_custom_call" | custom-call | flops 1 | bytes 1 | tf_op jit(solution)/shard_map/add_pairs/pallas_call | solution.py:232
  117.4 34.9 %all_to_all.5 = bf16[128,16,256]{2,1,0:T(8,128)(2,1)S(1)} all-to-all(bf16[128,16,256]{2,1,0:T(8,128)(2,1)S(1)} %add_pairs.7), channel_id=1, replica_groups=mesh['chan'=32,'freq'=4] {'chan','freq'}, dimensions={0} | all-to-all | bytes 2097152 | tf_op jit(solution)/shard_map/all_to_all | solution.py:321
  152.3 0.8 convert_reduce_fusion
  (60 shorter events, 2.3 us)
Async XLA Ops:
  0.0 6.6 %copy-start.6 = (s32[32768]{0:T(1024)S(1)}, s32[32768]{0:T(1024)}, u32[]{:S(2)}) copy-start(s32[32768]{0:T(1024)} %param.5) | copy-start | bytes 393220
  0.0 6.9 %copy-start.7 = (s32[512]{0:T(512)S(1)}, s32[512]{0:T(512)}, u32[]{:S(2)}) copy-start(s32[512]{0:T(512)} %param.6) | copy-start | bytes 6148
  0.0 7.8 %copy-start.8 = (s32[1,2]{1,0:T(1,128)S(1)}, s32[1,2]{1,0:T(1,128)}, u32[]{:S(2)}) copy-start(s32[1,2]{1,0:T(1,128)} %param.7) | copy-start | bytes 28
  5.2 3.6 %collective-permute-start = (bf16[2,512,768]{2,1,0:T(8,128)(2,1)}, bf16[2,512,768]{2,1,0:T(8,128)(2,1)S(1)}, u32[]{:S(2)}, u32[]{:S(2)}) collective-permute-start(bf16[2,512,768]{2,1,0:T(8,128)(2,1)} %get-tuple-element.33), channel_id=1, source_target_pairs={{0,4},{4,0},{8,12},{12,8},{16,20},{20,16},{24,28},{28,24},{32,36},... | collective-permute-start | bytes 4718600 | tf_op jit(solution)/shard_map/ppermute | solution.py:38
  5.2 56.3 %collective-permute-start.10 = (bf16[2,512,768]{2,1,0:T(8,128)(2,1)}, bf16[2,512,768]{2,1,0:T(8,128)(2,1)}, u32[]{:S(2)}, u32[]{:S(2)}) collective-permute-start(bf16[2,512,768]{2,1,0:T(8,128)(2,1)} %get-tuple-element.50.own), channel_id=1, source_target_pairs={{4,12},{8,0},{12,20},{16,8},{20,28},{24,16},{28,36},{32,24},{36,44... | collective-permute-start | bytes 4718600 | tf_op jit(solution)/shard_map/ppermute | solution.py:44
  7.9 8.9 %copy-start.4 = (f32[512,128]{1,0:T(8,128)S(1)}, f32[512,128]{1,0:T(8,128)}, u32[]{:S(2)}) copy-start(f32[512,128]{1,0:T(8,128)} %get-tuple-element.32) | copy-start | bytes 786436
  7.9 8.9 %copy-start.5 = (f32[512,128]{1,0:T(8,128)S(1)}, f32[512,128]{1,0:T(8,128)}, u32[]{:S(2)}) copy-start(f32[512,128]{1,0:T(8,128)} %get-tuple-element.36) | copy-start | bytes 786436
  17.9 43.7 %copy-start = (bf16[2,512,768]{2,1,0:T(8,128)(2,1)S(1)}, bf16[2,512,768]{2,1,0:T(8,128)(2,1)}, u32[]{:S(2)}) copy-start(bf16[2,512,768]{2,1,0:T(8,128)(2,1)} %get-tuple-element.50.own) | copy-start | bytes 4718596
  28.9 6.6 %collective-permute-start.1 = (f32[514]{0:T(1024)S(1)}, f32[514]{0:T(1024)S(1)}, u32[]{:S(2)}, u32[]{:S(2)}) collective-permute-start(f32[514]{0:T(1024)S(1)} %get-tuple-element.78), channel_id=1, source_target_pairs={{0,4},{4,0},{8,12},{12,8},{16,20},{20,16},{24,28},{28,24},{32,36},... | collective-permute-start | bytes 6176 | tf_op jit(solution)/shard_map/ppermute | solution.py:38
  30.0 22.6 %collective-permute-start.5 = (bf16[2,512,768]{2,1,0:T(8,128)(2,1)S(1)}, bf16[2,512,768]{2,1,0:T(8,128)(2,1)}, u32[]{:S(2)}, u32[]{:S(2)}) collective-permute-start(bf16[2,512,768]{2,1,0:T(8,128)(2,1)S(1)} %collective-permute-done.sib), channel_id=1, source_target_pairs={{0,8},{8,16},{12,4},{16,24},{20,12},{24,32},{28,20},{32,40},{36,28... | collective-permute-start | bytes 4718600 | tf_op jit(solution)/shard_map/ppermute | solution.py:44
  34.1 7.6 %collective-permute-start.2 = (f32[514]{0:T(1024)S(1)}, f32[514]{0:T(1024)S(1)}, u32[]{:S(2)}, u32[]{:S(2)}) collective-permute-start(f32[514]{0:T(1024)S(1)} %get-tuple-element.79), channel_id=1, source_target_pairs={{4,12},{8,0},{12,20},{16,8},{20,28},{24,16},{28,36},{32,24},{36,44... | collective-permute-start | bytes 6176 | tf_op jit(solution)/shard_map/ppermute | solution.py:44
  35.4 15.9 %collective-permute-start.3 = (bf16[2,512,512]{2,1,0:T(8,128)(2,1)}, bf16[2,512,512]{2,1,0:T(8,128)(2,1)}, u32[]{:S(2)}, u32[]{:S(2)}) collective-permute-start(bf16[2,512,512]{2,1,0:T(8,128)(2,1)} %get-tuple-element.41), channel_id=1, source_target_pairs={{0,4},{4,0},{8,12},{12,8},{16,20},{20,16},{24,28},{28,24},{32,36},... | collective-permute-start | bytes 3145736 | tf_op jit(solution)/shard_map/ppermute | solution.py:38
  35.5 38.0 %collective-permute-start.9 = (bf16[2,512,512]{2,1,0:T(8,128)(2,1)}, bf16[2,512,512]{2,1,0:T(8,128)(2,1)}, u32[]{:S(2)}, u32[]{:S(2)}) collective-permute-start(bf16[2,512,512]{2,1,0:T(8,128)(2,1)} %get-tuple-element.49), channel_id=1, source_target_pairs={{0,4},{4,0},{8,12},{12,8},{16,20},{20,16},{24,28},{28,24},{32,36},... | collective-permute-start | bytes 3145736 | tf_op jit(solution)/shard_map/ppermute | solution.py:38
  41.7 9.3 %collective-permute-start.4 = (f32[514]{0:T(1024)S(1)}, f32[514]{0:T(1024)S(1)}, u32[]{:S(2)}, u32[]{:S(2)}) collective-permute-start(f32[514]{0:T(1024)S(1)} %collective-permute-done.1), channel_id=1, source_target_pairs={{0,8},{8,16},{12,4},{16,24},{20,12},{24,32},{28,20},{32,40},{36,28... | collective-permute-start | bytes 6176 | tf_op jit(solution)/shard_map/ppermute | solution.py:44
  50.9 37.4 %collective-permute-start.6 = (bf16[2,512,256]{2,1,0:T(8,128)(2,1)}, bf16[2,512,256]{2,1,0:T(8,128)(2,1)}, u32[]{:S(2)}, u32[]{:S(2)}) collective-permute-start(bf16[2,512,256]{2,1,0:T(8,128)(2,1)} %get-tuple-element.44), channel_id=1, source_target_pairs={{0,4},{4,0},{8,12},{12,8},{16,20},{20,16},{24,28},{28,24},{32,36},... | collective-permute-start | bytes 1572872 | tf_op jit(solution)/shard_map/ppermute | solution.py:38
  51.3 28.5 %collective-permute-start.7 = (bf16[2,512,512]{2,1,0:T(8,128)(2,1)}, bf16[2,512,512]{2,1,0:T(8,128)(2,1)}, u32[]{:S(2)}, u32[]{:S(2)}) collective-permute-start(bf16[2,512,512]{2,1,0:T(8,128)(2,1)} %get-tuple-element.45.own), channel_id=1, source_target_pairs={{4,12},{8,0},{12,20},{16,8},{20,28},{24,16},{28,36},{32,24},{36,44... | collective-permute-start | bytes 3145736 | tf_op jit(solution)/shard_map/ppermute | solution.py:44
  54.7 25.1 %collective-permute-start.8 = (bf16[2,512,512]{2,1,0:T(8,128)(2,1)}, bf16[2,512,512]{2,1,0:T(8,128)(2,1)}, u32[]{:S(2)}, u32[]{:S(2)}) collective-permute-start(bf16[2,512,512]{2,1,0:T(8,128)(2,1)} %collective-permute-done.3.sib), channel_id=1, source_target_pairs={{0,8},{8,16},{12,4},{16,24},{20,12},{24,32},{28,20},{32,40},{36,28... | collective-permute-start | bytes 3145736 | tf_op jit(solution)/shard_map/ppermute | solution.py:44
  61.6 11.9 %copy-start.1 = (bf16[2,512,512]{2,1,0:T(8,128)(2,1)S(1)}, bf16[2,512,512]{2,1,0:T(8,128)(2,1)}, u32[]{:S(2)}) copy-start(bf16[2,512,512]{2,1,0:T(8,128)(2,1)} %get-tuple-element.56.own) | copy-start | bytes 3145732
  61.6 18.2 %copy-start.2 = (bf16[2,512,512]{2,1,0:T(8,128)(2,1)S(1)}, bf16[2,512,512]{2,1,0:T(8,128)(2,1)}, u32[]{:S(2)}) copy-start(bf16[2,512,512]{2,1,0:T(8,128)(2,1)} %get-tuple-element.45.own) | copy-start | bytes 3145732
  73.5 14.8 %copy-start.3 = (bf16[2,512,256]{2,1,0:T(8,128)(2,1)S(1)}, bf16[2,512,256]{2,1,0:T(8,128)(2,1)}, u32[]{:S(2)}) copy-start(bf16[2,512,256]{2,1,0:T(8,128)(2,1)} %get-tuple-element.54.own) | copy-start | bytes 1572868
  73.5 25.6 %collective-permute-start.13 = (bf16[2,512,512]{2,1,0:T(8,128)(2,1)S(1)}, bf16[2,512,512]{2,1,0:T(8,128)(2,1)S(1)}, u32[]{:S(2)}, u32[]{:S(2)}) collective-permute-start(bf16[2,512,512]{2,1,0:T(8,128)(2,1)S(1)} %copy-done.1), channel_id=1, source_target_pairs={{4,12},{8,0},{12,20},{16,8},{20,28},{24,16},{28,36},{32,24},{36,44... | collective-permute-start | bytes 3145736 | tf_op jit(solution)/shard_map/ppermute | solution.py:44
  74.9 28.5 %collective-permute-start.14 = (bf16[2,512,512]{2,1,0:T(8,128)(2,1)}, bf16[2,512,512]{2,1,0:T(8,128)(2,1)S(1)}, u32[]{:S(2)}, u32[]{:S(2)}) collective-permute-start(bf16[2,512,512]{2,1,0:T(8,128)(2,1)} %collective-permute-done.9.sib), channel_id=1, source_target_pairs={{0,8},{8,16},{12,4},{16,24},{20,12},{24,32},{28,20},{32,40},{36,28... | collective-permute-start | bytes 3145736 | tf_op jit(solution)/shard_map/ppermute | solution.py:44
  88.3 23.2 %collective-permute-start.11 = (bf16[2,512,256]{2,1,0:T(8,128)(2,1)S(1)}, bf16[2,512,256]{2,1,0:T(8,128)(2,1)S(1)}, u32[]{:S(2)}, u32[]{:S(2)}) collective-permute-start(bf16[2,512,256]{2,1,0:T(8,128)(2,1)S(1)} %copy-done.3), channel_id=1, source_target_pairs={{4,12},{8,0},{12,20},{16,8},{20,28},{24,16},{28,36},{32,24},{36,44... | collective-permute-start | bytes 1572872 | tf_op jit(solution)/shard_map/ppermute | solution.py:44
  89.6 22.8 %collective-permute-start.12 = (bf16[2,512,256]{2,1,0:T(8,128)(2,1)}, bf16[2,512,256]{2,1,0:T(8,128)(2,1)S(1)}, u32[]{:S(2)}, u32[]{:S(2)}) collective-permute-start(bf16[2,512,256]{2,1,0:T(8,128)(2,1)} %collective-permute-done.6.sib), channel_id=1, source_target_pairs={{0,8},{8,16},{12,4},{16,24},{20,12},{24,32},{28,20},{32,40},{36,28... | collective-permute-start | bytes 1572872 | tf_op jit(solution)/shard_map/ppermute | solution.py:44

commit v3 on v2

--- a/solution.py
+++ b/solution.py
@@ -19,7 +19,7 @@
 FINE = 16
 LANES = 128
 PARTS = 4
-CUTS = (768, 512, 512, 256)
+CUTS = (1024, 768, 256)
 
 
 def params(mebibytes=57):
@@ -38,10 +38,16 @@
     return lax.ppermute(block, "chan", [(i, i ^ 1) for i in range(lax.axis_size("chan"))])
 
 
-def to_chips(block, core_steps):
-    devices = range(lax.axis_size("chan"))
+def to_chips(block, core_steps, bands=0):
+    devices, count = range(lax.axis_size("chan")), lax.axis_size("freq")
     route = [(i, i + 2 * core_steps[i % 2]) for i in devices]
-    return lax.ppermute(block, "chan", [(i, j) for i, j in route if j in devices])
+    route = [(i, j) for i, j in route if j in devices]
+    if not bands:
+        return lax.ppermute(block, "chan", route)
+    route = [
+        (i * count + f, j * count + (f + bands) % count) for i, j in route for f in range(count)
+    ]
+    return lax.ppermute(block, ("chan", "freq"), route)
 
 
 def phases(first, tiles):
@@ -52,7 +58,7 @@
     phase = jnp.mod(freqs[:, None] * lagvec[None, :], 2 * NF)
     theta = 2.0 * math.pi / (2 * NF) * phase.astype(jnp.float32)
     scale = jnp.where(jnp.arange(len(freqs)) < tiles, 1.0 / math.sqrt(NF), 1.0)[:, None]
-    return jnp.stack([jnp.cos(theta) * scale, -jnp.sin(theta) * scale], axis=1)
+    return jnp.cos(theta) * scale, -jnp.sin(theta) * scale
 
 
 def turned(one, other):
@@ -124,9 +130,9 @@
     )
 
 
-def pairs_kernel(is_first, is_last, core, row_ref, own, sib, from_own, from_sib, *refs):
-    levels, tile_ref, coarse_ref, fine_ref, *refs = refs
-    total_in = None if is_first else refs.pop(0)
+def pairs_kernel(first, is_last, core, row_ref, own, sib, from_own, from_sib, *refs):
+    levels, cos_ref, sin_ref, *refs = refs
+    total_in = refs.pop(0) if first else None
     out_ref, onehot, table, *refs = refs
     total = refs.pop(0) if is_last else out_ref
     step = pl.program_id(0)
@@ -141,12 +147,16 @@
             onehot[:, k : k + 256] = jnp.where(hit, 1.0, 0.0).astype(jnp.bfloat16)
 
     def fill_table():
-        coarse = turned(
-            (tile_ref[0, 0:1, :], tile_ref[0, 1:2, :]), (coarse_ref[0], coarse_ref[1])
+        tiles = cos_ref.shape[0] - TILE // FINE - FINE
+        start = pl.ds(first + step, 1)
+        coarse, fine = slice(tiles, tiles + TILE // FINE), slice(tiles + TILE // FINE, None)
+        turn = turned(
+            (cos_ref[start, :], sin_ref[start, :]), (cos_ref[coarse, :], sin_ref[coarse, :])
         )
+        steps = cos_ref[fine, :], sin_ref[fine, :]
         for a in range(TILE // FINE):
             rows = slice(a * FINE, (a + 1) * FINE)
-            cos, sin = turned([part[a : a + 1, :] for part in coarse], (fine_ref[0], fine_ref[1]))
+            cos, sin = turned([part[a : a + 1, :] for part in turn], steps)
             table[rows, :] = cos.astype(jnp.bfloat16)
             table[TILE + a * FINE : TILE + (a + 1) * FINE, :] = sin.astype(jnp.bfloat16)
 
@@ -184,7 +194,7 @@
 
         @pl.when(step == 0)
         def _():
-            total[...] = lagged if is_first else total_in[...] + lagged
+            total[...] = total_in[...] + lagged if first else lagged
 
         @pl.when(step > 0)
         def _():
@@ -207,7 +217,6 @@
 def add_pairs(first, core, row, own, sib, from_own, from_sib, levels, phase, total, out, bins):
     cut = own.shape[2]
     pairs = row.shape[1]
-    by_tile, coarse, fine = phase
 
     def whole(array):
         return pl.BlockSpec(array.shape, lambda t: (0,) * array.ndim)
@@ -216,10 +225,9 @@
         return pl.BlockSpec((2, array.shape[1], TILE), lambda t: (0, 0, t))
 
     blocks = [own, sib, from_own, from_sib]
-    ins = [core, row, *blocks, levels, by_tile, coarse, fine]
+    ins = [core, row, *blocks, levels, *phase]
     specs = [pl.BlockSpec(memory_space=pltpu.SMEM), whole(row)]
-    specs += [columns(b) for b in blocks] + [whole(levels)]
-    specs += [pl.BlockSpec((1, 2, LAGS), lambda t: (t + first, 0, 0)), whole(coarse), whole(fine)]
+    specs += [columns(b) for b in blocks] + [whole(levels)] + [whole(p) for p in phase]
     scratch = [pltpu.VMEM((bins, pairs), jnp.bfloat16), pltpu.VMEM((2 * TILE, LAGS), jnp.bfloat16)]
     if total is not None:
         ins.append(total)
@@ -230,7 +238,7 @@
     else:
         out = jax.ShapeDtypeStruct((bins, LAGS), jnp.float32)
     return pl.pallas_call(
-        functools.partial(pairs_kernel, total is None, is_last),
+        functools.partial(pairs_kernel, first, is_last),
         grid=(cut // TILE,),
         in_specs=specs,
         out_specs=whole(out),
@@ -263,14 +271,13 @@
     mask = pair_mask[0].astype(jnp.float32)
     own_info = jnp.concatenate([totals[0], mask])
     sib_info = to_sibling(jnp.concatenate([totals[1], mask]))
-    own_info_moved = to_chips(own_info, (-1, 1))
-    sib_info_moved = to_chips(sib_info, (1, -1))
+    own_info_moved = to_chips(own_info, (-1, 1), 1)
+    sib_info_moved = to_chips(sib_info, (1, -1), 1)
     own[1], own_info_moved = after(own[1], own_info_moved)
 
     first, sib_info = after(lax.axis_index("freq") * band, sib_info)
     phase = phases(first, band // TILE)
 
-    phase = phase[: band // TILE], *phase[band // TILE :].reshape(2, FINE, 2, LAGS).swapaxes(1, 2)
 
     sib += [to_sibling(block) for block in rest]
     sib[1], sib_info_moved, moved[1] = after(sib[1], sib_info_moved, moved[1])

time: 155 us -> 143 us (0.923)
  waiting for transfers between devices: 13.4 us -> 22.5 us
  starting transfers between devices: 32.9 us -> 25.2 us
  other arithmetic: 9.98 us -> 4.42 us
  blocking collectives: 45.7 us -> 41.4 us
  Pallas kernels: 46.6 us -> 43.4 us
    ppermute x10 -> x8, waiting for transfers between devices: 12.4 us -> 19.5 us  [the longest x6 18 us: to_chips(): return lax.ppermute(block, 'chan', route)]
    ppermute x10 -> x8, starting transfers between devices: 30.9 us -> 25 us  [the longest x6 19.5 us: to_chips(): return lax.ppermute(block, 'chan', route)]
    mul x1, other arithmetic: 4.99 us -> 0.73 us  [phases(): return (jnp.cos(theta) * scale, -jnp.sin(theta) * scale)]
    all_to_all x1, blocking collectives: 34.9 us -> 30.9 us  [shards(): parts = lax.all_to_all(total, ('chan', 'freq'), 0, 0, tiled=True)]
    pallas_call x4 -> x3, Pallas kernels: 33.4 us -> 30.4 us  [add_pairs(): pl.pallas_call(functools.partial(pairs_kernel, first, is_last), grid=(cut...]
    ppermute x5 -> x4, waiting for transfers between devices: 1 us -> 3.03 us  [to_sibling(): lax.ppermute(block, 'chan', [(i, i ^ 1) for i in range(lax.axis_size('cha...]
    ppermute x5 -> x4, starting transfers between devices: 1.97 us -> 0.17 us  [to_sibling(): lax.ppermute(block, 'chan', [(i, i ^ 1) for i in range(lax.axis_size('cha...]
  transfers between devices with their start and end apart: 15 -> 12, of which waited for: 5 -> 4; matrix products, arithmetic and copies ran while one was open for 7% -> 4% of each run, Pallas kernels for 24% -> 24%
where the time goes in v3:
time: 143 us; the launch traced here: 141 us
  Pallas kernels  43.4 us (30%)
  blocking collectives  41.4 us (29%)
  starting transfers between devices  25.2 us (18%)
  waiting for transfers between devices  22.5 us (16%)
  other arithmetic  4.42 us (3%)
  between operations  2.42 us (2%)
  local copies, waits for them, and re-layouts  1.49 us (1%)
    all_to_all x1, blocking collectives, shards(): parts = lax.all_to_all(total, ('chan', 'freq'), 0, 0, tiled=True)  30.9 us
    pallas_call x3, Pallas kernels, add_pairs(): pl.pallas_call(functools.partial(pairs_kernel, first, is_last), grid=(cut...  30.4 us
    ppermute x6, starting transfers between devices, to_chips(): return lax.ppermute(block, 'chan', route)  19.5 us
    ppermute x6, waiting for transfers between devices, to_chips(): return lax.ppermute(block, 'chan', route)  18 us
    pallas_call x2, Pallas kernels, planes(): pl.pallas_call(functools.partial(planes_kernel, start), grid_spec=spec, o...  13 us
    psum x1, blocking collectives, shards(): lax.psum(jnp.sum(jnp.stack([own_power, give_power]), axis=2), 'freq')  10.5 us
    ppermute x2, starting transfers between devices, to_chips(): return lax.ppermute(block, ('chan', 'freq'), route)  5.52 us
    ppermute x4, waiting for transfers between devices, to_sibling(): lax.ppermute(block, 'chan', [(i, i ^ 1) for i in range(lax.axis_size('cha...  3.03 us
  transfers between devices with their start and end apart: 12, of which 4 were waited for; matrix products, arithmetic and copies ran while one was open for 4% of the time, Pallas kernels for 24%

profile of v3, /device:TPU:0, one launch (start us, length us, event | category | flops | bytes accessed | tf_op | source)
XLA Modules:
  0.0 140.9 jit_solution(12284189176340706914)
XLA Ops:
  0.0 6.0 %planes.2 = (bf16[2,512,1024]{2,1,0:T(8,128)(2,1)}, f32[512,128]{1,0:T(8,128)}, bf16[2,512,1024]{2,1,0:T(8,128)(2,1)}, f32[512,128]{1,0:T(8,128)}) custom-call(s32[1]{0:T(128)} %bitcast.core_ref.core, bf16[1024,2,2048]{2,1,0:T(2,128)(2,1)} %refs_1_.2, bf16[1024,2,2048]{2,1,0:T(2,128)(2,1)} %refs_1_.2), custom_call_target="tpu_custom_call" | custom-call | flops 1 | bytes 1 | tf_op jit(solution)/shard_map/planes/pallas_call | solution.py:108
  6.0 1.3 collective-permute-start.7
  7.4 0.1 fusion.4
  7.5 3.0 %collective-permute-done.sib = bf16[2,512,1024]{2,1,0:T(8,128)(2,1)} collective-permute-done((bf16[2,512,1024]{2,1,0:T(8,128)(2,1)}, bf16[2,512,1024]{2,1,0:T(8,128)(2,1)}, u32[]{:S(2)}, u32[]{:S(2)}) %collective-permute-start) | collective-permute-done | bytes 2097184 | tf_op jit(solution)/shard_map/ppermute | solution.py:38
  10.5 5.3 %collective-permute-start.5 = (bf16[2,512,1024]{2,1,0:T(8,128)(2,1)}, bf16[2,512,1024]{2,1,0:T(8,128)(2,1)}, u32[]{:S(2)}, u32[]{:S(2)}) collective-permute-start(bf16[2,512,1024]{2,1,0:T(8,128)(2,1)} %collective-permute-done.sib), channel_id=1, source_target_pairs={{0,8},{8,16},{12,4},{16,24},{20,12},{24,32},{28,20},{32,40},{36,28... | collective-permute-start | bytes 6291464 | tf_op jit(solution)/shard_map/ppermute | solution.py:46
  15.8 0.1 fusion.5
  15.9 1.0 select_reduce_fusion
  16.9 7.0 %planes.3 = (bf16[2,512,768]{2,1,0:T(8,128)(2,1)}, bf16[2,512,256]{2,1,0:T(8,128)(2,1)}, f32[512,128]{1,0:T(8,128)}, bf16[2,512,768]{2,1,0:T(8,128)(2,1)}, bf16[...) custom-call(s32[1]{0:T(128)} %bitcast.core_ref.core, bf16[1024,2,2048]{2,1,0:T(2,128)(2,1)} %refs_1_.2, ...), custom_call_target="tpu_custom_call" | custom-call | flops 1 | bytes 1 | tf_op jit(solution)/shard_map/planes/pallas_call | solution.py:108
  23.9 0.1 collective-permute-start.3
  24.1 1.2 add_bitcast_fusion
  25.3 0.2 maximum_reduce_fusion
  25.5 10.5 %psum.7 = f32[2,512]{1,0:T(2,128)S(1)} all-reduce(f32[2,512]{1,0:T(2,128)S(1)} %maximum_reduce_fusion), channel_id=1, replica_groups=mesh['chan'=32,'freq'=4] {'freq'}, use_global_device_ids=true, to_apply=%region_1.2 | all-reduce | flops 1024 | bytes 8192 | tf_op jit(solution)/shard_map/psum | solution.py:270
  36.0 0.1 collective-permute-start.1
  36.1 1.3 collective-permute-start.2
  37.4 4.2 %collective-permute-start.4 = (f32[514]{0:T(1024)S(1)}, f32[514]{0:T(1024)S(1)}, u32[]{:S(2)}, u32[]{:S(2)}) collective-permute-start(f32[514]{0:T(1024)S(1)} %collective-permute-done.1), channel_id=1, source_target_pairs={{0,9},{1,10},{2,11},{3,8},{8,17},{9,18},{10,19},{11,16},{12,5},{13... | collective-permute-start | bytes 6176 | tf_op jit(solution)/shard_map/ppermute | solution.py:50
  41.7 0.6 fusion.6
  42.4 1.5 %collective-permute-done.2 = f32[514]{0:T(1024)S(1)} collective-permute-done((f32[514]{0:T(1024)S(1)}, f32[514]{0:T(1024)S(1)}, u32[]{:S(2)}, u32[]{:S(2)}) %collective-permute-start.2) | collective-permute-done | bytes 2088 | tf_op jit(solution)/shard_map/ppermute | solution.py:50
  45.1 1.3 collective-permute-start.10
  46.5 14.4 %collective-permute-done.5.from_sib = bf16[2,512,1024]{2,1,0:T(8,128)(2,1)} collective-permute-done((bf16[2,512,1024]{2,1,0:T(8,128)(2,1)}, bf16[2,512,1024]{2,1,0:T(8,128)(2,1)}, u32[]{:S(2)}, u32[]{:S(2)}) %collective-permute-start.5) | collective-permute-done | bytes 2097184 | tf_op jit(solution)/shard_map/ppermute | solution.py:46
  60.9 5.6 %collective-permute-start.11 = (bf16[2,512,768]{2,1,0:T(8,128)(2,1)}, bf16[2,512,768]{2,1,0:T(8,128)(2,1)}, u32[]{:S(2)}, u32[]{:S(2)}) collective-permute-start(bf16[2,512,768]{2,1,0:T(8,128)(2,1)} %collective-permute-done.3.sib), channel_id=1, source_target_pairs={{0,8},{8,16},{12,4},{16,24},{20,12},{24,32},{28,20},{32,40},{36,28... | collective-permute-start | bytes 4718600 | tf_op jit(solution)/shard_map/ppermute | solution.py:46
  66.5 0.7 negate_multiply_fusion
  67.3 0.7 slice.34
  68.6 0.1 pad_add_fusion
  68.8 0.1 copy.16
  69.0 15.2 %add_pairs.3.refs_3_ = f32[512,1024]{1,0:T(8,128)S(1)} custom-call(s32[1]{0:T(128)} %bitcast.core_ref.core, s32[1,2048]{1,0:T(1,128)S(1)} %bitcast.32, bf16[2,512,1024]{2,1,0:T(8,128)(2,1)S(1)} %copy-done, bf16[2,512,1024]{2,1,0:T(8,128)(2,1)} %collective-permute-done.sib, bf16[2,512,1024]{2,1,0:T(8,128)(2,1)} %collective-permute-done.7.from_own, ...), custom_call_target="tpu_custom_call" | custom-call | flops 1 | bytes 1 | tf_op jit(solution)/shard_map/add_pairs/pallas_call | solution.py:240
  84.3 1.3 collective-permute-start.8
  85.6 4.8 %collective-permute-start.9 = (bf16[2,512,256]{2,1,0:T(8,128)(2,1)S(1)}, bf16[2,512,256]{2,1,0:T(8,128)(2,1)S(1)}, u32[]{:S(2)}, u32[]{:S(2)}) collective-permute-start(bf16[2,512,256]{2,1,0:T(8,128)(2,1)S(1)} %collective-permute-done.6.sib), channel_id=1, source_target_pairs={{0,8},{8,16},{12,4},{16,24},{20,12},{24,32},{28,20},{32,40},{36,28... | collective-permute-start | bytes 1572872 | tf_op jit(solution)/shard_map/ppermute | solution.py:46
  90.3 3.6 %collective-permute-done.11.from_sib = bf16[2,512,768]{2,1,0:T(8,128)(2,1)} collective-permute-done((bf16[2,512,768]{2,1,0:T(8,128)(2,1)}, bf16[2,512,768]{2,1,0:T(8,128)(2,1)}, u32[]{:S(2)}, u32[]{:S(2)}) %collective-permute-start.11) | collective-permute-done | bytes 1572896 | tf_op jit(solution)/shard_map/ppermute | solution.py:46
  93.9 11.6 %add_pairs.4.refs_3_ = f32[512,1024]{1,0:T(8,128)S(1)} custom-call(s32[1]{0:T(128)} %bitcast.core_ref.core, s32[1,2048]{1,0:T(1,128)S(1)} %bitcast.33, bf16[2,512,768]{2,1,0:T(8,128)(2,1)S(1)} %copy-done.1, bf16[2,512,768]{2,1,0:T(8,128)(2,1)} %collective-permute-done.3.sib, bf16[2,512,768]{2,1,0:T(8,128)(2,1)} %collective-permute-done.10.from_own, ...), custom_call_target="tpu_custom_call" | custom-call | flops 1 | bytes 1 | tf_op jit(solution)/shard_map/add_pairs/pallas_call | solution.py:240
  105.6 3.6 %add_pairs.5 = bf16[128,16,256]{2,1,0:T(8,128)(2,1)S(1)} custom-call(s32[1]{0:T(128)} %bitcast.core_ref.core, s32[1,2048]{1,0:T(1,128)S(1)} %bitcast.34, bf16[2,512,256]{2,1,0:T(8,128)(2,1)S(1)} %copy-done.2, bf16[2,512,256]{2,1,0:T(8,128)(2,1)S(1)} %collective-permute-done.6.sib, bf16[2,512,256]{2,1,0:T(8,128)(2,1)S(1)} %collective-permute-done.8.from_own, ...), custom_call_target="tpu_custom_call" | custom-call | flops 1 | bytes 1 | tf_op jit(solution)/shard_map/add_pairs/pallas_call | solution.py:240
  109.1 30.9 %all_to_all.5 = bf16[128,16,256]{2,1,0:T(8,128)(2,1)S(1)} all-to-all(bf16[128,16,256]{2,1,0:T(8,128)(2,1)S(1)} %add_pairs.5), channel_id=1, replica_groups=mesh['chan'=32,'freq'=4] {'chan','freq'}, dimensions={0} | all-to-all | bytes 2097152 | tf_op jit(solution)/shard_map/all_to_all | solution.py:328
  140.1 0.8 convert_reduce_fusion
  (46 shorter events, 0.4 us)
Async XLA Ops:
  0.0 7.3 %copy-start.5 = (s32[32768]{0:T(1024)S(1)}, s32[32768]{0:T(1024)}, u32[]{:S(2)}) copy-start(s32[32768]{0:T(1024)} %param.5) | copy-start | bytes 393220
  0.0 15.9 %copy-start.6 = (s32[512]{0:T(512)S(1)}, s32[512]{0:T(512)}, u32[]{:S(2)}) copy-start(s32[512]{0:T(512)} %param.6) | copy-start | bytes 6148
  6.0 4.5 %collective-permute-start = (bf16[2,512,1024]{2,1,0:T(8,128)(2,1)}, bf16[2,512,1024]{2,1,0:T(8,128)(2,1)}, u32[]{:S(2)}, u32[]{:S(2)}) collective-permute-start(bf16[2,512,1024]{2,1,0:T(8,128)(2,1)} %get-tuple-element.28), channel_id=1, source_target_pairs={{0,4},{4,0},{8,12},{12,8},{16,20},{20,16},{24,28},{28,24},{32,36},... | collective-permute-start | bytes 6291464 | tf_op jit(solution)/shard_map/ppermute | solution.py:38
  6.0 63.0 %collective-permute-start.7 = (bf16[2,512,1024]{2,1,0:T(8,128)(2,1)}, bf16[2,512,1024]{2,1,0:T(8,128)(2,1)}, u32[]{:S(2)}, u32[]{:S(2)}) collective-permute-start(bf16[2,512,1024]{2,1,0:T(8,128)(2,1)} %get-tuple-element.40.own), channel_id=1, source_target_pairs={{4,12},{8,0},{12,20},{16,8},{20,28},{24,16},{28,36},{32,24},{36,44... | collective-permute-start | bytes 6291464 | tf_op jit(solution)/shard_map/ppermute | solution.py:46
  10.5 50.4 %collective-permute-start.5 = (bf16[2,512,1024]{2,1,0:T(8,128)(2,1)}, bf16[2,512,1024]{2,1,0:T(8,128)(2,1)}, u32[]{:S(2)}, u32[]{:S(2)}) collective-permute-start(bf16[2,512,1024]{2,1,0:T(8,128)(2,1)} %collective-permute-done.sib), channel_id=1, source_target_pairs={{0,8},{8,16},{12,4},{16,24},{20,12},{24,32},{28,20},{32,40},{36,28... | collective-permute-start | bytes 6291464 | tf_op jit(solution)/shard_map/ppermute | solution.py:46
  16.9 7.1 %copy-start.7 = (s32[1,2]{1,0:T(1,128)S(1)}, s32[1,2]{1,0:T(1,128)}, u32[]{:S(2)}) copy-start(s32[1,2]{1,0:T(1,128)} %param.7) | copy-start | bytes 28
  16.9 7.2 %copy-start.3 = (f32[512,128]{1,0:T(8,128)S(1)}, f32[512,128]{1,0:T(8,128)}, u32[]{:S(2)}) copy-start(f32[512,128]{1,0:T(8,128)} %get-tuple-element.27) | copy-start | bytes 786436
  16.9 7.2 %copy-start.4 = (f32[512,128]{1,0:T(8,128)S(1)}, f32[512,128]{1,0:T(8,128)}, u32[]{:S(2)}) copy-start(f32[512,128]{1,0:T(8,128)} %get-tuple-element.31) | copy-start | bytes 786436
  23.9 45.1 %copy-start = (bf16[2,512,1024]{2,1,0:T(8,128)(2,1)S(1)}, bf16[2,512,1024]{2,1,0:T(8,128)(2,1)}, u32[]{:S(2)}) copy-start(bf16[2,512,1024]{2,1,0:T(8,128)(2,1)} %get-tuple-element.40.own) | copy-start | bytes 6291460
  23.9 22.5 %collective-permute-start.3 = (bf16[2,512,768]{2,1,0:T(8,128)(2,1)}, bf16[2,512,768]{2,1,0:T(8,128)(2,1)}, u32[]{:S(2)}, u32[]{:S(2)}) collective-permute-start(bf16[2,512,768]{2,1,0:T(8,128)(2,1)} %get-tuple-element.36), channel_id=1, source_target_pairs={{0,4},{4,0},{8,12},{12,8},{16,20},{20,16},{24,28},{28,24},{32,36},... | collective-permute-start | bytes 4718600 | tf_op jit(solution)/shard_map/ppermute | solution.py:38
  36.0 1.4 %collective-permute-start.1 = (f32[514]{0:T(1024)S(1)}, f32[514]{0:T(1024)S(1)}, u32[]{:S(2)}, u32[]{:S(2)}) collective-permute-start(f32[514]{0:T(1024)S(1)} %get-tuple-element.66), channel_id=1, source_target_pairs={{0,4},{4,0},{8,12},{12,8},{16,20},{20,16},{24,28},{28,24},{32,36},... | collective-permute-start | bytes 6176 | tf_op jit(solution)/shard_map/ppermute | solution.py:38
  36.1 7.7 %collective-permute-start.2 = (f32[514]{0:T(1024)S(1)}, f32[514]{0:T(1024)S(1)}, u32[]{:S(2)}, u32[]{:S(2)}) collective-permute-start(f32[514]{0:T(1024)S(1)} %get-tuple-element.67), channel_id=1, source_target_pairs={{4,13},{5,14},{6,15},{7,12},{8,1},{9,2},{10,3},{11,0},{12,21},{13,... | collective-permute-start | bytes 6176 | tf_op jit(solution)/shard_map/ppermute | solution.py:50
  37.4 7.7 %collective-permute-start.4 = (f32[514]{0:T(1024)S(1)}, f32[514]{0:T(1024)S(1)}, u32[]{:S(2)}, u32[]{:S(2)}) collective-permute-start(f32[514]{0:T(1024)S(1)} %collective-permute-done.1), channel_id=1, source_target_pairs={{0,9},{1,10},{2,11},{3,8},{8,17},{9,18},{10,19},{11,16},{12,5},{13... | collective-permute-start | bytes 6176 | tf_op jit(solution)/shard_map/ppermute | solution.py:50
  43.8 40.4 %collective-permute-start.6 = (bf16[2,512,256]{2,1,0:T(8,128)(2,1)}, bf16[2,512,256]{2,1,0:T(8,128)(2,1)S(1)}, u32[]{:S(2)}, u32[]{:S(2)}) collective-permute-start(bf16[2,512,256]{2,1,0:T(8,128)(2,1)} %get-tuple-element.39), channel_id=1, source_target_pairs={{0,4},{4,0},{8,12},{12,8},{16,20},{20,16},{24,28},{28,24},{32,36},... | collective-permute-start | bytes 1572872 | tf_op jit(solution)/shard_map/ppermute | solution.py:38
  45.1 45.2 %collective-permute-start.10 = (bf16[2,512,768]{2,1,0:T(8,128)(2,1)}, bf16[2,512,768]{2,1,0:T(8,128)(2,1)}, u32[]{:S(2)}, u32[]{:S(2)}) collective-permute-start(bf16[2,512,768]{2,1,0:T(8,128)(2,1)} %get-tuple-element.46.own), channel_id=1, source_target_pairs={{4,12},{8,0},{12,20},{16,8},{20,28},{24,16},{28,36},{32,24},{36,44... | collective-permute-start | bytes 4718600 | tf_op jit(solution)/shard_map/ppermute | solution.py:46
  60.9 33.0 %collective-permute-start.11 = (bf16[2,512,768]{2,1,0:T(8,128)(2,1)}, bf16[2,512,768]{2,1,0:T(8,128)(2,1)}, u32[]{:S(2)}, u32[]{:S(2)}) collective-permute-start(bf16[2,512,768]{2,1,0:T(8,128)(2,1)} %collective-permute-done.3.sib), channel_id=1, source_target_pairs={{0,8},{8,16},{12,4},{16,24},{20,12},{24,32},{28,20},{32,40},{36,28... | collective-permute-start | bytes 4718600 | tf_op jit(solution)/shard_map/ppermute | solution.py:46
  69.0 15.2 %copy-start.2 = (bf16[2,512,256]{2,1,0:T(8,128)(2,1)S(1)}, bf16[2,512,256]{2,1,0:T(8,128)(2,1)}, u32[]{:S(2)}) copy-start(bf16[2,512,256]{2,1,0:T(8,128)(2,1)} %get-tuple-element.44.own) | copy-start | bytes 1572868
  69.0 24.9 %copy-start.1 = (bf16[2,512,768]{2,1,0:T(8,128)(2,1)S(1)}, bf16[2,512,768]{2,1,0:T(8,128)(2,1)}, u32[]{:S(2)}) copy-start(bf16[2,512,768]{2,1,0:T(8,128)(2,1)} %get-tuple-element.46.own) | copy-start | bytes 4718596
  84.3 21.3 %collective-permute-start.8 = (bf16[2,512,256]{2,1,0:T(8,128)(2,1)S(1)}, bf16[2,512,256]{2,1,0:T(8,128)(2,1)S(1)}, u32[]{:S(2)}, u32[]{:S(2)}) collective-permute-start(bf16[2,512,256]{2,1,0:T(8,128)(2,1)S(1)} %copy-done.2), channel_id=1, source_target_pairs={{4,12},{8,0},{12,20},{16,8},{20,28},{24,16},{28,36},{32,24},{36,44... | collective-permute-start | bytes 1572872 | tf_op jit(solution)/shard_map/ppermute | solution.py:46
  85.6 20.0 %collective-permute-start.9 = (bf16[2,512,256]{2,1,0:T(8,128)(2,1)S(1)}, bf16[2,512,256]{2,1,0:T(8,128)(2,1)S(1)}, u32[]{:S(2)}, u32[]{:S(2)}) collective-permute-start(bf16[2,512,256]{2,1,0:T(8,128)(2,1)S(1)} %collective-permute-done.6.sib), channel_id=1, source_target_pairs={{0,8},{8,16},{12,4},{16,24},{20,12},{24,32},{28,20},{32,40},{36,28... | collective-permute-start | bytes 1572872 | tf_op jit(solution)/shard_map/ppermute | solution.py:46

commit v4 on v3

--- a/solution.py
+++ b/solution.py
@@ -133,7 +133,9 @@
 def pairs_kernel(first, is_last, core, row_ref, own, sib, from_own, from_sib, *refs):
     levels, cos_ref, sin_ref, *refs = refs
     total_in = refs.pop(0) if first else None
-    out_ref, onehot, table, *refs = refs
+    out_ref, *refs = refs
+    give_ref = refs.pop(0) if is_last else None
+    onehot, table, *refs = refs
     total = refs.pop(0) if is_last else out_ref
     step = pl.program_id(0)
     count = own.shape[1] // len(refs)
@@ -187,10 +189,8 @@
             pairs = slice(part * 4 * count, (part + 1) * 4 * count)
             sums = jnp.dot(onehot[:, pairs], prods[...], preferred_element_type=jnp.float32)
             stack = sums if stack is None else stack + sums
-        high = stack.astype(jnp.bfloat16)
-        low = (stack - high.astype(jnp.float32)).astype(jnp.bfloat16)
-        lagged = jnp.dot(high, table[...], preferred_element_type=jnp.float32)
-        lagged += jnp.dot(low, table[...], preferred_element_type=jnp.float32)
+        stack = stack.astype(jnp.bfloat16)
+        lagged = jnp.dot(stack, table[...], preferred_element_type=jnp.float32)
 
         @pl.when(step == 0)
         def _():
@@ -210,8 +210,10 @@
         @pl.when(step == pl.num_programs(0) - 1)
         def _():
             for part in range(parts):
-                r, f = part // bands * rows, part % bands * lags
-                out_ref[part] = total[r : r + rows, f : f + lags].astype(jnp.bfloat16)
+                chip, f = part // bands, part % bands * lags
+                for ref, owner in ((out_ref, core[0]), (give_ref, 1 - core[0])):
+                    start = pl.multiple_of((2 * chip + owner) * rows, rows)
+                    ref[part] = total[pl.ds(start, rows), f : f + lags]
 
 
 def add_pairs(first, core, row, own, sib, from_own, from_sib, levels, phase, total, out, bins):
@@ -241,8 +243,8 @@
         functools.partial(pairs_kernel, first, is_last),
         grid=(cut // TILE,),
         in_specs=specs,
-        out_specs=whole(out),
-        out_shape=out,
+        out_specs=[whole(out)] * (1 + is_last),
+        out_shape=[out] * (1 + is_last),
         scratch_shapes=scratch
         + [pltpu.VMEM((pairs // PARTS, 2 * TILE), jnp.bfloat16)] * PARTS,
         compiler_params=params(40),
@@ -273,10 +275,9 @@
     sib_info = to_sibling(jnp.concatenate([totals[1], mask]))
     own_info_moved = to_chips(own_info, (-1, 1), 1)
     sib_info_moved = to_chips(sib_info, (1, -1), 1)
-    own[1], own_info_moved = after(own[1], own_info_moved)
-
-    first, sib_info = after(lax.axis_index("freq") * band, sib_info)
-    phase = phases(first, band // TILE)
+    phase = phases(lax.axis_index("freq") * band, band // TILE)
+
+    own[1], own_info_moved, phase = after(own[1], own_info_moved, phase)
 
 
     sib += [to_sibling(block) for block in rest]
@@ -312,12 +313,12 @@
     row = jnp.where(jnp.repeat(used, half), row, -1)
     row = row.reshape(4, PARTS, half // PARTS).transpose(1, 0, 2).reshape(-1)
 
-    out = jax.ShapeDtypeStruct((blocks * bands, bins // blocks, LAGS // bands), jnp.bfloat16)
+    out = jax.ShapeDtypeStruct((blocks // 2 * bands, bins // blocks, LAGS // bands), jnp.float32)
     total, start = None, 0
     for k, cut in enumerate(CUTS):
         arrays = own[k], sib[k], moved[2 * k], moved[2 * k + 1]
         goal = out if k == len(CUTS) - 1 else None
-        total = add_pairs(
+        total, *give = add_pairs(
             start // TILE, core_ref, row[None, :], *arrays, levels, phase, total, goal, bins
         )
         if k + 2 < len(CUTS):
@@ -325,7 +326,11 @@
             moved += [to_chips(own[k + 2], (-1, 1)), to_chips(sib[k + 2], (1, -1))]
         start += cut
 
-    parts = lax.all_to_all(total, ("chan", "freq"), 0, 0, tiled=True)
+    total = (total + to_sibling(*give)).astype(jnp.bfloat16)
+    ways = [[i * bands + f for i in range(c, blocks, 2) for f in range(bands)] for c in (0, 1)]
+    parts = lax.all_to_all(
+        total, ("chan", "freq"), 0, 0, axis_index_groups=ways, tiled=True
+    )
     return jnp.sum(parts.astype(jnp.float32), axis=0)
 
 

time: 143 us -> 138 us (0.965); the launches traced: 141 us -> 137 us
  waiting for transfers between devices: 22.5 us -> 28.6 us
  blocking collectives: 41.4 us -> 36.1 us
  Pallas kernels: 43.4 us -> 39 us
    all_to_all x1, blocking collectives: 30.9 us -> 25.6 us  [shards(): lax.all_to_all(total, ('chan', 'freq'), 0, 0, axis_index_groups=ways, til...]
    pallas_call x3, Pallas kernels: 30.4 us -> 26.1 us  [add_pairs(): pl.pallas_call(functools.partial(pairs_kernel, first, is_last), grid=(cut...]
    ppermute x6, waiting for transfers between devices: 18 us -> 21.7 us  [to_chips(): return lax.ppermute(block, 'chan', route)]
    ppermute x4 -> x5, waiting for transfers between devices: 3.03 us -> 5.68 us  [to_sibling(): lax.ppermute(block, 'chan', [(i, i ^ 1) for i in range(lax.axis_size('cha...]
  transfers between devices with their start and end apart: 12 -> 13, of which waited for: 4 -> 5; matrix products, arithmetic and copies ran while one was open for 4% -> 4% of each run, Pallas kernels for 24% -> 22%
where the time goes in v4:
time: 138 us; the launch traced here: 137 us
  Pallas kernels  39 us (28%)
  blocking collectives  36.1 us (26%)
  waiting for transfers between devices  28.6 us (21%)
  starting transfers between devices  25.2 us (18%)
  other arithmetic  4.46 us (3%)
  between operations  2.42 us (2%)
  local copies, waits for them, and re-layouts  1.48 us (1%)
    pallas_call x3, Pallas kernels, add_pairs(): pl.pallas_call(functools.partial(pairs_kernel, first, is_last), grid=(cut...  26.1 us
    all_to_all x1, blocking collectives, shards(): lax.all_to_all(total, ('chan', 'freq'), 0, 0, axis_index_groups=ways, til...  25.6 us
    ppermute x6, waiting for transfers between devices, to_chips(): return lax.ppermute(block, 'chan', route)  21.7 us
    ppermute x6, starting transfers between devices, to_chips(): return lax.ppermute(block, 'chan', route)  19.4 us
    pallas_call x2, Pallas kernels, planes(): pl.pallas_call(functools.partial(planes_kernel, start), grid_spec=spec, o...  12.9 us
    psum x1, blocking collectives, shards(): lax.psum(jnp.sum(jnp.stack([own_power, give_power]), axis=2), 'freq')  10.5 us
    ppermute x5, waiting for transfers between devices, to_sibling(): lax.ppermute(block, 'chan', [(i, i ^ 1) for i in range(lax.axis_size('cha...  5.68 us
    ppermute x2, starting transfers between devices, to_chips(): return lax.ppermute(block, ('chan', 'freq'), route)  5.52 us
  transfers between devices with their start and end apart: 13, of which 5 were waited for; matrix products, arithmetic and copies ran while one was open for 4% of the time, Pallas kernels for 22%

profile of v4, /device:TPU:0, one launch (start us, length us, event | category | flops | bytes accessed | tf_op | source)
XLA Modules:
  0.0 137.3 jit_solution(9867153729481267490)
XLA Ops:
  0.0 6.0 %planes.2 = (bf16[2,512,1024]{2,1,0:T(8,128)(2,1)}, f32[512,128]{1,0:T(8,128)}, bf16[2,512,1024]{2,1,0:T(8,128)(2,1)}, f32[512,128]{1,0:T(8,128)}) custom-call(s32[1]{0:T(128)} %bitcast.core_ref.core, bf16[1024,2,2048]{2,1,0:T(2,128)(2,1)} %refs_1_.2, bf16[1024,2,2048]{2,1,0:T(2,128)(2,1)} %refs_1_.2), custom_call_target="tpu_custom_call" | custom-call | flops 1 | bytes 1 | tf_op jit(solution)/shard_map/planes/pallas_call | solution.py:108
  6.0 1.3 collective-permute-start.7
  7.3 0.1 fusion.4
  7.4 3.0 %collective-permute-done.sib = bf16[2,512,1024]{2,1,0:T(8,128)(2,1)} collective-permute-done((bf16[2,512,1024]{2,1,0:T(8,128)(2,1)}, bf16[2,512,1024]{2,1,0:T(8,128)(2,1)}, u32[]{:S(2)}, u32[]{:S(2)}) %collective-permute-start) | collective-permute-done | bytes 2097184 | tf_op jit(solution)/shard_map/ppermute | solution.py:38
  10.5 5.3 %collective-permute-start.5 = (bf16[2,512,1024]{2,1,0:T(8,128)(2,1)}, bf16[2,512,1024]{2,1,0:T(8,128)(2,1)}, u32[]{:S(2)}, u32[]{:S(2)}) collective-permute-start(bf16[2,512,1024]{2,1,0:T(8,128)(2,1)} %collective-permute-done.sib), channel_id=1, source_target_pairs={{0,8},{8,16},{12,4},{16,24},{20,12},{24,32},{28,20},{32,40},{36,28... | collective-permute-start | bytes 6291464 | tf_op jit(solution)/shard_map/ppermute | solution.py:46
  15.7 0.1 fusion.5
  15.9 7.0 %planes.3 = (bf16[2,512,768]{2,1,0:T(8,128)(2,1)}, bf16[2,512,256]{2,1,0:T(8,128)(2,1)}, f32[512,128]{1,0:T(8,128)}, bf16[2,512,768]{2,1,0:T(8,128)(2,1)}, bf16[...) custom-call(s32[1]{0:T(128)} %bitcast.core_ref.core, bf16[1024,2,2048]{2,1,0:T(2,128)(2,1)} %refs_1_.2, ...), custom_call_target="tpu_custom_call" | custom-call | flops 1 | bytes 1 | tf_op jit(solution)/shard_map/planes/pallas_call | solution.py:108
  22.9 0.1 collective-permute-start.3
  23.1 0.7 negate_multiply_fusion
  23.8 1.1 add_bitcast_fusion
  24.9 0.2 maximum_reduce_fusion
  25.1 10.5 %psum.7 = f32[2,512]{1,0:T(2,128)S(1)} all-reduce(f32[2,512]{1,0:T(2,128)S(1)} %maximum_reduce_fusion), channel_id=1, replica_groups=mesh['chan'=32,'freq'=4] {'freq'}, use_global_device_ids=true, to_apply=%region_1.2 | all-reduce | flops 1024 | bytes 8192 | tf_op jit(solution)/shard_map/psum | solution.py:272
  35.8 1.3 collective-permute-start.2
  37.1 4.2 %collective-permute-start.4 = (f32[514]{0:T(1024)S(1)}, f32[514]{0:T(1024)S(1)}, u32[]{:S(2)}, u32[]{:S(2)}) collective-permute-start(f32[514]{0:T(1024)S(1)} %collective-permute-done.1), channel_id=1, source_target_pairs={{0,9},{1,10},{2,11},{3,8},{8,17},{9,18},{10,19},{11,16},{12,5},{13... | collective-permute-start | bytes 6176 | tf_op jit(solution)/shard_map/ppermute | solution.py:50
  41.3 1.0 select_reduce_fusion
  42.3 1.2 collective-permute-done.2
  43.5 1.3 collective-permute-start.10
  44.8 16.1 %collective-permute-done.5.from_sib = bf16[2,512,1024]{2,1,0:T(8,128)(2,1)} collective-permute-done((bf16[2,512,1024]{2,1,0:T(8,128)(2,1)}, bf16[2,512,1024]{2,1,0:T(8,128)(2,1)}, u32[]{:S(2)}, u32[]{:S(2)}) %collective-permute-start.5) | collective-permute-done | bytes 2097184 | tf_op jit(solution)/shard_map/ppermute | solution.py:46
  60.9 5.5 %collective-permute-start.11 = (bf16[2,512,768]{2,1,0:T(8,128)(2,1)}, bf16[2,512,768]{2,1,0:T(8,128)(2,1)}, u32[]{:S(2)}, u32[]{:S(2)}) collective-permute-start(bf16[2,512,768]{2,1,0:T(8,128)(2,1)} %collective-permute-done.3.sib), channel_id=1, source_target_pairs={{0,8},{8,16},{12,4},{16,24},{20,12},{24,32},{28,20},{32,40},{36,28... | collective-permute-start | bytes 4718600 | tf_op jit(solution)/shard_map/ppermute | solution.py:46
  66.4 0.7 fusion.6
  68.4 0.6 slice.34
  69.8 0.1 copy.16
  70.1 13.0 %add_pairs.3.refs_3_ = f32[512,1024]{1,0:T(8,128)S(1)} custom-call(s32[1]{0:T(128)} %bitcast.core_ref.core, s32[1,2048]{1,0:T(1,128)S(1)} %bitcast.32, bf16[2,512,1024]{2,1,0:T(8,128)(2,1)S(1)} %copy-done, bf16[2,512,1024]{2,1,0:T(8,128)(2,1)} %collective-permute-done.sib, bf16[2,512,1024]{2,1,0:T(8,128)(2,1)} %collective-permute-done.7.from_own, ...), custom_call_target="tpu_custom_call" | custom-call | flops 1 | bytes 1 | tf_op jit(solution)/shard_map/add_pairs/pallas_call | solution.py:242
  83.1 1.3 collective-permute-start.8
  84.4 4.8 %collective-permute-start.9 = (bf16[2,512,256]{2,1,0:T(8,128)(2,1)S(1)}, bf16[2,512,256]{2,1,0:T(8,128)(2,1)S(1)}, u32[]{:S(2)}, u32[]{:S(2)}) collective-permute-start(bf16[2,512,256]{2,1,0:T(8,128)(2,1)S(1)} %collective-permute-done.6.sib), channel_id=1, source_target_pairs={{0,8},{8,16},{12,4},{16,24},{20,12},{24,32},{28,20},{32,40},{36,28... | collective-permute-start | bytes 1572872 | tf_op jit(solution)/shard_map/ppermute | solution.py:46
  89.2 5.7 %collective-permute-done.11.from_sib = bf16[2,512,768]{2,1,0:T(8,128)(2,1)} collective-permute-done((bf16[2,512,768]{2,1,0:T(8,128)(2,1)}, bf16[2,512,768]{2,1,0:T(8,128)(2,1)}, u32[]{:S(2)}, u32[]{:S(2)}) %collective-permute-start.11) | collective-permute-done | bytes 1572896 | tf_op jit(solution)/shard_map/ppermute | solution.py:46
  94.9 10.0 %add_pairs.4.refs_3_ = f32[512,1024]{1,0:T(8,128)S(1)} custom-call(s32[1]{0:T(128)} %bitcast.core_ref.core, s32[1,2048]{1,0:T(1,128)S(1)} %bitcast.33, bf16[2,512,768]{2,1,0:T(8,128)(2,1)S(1)} %copy-done.1, bf16[2,512,768]{2,1,0:T(8,128)(2,1)} %collective-permute-done.3.sib, bf16[2,512,768]{2,1,0:T(8,128)(2,1)} %collective-permute-done.10.from_own, ...), custom_call_target="tpu_custom_call" | custom-call | flops 1 | bytes 1 | tf_op jit(solution)/shard_map/add_pairs/pallas_call | solution.py:242
  104.9 3.1 %add_pairs.5 = (f32[64,16,256]{2,1,0:T(8,128)S(1)}, f32[64,16,256]{2,1,0:T(8,128)S(1)}) custom-call(s32[1]{0:T(128)} %bitcast.core_ref.core, s32[1,2048]{1,0:T(1,128)S(1)} %bitcast.34, bf16[2,512,256]{2,1,0:T(8,128)(2,1)S(1)} %copy-done.2, bf16[2,512,256]{2,1,0:T(8,128)(2,1)S(1)} %collective-permute-done.6.sib, ...), custom_call_target="tpu_custom_call" | custom-call | flops 1 | bytes 1 | tf_op jit(solution)/shard_map/add_pairs/pallas_call | solution.py:242
  108.1 2.6 %collective-permute-done.12 = f32[64,16,256]{2,1,0:T(8,128)S(1)} collective-permute-done((f32[64,16,256]{2,1,0:T(8,128)S(1)}, f32[64,16,256]{2,1,0:T(8,128)S(1)}, u32[]{:S(2)}, u32[]{:S(2)}) %collective-permute-start.12) | collective-permute-done | bytes 1048608 | tf_op jit(solution)/shard_map/ppermute | solution.py:38
  110.7 0.3 add_convert_fusion
  111.0 25.6 %all_to_all.5 = bf16[64,16,256]{2,1,0:T(8,128)(2,1)S(1)} all-to-all(bf16[64,16,256]{2,1,0:T(8,128)(2,1)S(1)} %add_convert_fusion), channel_id=1, replica_groups={{0,1,2,3,8,9,10,11,16,17,18,19,24,25,26,27,32,33,34,35,40,41,42,43,48,4..., dimensions={0} | all-to-all | bytes 1048576 | tf_op jit(solution)/shard_map/all_to_all | solution.py:331
  136.6 0.7 convert_reduce_fusion
  (49 shorter events, 0.6 us)
Async XLA Ops:
  0.0 7.3 %copy-start.5 = (s32[32768]{0:T(1024)S(1)}, s32[32768]{0:T(1024)}, u32[]{:S(2)}) copy-start(s32[32768]{0:T(1024)} %param.5) | copy-start | bytes 393220
  6.0 4.5 %collective-permute-start = (bf16[2,512,1024]{2,1,0:T(8,128)(2,1)}, bf16[2,512,1024]{2,1,0:T(8,128)(2,1)}, u32[]{:S(2)}, u32[]{:S(2)}) collective-permute-start(bf16[2,512,1024]{2,1,0:T(8,128)(2,1)} %get-tuple-element.30), channel_id=1, source_target_pairs={{0,4},{4,0},{8,12},{12,8},{16,20},{20,16},{24,28},{28,24},{32,36},... | collective-permute-start | bytes 6291464 | tf_op jit(solution)/shard_map/ppermute | solution.py:38
  6.0 64.1 %collective-permute-start.7 = (bf16[2,512,1024]{2,1,0:T(8,128)(2,1)}, bf16[2,512,1024]{2,1,0:T(8,128)(2,1)}, u32[]{:S(2)}, u32[]{:S(2)}) collective-permute-start(bf16[2,512,1024]{2,1,0:T(8,128)(2,1)} %get-tuple-element.41.own), channel_id=1, source_target_pairs={{4,12},{8,0},{12,20},{16,8},{20,28},{24,16},{28,36},{32,24},{36,44... | collective-permute-start | bytes 6291464 | tf_op jit(solution)/shard_map/ppermute | solution.py:46
  10.5 50.4 %collective-permute-start.5 = (bf16[2,512,1024]{2,1,0:T(8,128)(2,1)}, bf16[2,512,1024]{2,1,0:T(8,128)(2,1)}, u32[]{:S(2)}, u32[]{:S(2)}) collective-permute-start(bf16[2,512,1024]{2,1,0:T(8,128)(2,1)} %collective-permute-done.sib), channel_id=1, source_target_pairs={{0,8},{8,16},{12,4},{16,24},{20,12},{24,32},{28,20},{32,40},{36,28... | collective-permute-start | bytes 6291464 | tf_op jit(solution)/shard_map/ppermute | solution.py:46
  15.9 7.2 %copy-start.7 = (s32[1,2]{1,0:T(1,128)S(1)}, s32[1,2]{1,0:T(1,128)}, u32[]{:S(2)}) copy-start(s32[1,2]{1,0:T(1,128)} %param.7) | copy-start | bytes 28
  15.9 7.9 %copy-start.3 = (f32[512,128]{1,0:T(8,128)S(1)}, f32[512,128]{1,0:T(8,128)}, u32[]{:S(2)}) copy-start(f32[512,128]{1,0:T(8,128)} %get-tuple-element.29) | copy-start | bytes 786436
  15.9 7.9 %copy-start.4 = (f32[512,128]{1,0:T(8,128)S(1)}, f32[512,128]{1,0:T(8,128)}, u32[]{:S(2)}) copy-start(f32[512,128]{1,0:T(8,128)} %get-tuple-element.33) | copy-start | bytes 786436
  22.9 18.4 %copy-start.6 = (s32[512]{0:T(512)S(1)}, s32[512]{0:T(512)}, u32[]{:S(2)}) copy-start(s32[512]{0:T(512)} %param.6) | copy-start | bytes 6148
  22.9 47.2 %copy-start = (bf16[2,512,1024]{2,1,0:T(8,128)(2,1)S(1)}, bf16[2,512,1024]{2,1,0:T(8,128)(2,1)}, u32[]{:S(2)}) copy-start(bf16[2,512,1024]{2,1,0:T(8,128)(2,1)} %get-tuple-element.41.own) | copy-start | bytes 6291460
  22.9 21.9 %collective-permute-start.3 = (bf16[2,512,768]{2,1,0:T(8,128)(2,1)}, bf16[2,512,768]{2,1,0:T(8,128)(2,1)}, u32[]{:S(2)}, u32[]{:S(2)}) collective-permute-start(bf16[2,512,768]{2,1,0:T(8,128)(2,1)} %get-tuple-element.37), channel_id=1, source_target_pairs={{0,4},{4,0},{8,12},{12,8},{16,20},{20,16},{24,28},{28,24},{32,36},... | collective-permute-start | bytes 4718600 | tf_op jit(solution)/shard_map/ppermute | solution.py:38
  35.7 1.4 %collective-permute-start.1 = (f32[514]{0:T(1024)S(1)}, f32[514]{0:T(1024)S(1)}, u32[]{:S(2)}, u32[]{:S(2)}) collective-permute-start(f32[514]{0:T(1024)S(1)} %get-tuple-element.70), channel_id=1, source_target_pairs={{0,4},{4,0},{8,12},{12,8},{16,20},{20,16},{24,28},{28,24},{32,36},... | collective-permute-start | bytes 6176 | tf_op jit(solution)/shard_map/ppermute | solution.py:38
  35.8 7.7 %collective-permute-start.2 = (f32[514]{0:T(1024)S(1)}, f32[514]{0:T(1024)S(1)}, u32[]{:S(2)}, u32[]{:S(2)}) collective-permute-start(f32[514]{0:T(1024)S(1)} %get-tuple-element.71), channel_id=1, source_target_pairs={{4,13},{5,14},{6,15},{7,12},{8,1},{9,2},{10,3},{11,0},{12,21},{13,... | collective-permute-start | bytes 6176 | tf_op jit(solution)/shard_map/ppermute | solution.py:50
  37.1 6.4 %collective-permute-start.4 = (f32[514]{0:T(1024)S(1)}, f32[514]{0:T(1024)S(1)}, u32[]{:S(2)}, u32[]{:S(2)}) collective-permute-start(f32[514]{0:T(1024)S(1)} %collective-permute-done.1), channel_id=1, source_target_pairs={{0,9},{1,10},{2,11},{3,8},{8,17},{9,18},{10,19},{11,16},{12,5},{13... | collective-permute-start | bytes 6176 | tf_op jit(solution)/shard_map/ppermute | solution.py:50
  43.5 39.6 %collective-permute-start.6 = (bf16[2,512,256]{2,1,0:T(8,128)(2,1)}, bf16[2,512,256]{2,1,0:T(8,128)(2,1)S(1)}, u32[]{:S(2)}, u32[]{:S(2)}) collective-permute-start(bf16[2,512,256]{2,1,0:T(8,128)(2,1)} %get-tuple-element.40), channel_id=1, source_target_pairs={{0,4},{4,0},{8,12},{12,8},{16,20},{20,16},{24,28},{28,24},{32,36},... | collective-permute-start | bytes 1572872 | tf_op jit(solution)/shard_map/ppermute | solution.py:38
  43.5 45.7 %collective-permute-start.10 = (bf16[2,512,768]{2,1,0:T(8,128)(2,1)}, bf16[2,512,768]{2,1,0:T(8,128)(2,1)}, u32[]{:S(2)}, u32[]{:S(2)}) collective-permute-start(bf16[2,512,768]{2,1,0:T(8,128)(2,1)} %get-tuple-element.48.own), channel_id=1, source_target_pairs={{4,12},{8,0},{12,20},{16,8},{20,28},{24,16},{28,36},{32,24},{36,44... | collective-permute-start | bytes 4718600 | tf_op jit(solution)/shard_map/ppermute | solution.py:46
  60.9 34.0 %collective-permute-start.11 = (bf16[2,512,768]{2,1,0:T(8,128)(2,1)}, bf16[2,512,768]{2,1,0:T(8,128)(2,1)}, u32[]{:S(2)}, u32[]{:S(2)}) collective-permute-start(bf16[2,512,768]{2,1,0:T(8,128)(2,1)} %collective-permute-done.3.sib), channel_id=1, source_target_pairs={{0,8},{8,16},{12,4},{16,24},{20,12},{24,32},{28,20},{32,40},{36,28... | collective-permute-start | bytes 4718600 | tf_op jit(solution)/shard_map/ppermute | solution.py:46
  70.1 13.1 %copy-start.2 = (bf16[2,512,256]{2,1,0:T(8,128)(2,1)S(1)}, bf16[2,512,256]{2,1,0:T(8,128)(2,1)}, u32[]{:S(2)}) copy-start(bf16[2,512,256]{2,1,0:T(8,128)(2,1)} %get-tuple-element.46.own) | copy-start | bytes 1572868
  70.1 24.8 %copy-start.1 = (bf16[2,512,768]{2,1,0:T(8,128)(2,1)S(1)}, bf16[2,512,768]{2,1,0:T(8,128)(2,1)}, u32[]{:S(2)}) copy-start(bf16[2,512,768]{2,1,0:T(8,128)(2,1)} %get-tuple-element.48.own) | copy-start | bytes 4718596
  83.1 21.8 %collective-permute-start.8 = (bf16[2,512,256]{2,1,0:T(8,128)(2,1)S(1)}, bf16[2,512,256]{2,1,0:T(8,128)(2,1)S(1)}, u32[]{:S(2)}, u32[]{:S(2)}) collective-permute-start(bf16[2,512,256]{2,1,0:T(8,128)(2,1)S(1)} %copy-done.2), channel_id=1, source_target_pairs={{4,12},{8,0},{12,20},{16,8},{20,28},{24,16},{28,36},{32,24},{36,44... | collective-permute-start | bytes 1572872 | tf_op jit(solution)/shard_map/ppermute | solution.py:46
  84.4 20.5 %collective-permute-start.9 = (bf16[2,512,256]{2,1,0:T(8,128)(2,1)S(1)}, bf16[2,512,256]{2,1,0:T(8,128)(2,1)S(1)}, u32[]{:S(2)}, u32[]{:S(2)}) collective-permute-start(bf16[2,512,256]{2,1,0:T(8,128)(2,1)S(1)} %collective-permute-done.6.sib), channel_id=1, source_target_pairs={{0,8},{8,16},{12,4},{16,24},{20,12},{24,32},{28,20},{32,40},{36,28... | collective-permute-start | bytes 1572872 | tf_op jit(solution)/shard_map/ppermute | solution.py:46
  108.0 2.7 %collective-permute-start.12 = (f32[64,16,256]{2,1,0:T(8,128)S(1)}, f32[64,16,256]{2,1,0:T(8,128)S(1)}, u32[]{:S(2)}, u32[]{:S(2)}) collective-permute-start(f32[64,16,256]{2,1,0:T(8,128)S(1)} %get-tuple-element.52), channel_id=1, source_target_pairs={{0,4},{4,0},{8,12},{12,8},{16,20},{20,16},{24,28},{28,24},{32,36},... | collective-permute-start | bytes 3145736 | tf_op jit(solution)/shard_map/ppermute | solution.py:38

commit v5 on v4

--- a/solution.py
+++ b/solution.py
@@ -89,8 +89,9 @@
 def planes(records, core, start, cuts):
     half = records.shape[0] // 2
     width = sum(cuts)
-    loaded = width if start == 0 else records.shape[2]
-    block = 128
+    aligned = start % width == 0
+    loaded, column = (width, start // width) if aligned else (records.shape[2], 0)
+    block = 256
     steps = half // block
     outs = [pl.BlockSpec((2, block, cut), lambda t, c: (0, t, 0)) for cut in cuts]
     outs += [pl.BlockSpec((block, LANES), lambda t, c: (t, 0))]
@@ -100,13 +101,13 @@
         num_scalar_prefetch=1,
         grid=(steps,),
         in_specs=[
-            pl.BlockSpec((block, 2, loaded), lambda t, c: (c[0] * steps + t, 0, 0)),
-            pl.BlockSpec((block, 2, loaded), lambda t, c: ((1 - c[0]) * steps + t, 0, 0)),
+            pl.BlockSpec((block, 2, loaded), lambda t, c: (c[0] * steps + t, 0, column)),
+            pl.BlockSpec((block, 2, loaded), lambda t, c: ((1 - c[0]) * steps + t, 0, column)),
         ],
         out_specs=outs * 2,
     )
     results = pl.pallas_call(
-        functools.partial(planes_kernel, start),
+        functools.partial(planes_kernel, 0 if aligned else start),
         grid_spec=spec,
         out_shape=shapes * 2,
         compiler_params=params(),

time: 138 us -> 137 us (level)
  Pallas kernels: 39 us -> 37 us
    pallas_call x2, Pallas kernels: 12.9 us -> 10.9 us  [planes(): pl.pallas_call(functools.partial(planes_kernel, 0 if aligned else start),...]
  transfers between devices with their start and end apart: 13 -> 13, of which waited for: 5 -> 5; matrix products, arithmetic and copies ran while one was open for 4% -> 4% of each run, Pallas kernels for 22% -> 21%
where the time goes in v5:
time: 137 us
  Pallas kernels  37 us (27%)
  blocking collectives  36.3 us (26%)
  waiting for transfers between devices  29.8 us (22%)
  starting transfers between devices  25.3 us (18%)
  other arithmetic  4.46 us (3%)
  between operations  2.42 us (2%)
  local copies, waits for them, and re-layouts  1.48 us (1%)
    pallas_call x3, Pallas kernels, add_pairs(): pl.pallas_call(functools.partial(pairs_kernel, first, is_last), grid=(cut...  26.1 us
    all_to_all x1, blocking collectives, shards(): lax.all_to_all(total, ('chan', 'freq'), 0, 0, axis_index_groups=ways, til...  25.8 us
    ppermute x6, waiting for transfers between devices, to_chips(): return lax.ppermute(block, 'chan', route)  23 us
    ppermute x6, starting transfers between devices, to_chips(): return lax.ppermute(block, 'chan', route)  19.5 us
    pallas_call x2, Pallas kernels, planes(): pl.pallas_call(functools.partial(planes_kernel, 0 if aligned else start),...  10.9 us
    psum x1, blocking collectives, shards(): lax.psum(jnp.sum(jnp.stack([own_power, give_power]), axis=2), 'freq')  10.5 us
    ppermute x5, waiting for transfers between devices, to_sibling(): lax.ppermute(block, 'chan', [(i, i ^ 1) for i in range(lax.axis_size('cha...  5.68 us
    ppermute x2, starting transfers between devices, to_chips(): return lax.ppermute(block, ('chan', 'freq'), route)  5.52 us
  transfers between devices with their start and end apart: 13, of which 5 were waited for; matrix products, arithmetic and copies ran while one was open for 4% of the time, Pallas kernels for 21%

profile of v5, /device:TPU:0, one launch (start us, length us, event | category | flops | bytes accessed | tf_op | source)
XLA Modules:
  0.0 136.8 jit_solution(14843253531578154248)
XLA Ops:
  0.0 5.4 %planes.2 = (bf16[2,512,1024]{2,1,0:T(8,128)(2,1)}, f32[512,128]{1,0:T(8,128)}, bf16[2,512,1024]{2,1,0:T(8,128)(2,1)}, f32[512,128]{1,0:T(8,128)}) custom-call(s32[1]{0:T(128)} %bitcast.core_ref.core, bf16[1024,2,2048]{2,1,0:T(2,128)(2,1)} %refs_1_.2, bf16[1024,2,2048]{2,1,0:T(2,128)(2,1)} %refs_1_.2), custom_call_target="tpu_custom_call" | custom-call | flops 1 | bytes 1 | tf_op jit(solution)/shard_map/planes/pallas_call | solution.py:109
  5.4 1.3 collective-permute-start.7
  6.8 0.1 fusion.4
  6.9 3.0 %collective-permute-done.sib = bf16[2,512,1024]{2,1,0:T(8,128)(2,1)} collective-permute-done((bf16[2,512,1024]{2,1,0:T(8,128)(2,1)}, bf16[2,512,1024]{2,1,0:T(8,128)(2,1)}, u32[]{:S(2)}, u32[]{:S(2)}) %collective-permute-start) | collective-permute-done | bytes 2097184 | tf_op jit(solution)/shard_map/ppermute | solution.py:38
  9.9 5.3 %collective-permute-start.5 = (bf16[2,512,1024]{2,1,0:T(8,128)(2,1)}, bf16[2,512,1024]{2,1,0:T(8,128)(2,1)}, u32[]{:S(2)}, u32[]{:S(2)}) collective-permute-start(bf16[2,512,1024]{2,1,0:T(8,128)(2,1)} %collective-permute-done.sib), channel_id=1, source_target_pairs={{0,8},{8,16},{12,4},{16,24},{20,12},{24,32},{28,20},{32,40},{36,28... | collective-permute-start | bytes 6291464 | tf_op jit(solution)/shard_map/ppermute | solution.py:46
  15.2 0.1 fusion.5
  15.4 5.5 %planes.3 = (bf16[2,512,768]{2,1,0:T(8,128)(2,1)}, bf16[2,512,256]{2,1,0:T(8,128)(2,1)}, f32[512,128]{1,0:T(8,128)}, bf16[2,512,768]{2,1,0:T(8,128)(2,1)}, bf16[...) custom-call(s32[1]{0:T(128)} %bitcast.core_ref.core, bf16[1024,2,2048]{2,1,0:T(2,128)(2,1)} %refs_1_.2, ...), custom_call_target="tpu_custom_call" | custom-call | flops 1 | bytes 1 | tf_op jit(solution)/shard_map/planes/pallas_call | solution.py:109
  20.9 0.1 collective-permute-start.3
  21.1 0.7 negate_multiply_fusion
  21.8 1.1 add_bitcast_fusion
  22.9 0.2 maximum_reduce_fusion
  23.1 10.5 %psum.7 = f32[2,512]{1,0:T(2,128)S(1)} all-reduce(f32[2,512]{1,0:T(2,128)S(1)} %maximum_reduce_fusion), channel_id=1, replica_groups=mesh['chan'=32,'freq'=4] {'freq'}, use_global_device_ids=true, to_apply=%region_1.2 | all-reduce | flops 1024 | bytes 8192 | tf_op jit(solution)/shard_map/psum | solution.py:273
  33.8 1.3 collective-permute-start.2
  35.1 4.2 %collective-permute-start.4 = (f32[514]{0:T(1024)S(1)}, f32[514]{0:T(1024)S(1)}, u32[]{:S(2)}, u32[]{:S(2)}) collective-permute-start(f32[514]{0:T(1024)S(1)} %collective-permute-done.1), channel_id=1, source_target_pairs={{0,9},{1,10},{2,11},{3,8},{8,17},{9,18},{10,19},{11,16},{12,5},{13... | collective-permute-start | bytes 6176 | tf_op jit(solution)/shard_map/ppermute | solution.py:50
  39.3 1.0 select_reduce_fusion
  40.3 1.2 collective-permute-done.2
  41.5 1.3 collective-permute-start.10
  42.8 17.5 %collective-permute-done.5.from_sib = bf16[2,512,1024]{2,1,0:T(8,128)(2,1)} collective-permute-done((bf16[2,512,1024]{2,1,0:T(8,128)(2,1)}, bf16[2,512,1024]{2,1,0:T(8,128)(2,1)}, u32[]{:S(2)}, u32[]{:S(2)}) %collective-permute-start.5) | collective-permute-done | bytes 2097184 | tf_op jit(solution)/shard_map/ppermute | solution.py:46
  60.3 5.5 %collective-permute-start.11 = (bf16[2,512,768]{2,1,0:T(8,128)(2,1)}, bf16[2,512,768]{2,1,0:T(8,128)(2,1)}, u32[]{:S(2)}, u32[]{:S(2)}) collective-permute-start(bf16[2,512,768]{2,1,0:T(8,128)(2,1)} %collective-permute-done.3.sib), channel_id=1, source_target_pairs={{0,8},{8,16},{12,4},{16,24},{20,12},{24,32},{28,20},{32,40},{36,28... | collective-permute-start | bytes 4718600 | tf_op jit(solution)/shard_map/ppermute | solution.py:46
  65.8 0.7 fusion.6
  67.9 0.6 slice.34
  69.3 0.1 copy.16
  69.5 13.0 %add_pairs.3.refs_3_ = f32[512,1024]{1,0:T(8,128)S(1)} custom-call(s32[1]{0:T(128)} %bitcast.core_ref.core, s32[1,2048]{1,0:T(1,128)S(1)} %bitcast.32, bf16[2,512,1024]{2,1,0:T(8,128)(2,1)S(1)} %copy-done, bf16[2,512,1024]{2,1,0:T(8,128)(2,1)} %collective-permute-done.sib, bf16[2,512,1024]{2,1,0:T(8,128)(2,1)} %collective-permute-done.7.from_own, ...), custom_call_target="tpu_custom_call" | custom-call | flops 1 | bytes 1 | tf_op jit(solution)/shard_map/add_pairs/pallas_call | solution.py:243
  82.6 1.3 collective-permute-start.8
  83.9 4.8 %collective-permute-start.9 = (bf16[2,512,256]{2,1,0:T(8,128)(2,1)S(1)}, bf16[2,512,256]{2,1,0:T(8,128)(2,1)S(1)}, u32[]{:S(2)}, u32[]{:S(2)}) collective-permute-start(bf16[2,512,256]{2,1,0:T(8,128)(2,1)S(1)} %collective-permute-done.6.sib), channel_id=1, source_target_pairs={{0,8},{8,16},{12,4},{16,24},{20,12},{24,32},{28,20},{32,40},{36,28... | collective-permute-start | bytes 1572872 | tf_op jit(solution)/shard_map/ppermute | solution.py:46
  88.7 5.5 %collective-permute-done.11.from_sib = bf16[2,512,768]{2,1,0:T(8,128)(2,1)} collective-permute-done((bf16[2,512,768]{2,1,0:T(8,128)(2,1)}, bf16[2,512,768]{2,1,0:T(8,128)(2,1)}, u32[]{:S(2)}, u32[]{:S(2)}) %collective-permute-start.11) | collective-permute-done | bytes 1572896 | tf_op jit(solution)/shard_map/ppermute | solution.py:46
  94.2 10.0 %add_pairs.4.refs_3_ = f32[512,1024]{1,0:T(8,128)S(1)} custom-call(s32[1]{0:T(128)} %bitcast.core_ref.core, s32[1,2048]{1,0:T(1,128)S(1)} %bitcast.33, bf16[2,512,768]{2,1,0:T(8,128)(2,1)S(1)} %copy-done.1, bf16[2,512,768]{2,1,0:T(8,128)(2,1)} %collective-permute-done.3.sib, bf16[2,512,768]{2,1,0:T(8,128)(2,1)} %collective-permute-done.10.from_own, ...), custom_call_target="tpu_custom_call" | custom-call | flops 1 | bytes 1 | tf_op jit(solution)/shard_map/add_pairs/pallas_call | solution.py:243
  104.2 3.1 %add_pairs.5 = (f32[64,16,256]{2,1,0:T(8,128)S(1)}, f32[64,16,256]{2,1,0:T(8,128)S(1)}) custom-call(s32[1]{0:T(128)} %bitcast.core_ref.core, s32[1,2048]{1,0:T(1,128)S(1)} %bitcast.34, bf16[2,512,256]{2,1,0:T(8,128)(2,1)S(1)} %copy-done.2, bf16[2,512,256]{2,1,0:T(8,128)(2,1)S(1)} %collective-permute-done.6.sib, ...), custom_call_target="tpu_custom_call" | custom-call | flops 1 | bytes 1 | tf_op jit(solution)/shard_map/add_pairs/pallas_call | solution.py:243
  107.4 2.6 %collective-permute-done.12 = f32[64,16,256]{2,1,0:T(8,128)S(1)} collective-permute-done((f32[64,16,256]{2,1,0:T(8,128)S(1)}, f32[64,16,256]{2,1,0:T(8,128)S(1)}, u32[]{:S(2)}, u32[]{:S(2)}) %collective-permute-start.12) | collective-permute-done | bytes 1048608 | tf_op jit(solution)/shard_map/ppermute | solution.py:38
  110.0 0.3 add_convert_fusion
  110.3 25.8 %all_to_all.5 = bf16[64,16,256]{2,1,0:T(8,128)(2,1)S(1)} all-to-all(bf16[64,16,256]{2,1,0:T(8,128)(2,1)S(1)} %add_convert_fusion), channel_id=1, replica_groups={{0,1,2,3,8,9,10,11,16,17,18,19,24,25,26,27,32,33,34,35,40,41,42,43,48,4..., dimensions={0} | all-to-all | bytes 1048576 | tf_op jit(solution)/shard_map/all_to_all | solution.py:332
  136.1 0.7 convert_reduce_fusion
  (49 shorter events, 0.6 us)
Async XLA Ops:
  0.0 6.8 %copy-start.5 = (s32[32768]{0:T(1024)S(1)}, s32[32768]{0:T(1024)}, u32[]{:S(2)}) copy-start(s32[32768]{0:T(1024)} %param.5) | copy-start | bytes 393220
  5.4 4.5 %collective-permute-start = (bf16[2,512,1024]{2,1,0:T(8,128)(2,1)}, bf16[2,512,1024]{2,1,0:T(8,128)(2,1)}, u32[]{:S(2)}, u32[]{:S(2)}) collective-permute-start(bf16[2,512,1024]{2,1,0:T(8,128)(2,1)} %get-tuple-element.30), channel_id=1, source_target_pairs={{0,4},{4,0},{8,12},{12,8},{16,20},{20,16},{24,28},{28,24},{32,36},... | collective-permute-start | bytes 6291464 | tf_op jit(solution)/shard_map/ppermute | solution.py:38
  5.4 64.1 %collective-permute-start.7 = (bf16[2,512,1024]{2,1,0:T(8,128)(2,1)}, bf16[2,512,1024]{2,1,0:T(8,128)(2,1)}, u32[]{:S(2)}, u32[]{:S(2)}) collective-permute-start(bf16[2,512,1024]{2,1,0:T(8,128)(2,1)} %get-tuple-element.41.own), channel_id=1, source_target_pairs={{4,12},{8,0},{12,20},{16,8},{20,28},{24,16},{28,36},{32,24},{36,44... | collective-permute-start | bytes 6291464 | tf_op jit(solution)/shard_map/ppermute | solution.py:46
  9.9 50.4 %collective-permute-start.5 = (bf16[2,512,1024]{2,1,0:T(8,128)(2,1)}, bf16[2,512,1024]{2,1,0:T(8,128)(2,1)}, u32[]{:S(2)}, u32[]{:S(2)}) collective-permute-start(bf16[2,512,1024]{2,1,0:T(8,128)(2,1)} %collective-permute-done.sib), channel_id=1, source_target_pairs={{0,8},{8,16},{12,4},{16,24},{20,12},{24,32},{28,20},{32,40},{36,28... | collective-permute-start | bytes 6291464 | tf_op jit(solution)/shard_map/ppermute | solution.py:46
  15.3 5.7 %copy-start.7 = (s32[1,2]{1,0:T(1,128)S(1)}, s32[1,2]{1,0:T(1,128)}, u32[]{:S(2)}) copy-start(s32[1,2]{1,0:T(1,128)} %param.7) | copy-start | bytes 28
  15.4 6.5 %copy-start.3 = (f32[512,128]{1,0:T(8,128)S(1)}, f32[512,128]{1,0:T(8,128)}, u32[]{:S(2)}) copy-start(f32[512,128]{1,0:T(8,128)} %get-tuple-element.29) | copy-start | bytes 786436
  15.4 6.5 %copy-start.4 = (f32[512,128]{1,0:T(8,128)S(1)}, f32[512,128]{1,0:T(8,128)}, u32[]{:S(2)}) copy-start(f32[512,128]{1,0:T(8,128)} %get-tuple-element.33) | copy-start | bytes 786436
  20.9 18.4 %copy-start.6 = (s32[512]{0:T(512)S(1)}, s32[512]{0:T(512)}, u32[]{:S(2)}) copy-start(s32[512]{0:T(512)} %param.6) | copy-start | bytes 6148
  20.9 48.6 %copy-start = (bf16[2,512,1024]{2,1,0:T(8,128)(2,1)S(1)}, bf16[2,512,1024]{2,1,0:T(8,128)(2,1)}, u32[]{:S(2)}) copy-start(bf16[2,512,1024]{2,1,0:T(8,128)(2,1)} %get-tuple-element.41.own) | copy-start | bytes 6291460
  20.9 21.9 %collective-permute-start.3 = (bf16[2,512,768]{2,1,0:T(8,128)(2,1)}, bf16[2,512,768]{2,1,0:T(8,128)(2,1)}, u32[]{:S(2)}, u32[]{:S(2)}) collective-permute-start(bf16[2,512,768]{2,1,0:T(8,128)(2,1)} %get-tuple-element.37), channel_id=1, source_target_pairs={{0,4},{4,0},{8,12},{12,8},{16,20},{20,16},{24,28},{28,24},{32,36},... | collective-permute-start | bytes 4718600 | tf_op jit(solution)/shard_map/ppermute | solution.py:38
  33.7 1.4 %collective-permute-start.1 = (f32[514]{0:T(1024)S(1)}, f32[514]{0:T(1024)S(1)}, u32[]{:S(2)}, u32[]{:S(2)}) collective-permute-start(f32[514]{0:T(1024)S(1)} %get-tuple-element.70), channel_id=1, source_target_pairs={{0,4},{4,0},{8,12},{12,8},{16,20},{20,16},{24,28},{28,24},{32,36},... | collective-permute-start | bytes 6176 | tf_op jit(solution)/shard_map/ppermute | solution.py:38
  33.8 7.7 %collective-permute-start.2 = (f32[514]{0:T(1024)S(1)}, f32[514]{0:T(1024)S(1)}, u32[]{:S(2)}, u32[]{:S(2)}) collective-permute-start(f32[514]{0:T(1024)S(1)} %get-tuple-element.71), channel_id=1, source_target_pairs={{4,13},{5,14},{6,15},{7,12},{8,1},{9,2},{10,3},{11,0},{12,21},{13,... | collective-permute-start | bytes 6176 | tf_op jit(solution)/shard_map/ppermute | solution.py:50
  35.1 6.4 %collective-permute-start.4 = (f32[514]{0:T(1024)S(1)}, f32[514]{0:T(1024)S(1)}, u32[]{:S(2)}, u32[]{:S(2)}) collective-permute-start(f32[514]{0:T(1024)S(1)} %collective-permute-done.1), channel_id=1, source_target_pairs={{0,9},{1,10},{2,11},{3,8},{8,17},{9,18},{10,19},{11,16},{12,5},{13... | collective-permute-start | bytes 6176 | tf_op jit(solution)/shard_map/ppermute | solution.py:50
  41.5 41.1 %collective-permute-start.6 = (bf16[2,512,256]{2,1,0:T(8,128)(2,1)}, bf16[2,512,256]{2,1,0:T(8,128)(2,1)S(1)}, u32[]{:S(2)}, u32[]{:S(2)}) collective-permute-start(bf16[2,512,256]{2,1,0:T(8,128)(2,1)} %get-tuple-element.40), channel_id=1, source_target_pairs={{0,4},{4,0},{8,12},{12,8},{16,20},{20,16},{24,28},{28,24},{32,36},... | collective-permute-start | bytes 1572872 | tf_op jit(solution)/shard_map/ppermute | solution.py:38
  41.5 47.2 %collective-permute-start.10 = (bf16[2,512,768]{2,1,0:T(8,128)(2,1)}, bf16[2,512,768]{2,1,0:T(8,128)(2,1)}, u32[]{:S(2)}, u32[]{:S(2)}) collective-permute-start(bf16[2,512,768]{2,1,0:T(8,128)(2,1)} %get-tuple-element.48.own), channel_id=1, source_target_pairs={{4,12},{8,0},{12,20},{16,8},{20,28},{24,16},{28,36},{32,24},{36,44... | collective-permute-start | bytes 4718600 | tf_op jit(solution)/shard_map/ppermute | solution.py:46
  60.3 33.8 %collective-permute-start.11 = (bf16[2,512,768]{2,1,0:T(8,128)(2,1)}, bf16[2,512,768]{2,1,0:T(8,128)(2,1)}, u32[]{:S(2)}, u32[]{:S(2)}) collective-permute-start(bf16[2,512,768]{2,1,0:T(8,128)(2,1)} %collective-permute-done.3.sib), channel_id=1, source_target_pairs={{0,8},{8,16},{12,4},{16,24},{20,12},{24,32},{28,20},{32,40},{36,28... | collective-permute-start | bytes 4718600 | tf_op jit(solution)/shard_map/ppermute | solution.py:46
  69.5 13.1 %copy-start.2 = (bf16[2,512,256]{2,1,0:T(8,128)(2,1)S(1)}, bf16[2,512,256]{2,1,0:T(8,128)(2,1)}, u32[]{:S(2)}) copy-start(bf16[2,512,256]{2,1,0:T(8,128)(2,1)} %get-tuple-element.46.own) | copy-start | bytes 1572868
  69.5 24.6 %copy-start.1 = (bf16[2,512,768]{2,1,0:T(8,128)(2,1)S(1)}, bf16[2,512,768]{2,1,0:T(8,128)(2,1)}, u32[]{:S(2)}) copy-start(bf16[2,512,768]{2,1,0:T(8,128)(2,1)} %get-tuple-element.48.own) | copy-start | bytes 4718596
  82.6 21.6 %collective-permute-start.8 = (bf16[2,512,256]{2,1,0:T(8,128)(2,1)S(1)}, bf16[2,512,256]{2,1,0:T(8,128)(2,1)S(1)}, u32[]{:S(2)}, u32[]{:S(2)}) collective-permute-start(bf16[2,512,256]{2,1,0:T(8,128)(2,1)S(1)} %copy-done.2), channel_id=1, source_target_pairs={{4,12},{8,0},{12,20},{16,8},{20,28},{24,16},{28,36},{32,24},{36,44... | collective-permute-start | bytes 1572872 | tf_op jit(solution)/shard_map/ppermute | solution.py:46
  83.9 20.3 %collective-permute-start.9 = (bf16[2,512,256]{2,1,0:T(8,128)(2,1)S(1)}, bf16[2,512,256]{2,1,0:T(8,128)(2,1)S(1)}, u32[]{:S(2)}, u32[]{:S(2)}) collective-permute-start(bf16[2,512,256]{2,1,0:T(8,128)(2,1)S(1)} %collective-permute-done.6.sib), channel_id=1, source_target_pairs={{0,8},{8,16},{12,4},{16,24},{20,12},{24,32},{28,20},{32,40},{36,28... | collective-permute-start | bytes 1572872 | tf_op jit(solution)/shard_map/ppermute | solution.py:46
  107.3 2.7 %collective-permute-start.12 = (f32[64,16,256]{2,1,0:T(8,128)S(1)}, f32[64,16,256]{2,1,0:T(8,128)S(1)}, u32[]{:S(2)}, u32[]{:S(2)}) collective-permute-start(f32[64,16,256]{2,1,0:T(8,128)S(1)} %get-tuple-element.52), channel_id=1, source_target_pairs={{0,4},{4,0},{8,12},{12,8},{16,20},{20,16},{24,28},{28,24},{32,36},... | collective-permute-start | bytes 3145736 | tf_op jit(solution)/shard_map/ppermute | solution.py:38

commit v6 on v5

--- a/solution.py
+++ b/solution.py
@@ -65,57 +65,81 @@
     return one[0] * other[0] - one[1] * other[1], one[1] * other[0] + one[0] * other[1]
 
 
-def planes_kernel(column, core_ref, *refs):
-    count = (len(refs) - 4) // 2
+def power_of(planes):
+    re, im = planes[0].astype(jnp.float32), planes[1].astype(jnp.float32)
+    power = re * re + im * im
+    total = power[:, :LANES]
+    for f in range(LANES, power.shape[1], LANES):
+        total += power[:, f : f + LANES]
+    return total
+
+
+def planes_kernel(with_power, core_ref, *refs):
+    count = len(refs) // 2 - 1
     for n, records_ref in enumerate(refs[:2]):
-        *planes_refs, power_ref = refs[2 + n * (count + 1) : 2 + (n + 1) * (count + 1)]
-        channels, _, width = records_ref.shape
-        width -= column
-        for s in range(0, channels, SLAB):
-            planes = jnp.swapaxes(records_ref[s : s + SLAB, :, column:], 0, 1)
+        outs = refs[2 + n * count : 2 + (n + 1) * count]
+        for s in range(0, records_ref.shape[0], SLAB):
+            planes = jnp.swapaxes(records_ref[s : s + SLAB], 0, 1)
             start = 0
-            for ref in planes_refs:
+            for ref in outs[: count - with_power]:
                 cut = ref.shape[2]
                 ref[:, s : s + SLAB, :] = planes[:, :, start : start + cut]
                 start += cut
-            re, im = planes[0].astype(jnp.float32), planes[1].astype(jnp.float32)
-            power = re * re + im * im
-            total = power[:, :LANES]
-            for f in range(LANES, width, LANES):
-                total += power[:, f : f + LANES]
-            power_ref[s : s + SLAB, :] = total
-
-
-def planes(records, core, start, cuts):
+            if with_power:
+                outs[-1][s : s + SLAB, :] = power_of(planes)
+
+
+def planes(records, core, start, cuts, with_power):
     half = records.shape[0] // 2
     width = sum(cuts)
-    aligned = start % width == 0
-    loaded, column = (width, start // width) if aligned else (records.shape[2], 0)
+    column = start // width
     block = 256
     steps = half // block
     outs = [pl.BlockSpec((2, block, cut), lambda t, c: (0, t, 0)) for cut in cuts]
-    outs += [pl.BlockSpec((block, LANES), lambda t, c: (t, 0))]
     shapes = [jax.ShapeDtypeStruct((2, half, cut), jnp.bfloat16) for cut in cuts]
-    shapes += [jax.ShapeDtypeStruct((half, LANES), jnp.float32)]
+    if with_power:
+        outs += [pl.BlockSpec((block, LANES), lambda t, c: (t, 0))]
+        shapes += [jax.ShapeDtypeStruct((half, LANES), jnp.float32)]
     spec = pltpu.PrefetchScalarGridSpec(
         num_scalar_prefetch=1,
         grid=(steps,),
         in_specs=[
-            pl.BlockSpec((block, 2, loaded), lambda t, c: (c[0] * steps + t, 0, column)),
-            pl.BlockSpec((block, 2, loaded), lambda t, c: ((1 - c[0]) * steps + t, 0, column)),
+            pl.BlockSpec((block, 2, width), lambda t, c: (c[0] * steps + t, 0, column)),
+            pl.BlockSpec((block, 2, width), lambda t, c: ((1 - c[0]) * steps + t, 0, column)),
         ],
         out_specs=outs * 2,
     )
     results = pl.pallas_call(
-        functools.partial(planes_kernel, 0 if aligned else start),
+        functools.partial(planes_kernel, int(with_power)),
         grid_spec=spec,
         out_shape=shapes * 2,
         compiler_params=params(),
         cost_estimate=cost(),
         name="planes",
     )(core, records, records)
-    n = len(cuts)
-    return list(results[:n]), results[n], list(results[n + 1 : -1]), results[-1]
+    return list(results[: len(outs)]), list(results[len(outs) :])
+
+
+def power_kernel(*refs):
+    for planes_ref, power_ref in zip(refs[:2], refs[2:]):
+        for s in range(0, planes_ref.shape[1], SLAB):
+            power_ref[s : s + SLAB, :] = power_of(planes_ref[:, s : s + SLAB, :])
+
+
+def powers(*blocks):
+    _, channels, width = blocks[0].shape
+    block = channels // 2
+    out = jax.ShapeDtypeStruct((channels, LANES), jnp.float32)
+    return pl.pallas_call(
+        power_kernel,
+        grid=(channels // block,),
+        in_specs=[pl.BlockSpec((2, block, width), lambda t: (0, t, 0))] * 2,
+        out_specs=[pl.BlockSpec((block, LANES), lambda t: (t, 0))] * 2,
+        out_shape=[out, out],
+        compiler_params=params(),
+        cost_estimate=cost(),
+        name="powers",
+    )(*blocks)
 
 
 def load(ref, rows):
@@ -263,11 +287,14 @@
     bins = bin_row.shape[0]
 
     core_ref = core.astype(jnp.int32)[None]
-    own, own_power, give, give_power = planes(records, core_ref, 0, CUTS[:1])
+    own, give = planes(records, core_ref, 0, CUTS[:1], False)
+    own_power, give_power = powers(own[0], give[0])
     sib = [to_sibling(give[0])]
     moved = [to_chips(own[0], (-1, 1)), to_chips(sib[0], (1, -1))]
     records, sib[0] = after(records, sib[0])
-    rest_own, more_own, rest, more_give = planes(records, core_ref, CUTS[0], CUTS[1:])
+    (*rest_own, more_own), (*rest, more_give) = planes(
+        records, core_ref, CUTS[0], CUTS[1:], True
+    )
     own, own_power, give_power = own + rest_own, own_power + more_own, give_power + more_give
 
     totals = lax.psum(jnp.sum(jnp.stack([own_power, give_power]), axis=2), "freq")

time: 137 us -> 135 us (0.985)
  waiting for transfers between devices: 29.8 us -> 24.4 us
  Pallas kernels: 37 us -> 38.7 us
    ppermute x5, waiting for transfers between devices: 5.68 us -> 2.66 us  [to_sibling(): lax.ppermute(block, 'chan', [(i, i ^ 1) for i in range(lax.axis_size('cha...]
    ppermute x6, waiting for transfers between devices: 23 us -> 20.5 us  [to_chips(): return lax.ppermute(block, 'chan', route)]
    pallas_call x2 -> x3, Pallas kernels: 10.9 us -> 12.7 us  [the longest x2 9.41 us: planes(): pl.pallas_call(functools.partial(planes_kernel, int(with_power)), grid_sp...]
  transfers between devices with their start and end apart: 13 -> 13, of which waited for: 5 -> 4; matrix products, arithmetic and copies ran while one was open for 4% -> 4% of each run, Pallas kernels for 21% -> 24%
where the time goes in v6:
time: 135 us
  Pallas kernels  38.7 us (29%)
  blocking collectives  37.1 us (27%)
  starting transfers between devices  26.3 us (19%)
  waiting for transfers between devices  24.4 us (18%)
  other arithmetic  4.46 us (3%)
  between operations  2.19 us (2%)
  local copies, waits for them, and re-layouts  1.45 us (1%)
    all_to_all x1, blocking collectives, shards(): lax.all_to_all(total, ('chan', 'freq'), 0, 0, axis_index_groups=ways, til...  26.5 us
    pallas_call x3, Pallas kernels, add_pairs(): pl.pallas_call(functools.partial(pairs_kernel, first, is_last), grid=(cut...  26.1 us
    ppermute x6, starting transfers between devices, to_chips(): return lax.ppermute(block, 'chan', route)  20.6 us
    ppermute x6, waiting for transfers between devices, to_chips(): return lax.ppermute(block, 'chan', route)  20.5 us
    psum x1, blocking collectives, shards(): lax.psum(jnp.sum(jnp.stack([own_power, give_power]), axis=2), 'freq')  10.6 us
    pallas_call x2, Pallas kernels, planes(): pl.pallas_call(functools.partial(planes_kernel, int(with_power)), grid_sp...  9.41 us
    ppermute x2, starting transfers between devices, to_chips(): return lax.ppermute(block, ('chan', 'freq'), route)  5.52 us
    pallas_call x1, Pallas kernels, powers(): pl.pallas_call(power_kernel, grid=(channels // block,), in_specs=[pl.Bloc...  3.26 us
  transfers between devices with their start and end apart: 13, of which 4 were waited for; matrix products, arithmetic and copies ran while one was open for 4% of the time, Pallas kernels for 24%

profile of v6, /device:TPU:0, one launch (start us, length us, event | category | flops | bytes accessed | tf_op | source)
XLA Modules:
  0.0 134.7 jit_solution(1054621267049228375)
XLA Ops:
  0.0 3.9 %planes.2 = (bf16[2,512,1024]{2,1,0:T(8,128)(2,1)}, bf16[2,512,1024]{2,1,0:T(8,128)(2,1)}) custom-call(s32[1]{0:T(128)} %bitcast.core_ref.core, bf16[1024,2,2048]{2,1,0:T(2,128)(2,1)} %refs_1_.2, bf16[1024,2,2048]{2,1,0:T(2,128)(2,1)} %refs_1_.2), custom_call_target="tpu_custom_call" | custom-call | flops 1 | bytes 1 | tf_op jit(solution)/shard_map/planes/pallas_call | solution.py:112
  3.9 1.4 %collective-permute-start.7 = (bf16[2,512,1024]{2,1,0:T(8,128)(2,1)}, bf16[2,512,1024]{2,1,0:T(8,128)(2,1)}, u32[]{:S(2)}, u32[]{:S(2)}) collective-permute-start(bf16[2,512,1024]{2,1,0:T(8,128)(2,1)} %get-tuple-element.29.refs_0_.own), channel_id=1, source_target_pairs={{4,12},{8,0},{12,20},{16,8},{20,28},{24,16},{28,36},{32,24},{36,44... | collective-permute-start | bytes 6291464 | tf_op jit(solution)/shard_map/ppermute | solution.py:46
  5.3 3.3 %powers.1 = (f32[512,128]{1,0:T(8,128)}, f32[512,128]{1,0:T(8,128)}) custom-call(bf16[2,512,1024]{2,1,0:T(8,128)(2,1)} %get-tuple-element.29.refs_0_.own, bf16[2,512,1024]{2,1,0:T(8,128)(2,1)} %get-tuple-element.30.refs_1_), custom_call_target="tpu_custom_call" | custom-call | flops 1 | bytes 1 | tf_op jit(solution)/shard_map/powers/pallas_call | solution.py:133
  8.6 0.1 fusion.4
  8.7 5.9 %collective-permute-start.5 = (bf16[2,512,1024]{2,1,0:T(8,128)(2,1)}, bf16[2,512,1024]{2,1,0:T(8,128)(2,1)}, u32[]{:S(2)}, u32[]{:S(2)}) collective-permute-start(bf16[2,512,1024]{2,1,0:T(8,128)(2,1)} %collective-permute-done.sib), channel_id=1, source_target_pairs={{0,8},{8,16},{12,4},{16,24},{20,12},{24,32},{28,20},{32,40},{36,28... | collective-permute-start | bytes 6291464 | tf_op jit(solution)/shard_map/ppermute | solution.py:46
  14.7 0.1 fusion.5
  14.8 5.5 %planes.3 = (bf16[2,512,768]{2,1,0:T(8,128)(2,1)}, bf16[2,512,256]{2,1,0:T(8,128)(2,1)}, f32[512,128]{1,0:T(8,128)}, bf16[2,512,768]{2,1,0:T(8,128)(2,1)}, bf16[...) custom-call(s32[1]{0:T(128)} %bitcast.core_ref.core, bf16[1024,2,2048]{2,1,0:T(2,128)(2,1)} %refs_1_.2, ...), custom_call_target="tpu_custom_call" | custom-call | flops 1 | bytes 1 | tf_op jit(solution)/shard_map/planes/pallas_call | solution.py:112
  20.3 0.1 collective-permute-start.3
  20.5 0.7 negate_multiply_fusion
  21.3 1.1 add_bitcast_fusion
  22.4 0.2 maximum_reduce_fusion
  22.6 10.6 %psum.7 = f32[2,512]{1,0:T(2,128)S(1)} all-reduce(f32[2,512]{1,0:T(2,128)S(1)} %maximum_reduce_fusion), channel_id=1, replica_groups=mesh['chan'=32,'freq'=4] {'freq'}, use_global_device_ids=true, to_apply=%region_1.2 | all-reduce | flops 1024 | bytes 8192 | tf_op jit(solution)/shard_map/psum | solution.py:300
  33.3 1.3 collective-permute-start.2
  34.6 4.2 %collective-permute-start.4 = (f32[514]{0:T(1024)S(1)}, f32[514]{0:T(1024)S(1)}, u32[]{:S(2)}, u32[]{:S(2)}) collective-permute-start(f32[514]{0:T(1024)S(1)} %collective-permute-done.1), channel_id=1, source_target_pairs={{0,9},{1,10},{2,11},{3,8},{8,17},{9,18},{10,19},{11,16},{12,5},{13... | collective-permute-start | bytes 6176 | tf_op jit(solution)/shard_map/ppermute | solution.py:50
  38.9 1.0 select_reduce_fusion
  39.8 1.2 collective-permute-done.2
  41.0 1.3 collective-permute-start.10
  42.3 16.6 %collective-permute-done.5.from_sib = bf16[2,512,1024]{2,1,0:T(8,128)(2,1)} collective-permute-done((bf16[2,512,1024]{2,1,0:T(8,128)(2,1)}, bf16[2,512,1024]{2,1,0:T(8,128)(2,1)}, u32[]{:S(2)}, u32[]{:S(2)}) %collective-permute-start.5) | collective-permute-done | bytes 2097184 | tf_op jit(solution)/shard_map/ppermute | solution.py:46
  58.9 5.9 %collective-permute-start.11 = (bf16[2,512,768]{2,1,0:T(8,128)(2,1)}, bf16[2,512,768]{2,1,0:T(8,128)(2,1)}, u32[]{:S(2)}, u32[]{:S(2)}) collective-permute-start(bf16[2,512,768]{2,1,0:T(8,128)(2,1)} %collective-permute-done.3.sib), channel_id=1, source_target_pairs={{0,8},{8,16},{12,4},{16,24},{20,12},{24,32},{28,20},{32,40},{36,28... | collective-permute-start | bytes 4718600 | tf_op jit(solution)/shard_map/ppermute | solution.py:46
  64.8 0.6 fusion.6
  66.7 0.6 slice.34
  68.0 0.1 copy.16
  68.3 13.0 %add_pairs.3.refs_3_ = f32[512,1024]{1,0:T(8,128)S(1)} custom-call(s32[1]{0:T(128)} %bitcast.core_ref.core, s32[1,2048]{1,0:T(1,128)S(1)} %bitcast.32, bf16[2,512,1024]{2,1,0:T(8,128)(2,1)S(1)} %copy-done, bf16[2,512,1024]{2,1,0:T(8,128)(2,1)} %collective-permute-done.sib, bf16[2,512,1024]{2,1,0:T(8,128)(2,1)} %collective-permute-done.7.from_own, ...), custom_call_target="tpu_custom_call" | custom-call | flops 1 | bytes 1 | tf_op jit(solution)/shard_map/add_pairs/pallas_call | solution.py:267
  81.3 1.3 collective-permute-start.8
  82.6 4.8 %collective-permute-start.9 = (bf16[2,512,256]{2,1,0:T(8,128)(2,1)S(1)}, bf16[2,512,256]{2,1,0:T(8,128)(2,1)S(1)}, u32[]{:S(2)}, u32[]{:S(2)}) collective-permute-start(bf16[2,512,256]{2,1,0:T(8,128)(2,1)S(1)} %collective-permute-done.6.sib), channel_id=1, source_target_pairs={{0,8},{8,16},{12,4},{16,24},{20,12},{24,32},{28,20},{32,40},{36,28... | collective-permute-start | bytes 1572872 | tf_op jit(solution)/shard_map/ppermute | solution.py:46
  87.4 4.0 %collective-permute-done.11.from_sib = bf16[2,512,768]{2,1,0:T(8,128)(2,1)} collective-permute-done((bf16[2,512,768]{2,1,0:T(8,128)(2,1)}, bf16[2,512,768]{2,1,0:T(8,128)(2,1)}, u32[]{:S(2)}, u32[]{:S(2)}) %collective-permute-start.11) | collective-permute-done | bytes 1572896 | tf_op jit(solution)/shard_map/ppermute | solution.py:46
  91.4 10.0 %add_pairs.4.refs_3_ = f32[512,1024]{1,0:T(8,128)S(1)} custom-call(s32[1]{0:T(128)} %bitcast.core_ref.core, s32[1,2048]{1,0:T(1,128)S(1)} %bitcast.33, bf16[2,512,768]{2,1,0:T(8,128)(2,1)S(1)} %copy-done.1, bf16[2,512,768]{2,1,0:T(8,128)(2,1)} %collective-permute-done.3.sib, bf16[2,512,768]{2,1,0:T(8,128)(2,1)} %collective-permute-done.10.from_own, ...), custom_call_target="tpu_custom_call" | custom-call | flops 1 | bytes 1 | tf_op jit(solution)/shard_map/add_pairs/pallas_call | solution.py:267
  101.4 3.1 %add_pairs.5 = (f32[64,16,256]{2,1,0:T(8,128)S(1)}, f32[64,16,256]{2,1,0:T(8,128)S(1)}) custom-call(s32[1]{0:T(128)} %bitcast.core_ref.core, s32[1,2048]{1,0:T(1,128)S(1)} %bitcast.34, bf16[2,512,256]{2,1,0:T(8,128)(2,1)S(1)} %copy-done.2, bf16[2,512,256]{2,1,0:T(8,128)(2,1)S(1)} %collective-permute-done.6.sib, ...), custom_call_target="tpu_custom_call" | custom-call | flops 1 | bytes 1 | tf_op jit(solution)/shard_map/add_pairs/pallas_call | solution.py:267
  104.5 2.6 %collective-permute-done.12 = f32[64,16,256]{2,1,0:T(8,128)S(1)} collective-permute-done((f32[64,16,256]{2,1,0:T(8,128)S(1)}, f32[64,16,256]{2,1,0:T(8,128)S(1)}, u32[]{:S(2)}, u32[]{:S(2)}) %collective-permute-start.12) | collective-permute-done | bytes 1048608 | tf_op jit(solution)/shard_map/ppermute | solution.py:38
  107.2 0.3 add_convert_fusion
  107.5 26.5 %all_to_all.5 = bf16[64,16,256]{2,1,0:T(8,128)(2,1)S(1)} all-to-all(bf16[64,16,256]{2,1,0:T(8,128)(2,1)S(1)} %add_convert_fusion), channel_id=1, replica_groups={{0,1,2,3,8,9,10,11,16,17,18,19,24,25,26,27,32,33,34,35,40,41,42,43,48,4..., dimensions={0} | all-to-all | bytes 1048576 | tf_op jit(solution)/shard_map/all_to_all | solution.py:359
  134.0 0.7 convert_reduce_fusion
  (50 shorter events, 0.6 us)
Async XLA Ops:
  3.9 4.8 %collective-permute-start = (bf16[2,512,1024]{2,1,0:T(8,128)(2,1)}, bf16[2,512,1024]{2,1,0:T(8,128)(2,1)}, u32[]{:S(2)}, u32[]{:S(2)}) collective-permute-start(bf16[2,512,1024]{2,1,0:T(8,128)(2,1)} %get-tuple-element.30.refs_1_), channel_id=1, source_target_pairs={{0,4},{4,0},{8,12},{12,8},{16,20},{20,16},{24,28},{28,24},{32,36},... | collective-permute-start | bytes 6291464 | tf_op jit(solution)/shard_map/ppermute | solution.py:38
  3.9 4.7 %copy-start.5 = (s32[32768]{0:T(1024)S(1)}, s32[32768]{0:T(1024)}, u32[]{:S(2)}) copy-start(s32[32768]{0:T(1024)} %param.5) | copy-start | bytes 393220
  3.9 64.3 %collective-permute-start.7 = (bf16[2,512,1024]{2,1,0:T(8,128)(2,1)}, bf16[2,512,1024]{2,1,0:T(8,128)(2,1)}, u32[]{:S(2)}, u32[]{:S(2)}) collective-permute-start(bf16[2,512,1024]{2,1,0:T(8,128)(2,1)} %get-tuple-element.29.refs_0_.own), channel_id=1, source_target_pairs={{4,12},{8,0},{12,20},{16,8},{20,28},{24,16},{28,36},{32,24},{36,44... | collective-permute-start | bytes 6291464 | tf_op jit(solution)/shard_map/ppermute | solution.py:46
  8.7 50.2 %collective-permute-start.5 = (bf16[2,512,1024]{2,1,0:T(8,128)(2,1)}, bf16[2,512,1024]{2,1,0:T(8,128)(2,1)}, u32[]{:S(2)}, u32[]{:S(2)}) collective-permute-start(bf16[2,512,1024]{2,1,0:T(8,128)(2,1)} %collective-permute-done.sib), channel_id=1, source_target_pairs={{0,8},{8,16},{12,4},{16,24},{20,12},{24,32},{28,20},{32,40},{36,28... | collective-permute-start | bytes 6291464 | tf_op jit(solution)/shard_map/ppermute | solution.py:46
  14.8 5.7 %copy-start.7 = (s32[1,2]{1,0:T(1,128)S(1)}, s32[1,2]{1,0:T(1,128)}, u32[]{:S(2)}) copy-start(s32[1,2]{1,0:T(1,128)} %param.7) | copy-start | bytes 28
  14.8 6.5 %copy-start.3 = (f32[512,128]{1,0:T(8,128)S(1)}, f32[512,128]{1,0:T(8,128)}, u32[]{:S(2)}) copy-start(f32[512,128]{1,0:T(8,128)} %get-tuple-element.31) | copy-start | bytes 786436
  14.8 6.5 %copy-start.4 = (f32[512,128]{1,0:T(8,128)S(1)}, f32[512,128]{1,0:T(8,128)}, u32[]{:S(2)}) copy-start(f32[512,128]{1,0:T(8,128)} %get-tuple-element.34) | copy-start | bytes 786436
  20.3 18.5 %copy-start.6 = (s32[512]{0:T(512)S(1)}, s32[512]{0:T(512)}, u32[]{:S(2)}) copy-start(s32[512]{0:T(512)} %param.6) | copy-start | bytes 6148
  20.3 47.9 %copy-start = (bf16[2,512,1024]{2,1,0:T(8,128)(2,1)S(1)}, bf16[2,512,1024]{2,1,0:T(8,128)(2,1)}, u32[]{:S(2)}) copy-start(bf16[2,512,1024]{2,1,0:T(8,128)(2,1)} %get-tuple-element.29.refs_0_.own) | copy-start | bytes 6291460
  20.3 22.0 %collective-permute-start.3 = (bf16[2,512,768]{2,1,0:T(8,128)(2,1)}, bf16[2,512,768]{2,1,0:T(8,128)(2,1)}, u32[]{:S(2)}, u32[]{:S(2)}) collective-permute-start(bf16[2,512,768]{2,1,0:T(8,128)(2,1)} %get-tuple-element.38), channel_id=1, source_target_pairs={{0,4},{4,0},{8,12},{12,8},{16,20},{20,16},{24,28},{28,24},{32,36},... | collective-permute-start | bytes 4718600 | tf_op jit(solution)/shard_map/ppermute | solution.py:38
  33.2 1.4 %collective-permute-start.1 = (f32[514]{0:T(1024)S(1)}, f32[514]{0:T(1024)S(1)}, u32[]{:S(2)}, u32[]{:S(2)}) collective-permute-start(f32[514]{0:T(1024)S(1)} %get-tuple-element.70), channel_id=1, source_target_pairs={{0,4},{4,0},{8,12},{12,8},{16,20},{20,16},{24,28},{28,24},{32,36},... | collective-permute-start | bytes 6176 | tf_op jit(solution)/shard_map/ppermute | solution.py:38
  33.3 7.7 %collective-permute-start.2 = (f32[514]{0:T(1024)S(1)}, f32[514]{0:T(1024)S(1)}, u32[]{:S(2)}, u32[]{:S(2)}) collective-permute-start(f32[514]{0:T(1024)S(1)} %get-tuple-element.71), channel_id=1, source_target_pairs={{4,13},{5,14},{6,15},{7,12},{8,1},{9,2},{10,3},{11,0},{12,21},{13,... | collective-permute-start | bytes 6176 | tf_op jit(solution)/shard_map/ppermute | solution.py:50
  34.6 6.4 %collective-permute-start.4 = (f32[514]{0:T(1024)S(1)}, f32[514]{0:T(1024)S(1)}, u32[]{:S(2)}, u32[]{:S(2)}) collective-permute-start(f32[514]{0:T(1024)S(1)} %collective-permute-done.1), channel_id=1, source_target_pairs={{0,9},{1,10},{2,11},{3,8},{8,17},{9,18},{10,19},{11,16},{12,5},{13... | collective-permute-start | bytes 6176 | tf_op jit(solution)/shard_map/ppermute | solution.py:50
  41.0 40.3 %collective-permute-start.6 = (bf16[2,512,256]{2,1,0:T(8,128)(2,1)}, bf16[2,512,256]{2,1,0:T(8,128)(2,1)S(1)}, u32[]{:S(2)}, u32[]{:S(2)}) collective-permute-start(bf16[2,512,256]{2,1,0:T(8,128)(2,1)} %get-tuple-element.41), channel_id=1, source_target_pairs={{0,4},{4,0},{8,12},{12,8},{16,20},{20,16},{24,28},{28,24},{32,36},... | collective-permute-start | bytes 1572872 | tf_op jit(solution)/shard_map/ppermute | solution.py:38
  41.0 46.3 %collective-permute-start.10 = (bf16[2,512,768]{2,1,0:T(8,128)(2,1)}, bf16[2,512,768]{2,1,0:T(8,128)(2,1)}, u32[]{:S(2)}, u32[]{:S(2)}) collective-permute-start(bf16[2,512,768]{2,1,0:T(8,128)(2,1)} %get-tuple-element.48.own), channel_id=1, source_target_pairs={{4,12},{8,0},{12,20},{16,8},{20,28},{24,16},{28,36},{32,24},{36,44... | collective-permute-start | bytes 4718600 | tf_op jit(solution)/shard_map/ppermute | solution.py:46
  58.9 32.4 %collective-permute-start.11 = (bf16[2,512,768]{2,1,0:T(8,128)(2,1)}, bf16[2,512,768]{2,1,0:T(8,128)(2,1)}, u32[]{:S(2)}, u32[]{:S(2)}) collective-permute-start(bf16[2,512,768]{2,1,0:T(8,128)(2,1)} %collective-permute-done.3.sib), channel_id=1, source_target_pairs={{0,8},{8,16},{12,4},{16,24},{20,12},{24,32},{28,20},{32,40},{36,28... | collective-permute-start | bytes 4718600 | tf_op jit(solution)/shard_map/ppermute | solution.py:46
  68.3 13.1 %copy-start.2 = (bf16[2,512,256]{2,1,0:T(8,128)(2,1)S(1)}, bf16[2,512,256]{2,1,0:T(8,128)(2,1)}, u32[]{:S(2)}) copy-start(bf16[2,512,256]{2,1,0:T(8,128)(2,1)} %get-tuple-element.46.own) | copy-start | bytes 1572868
  68.3 23.1 %copy-start.1 = (bf16[2,512,768]{2,1,0:T(8,128)(2,1)S(1)}, bf16[2,512,768]{2,1,0:T(8,128)(2,1)}, u32[]{:S(2)}) copy-start(bf16[2,512,768]{2,1,0:T(8,128)(2,1)} %get-tuple-element.48.own) | copy-start | bytes 4718596
  81.3 20.1 %collective-permute-start.8 = (bf16[2,512,256]{2,1,0:T(8,128)(2,1)S(1)}, bf16[2,512,256]{2,1,0:T(8,128)(2,1)S(1)}, u32[]{:S(2)}, u32[]{:S(2)}) collective-permute-start(bf16[2,512,256]{2,1,0:T(8,128)(2,1)S(1)} %copy-done.2), channel_id=1, source_target_pairs={{4,12},{8,0},{12,20},{16,8},{20,28},{24,16},{28,36},{32,24},{36,44... | collective-permute-start | bytes 1572872 | tf_op jit(solution)/shard_map/ppermute | solution.py:46
  82.6 18.8 %collective-permute-start.9 = (bf16[2,512,256]{2,1,0:T(8,128)(2,1)S(1)}, bf16[2,512,256]{2,1,0:T(8,128)(2,1)S(1)}, u32[]{:S(2)}, u32[]{:S(2)}) collective-permute-start(bf16[2,512,256]{2,1,0:T(8,128)(2,1)S(1)} %collective-permute-done.6.sib), channel_id=1, source_target_pairs={{0,8},{8,16},{12,4},{16,24},{20,12},{24,32},{28,20},{32,40},{36,28... | collective-permute-start | bytes 1572872 | tf_op jit(solution)/shard_map/ppermute | solution.py:46
  104.5 2.7 %collective-permute-start.12 = (f32[64,16,256]{2,1,0:T(8,128)S(1)}, f32[64,16,256]{2,1,0:T(8,128)S(1)}, u32[]{:S(2)}, u32[]{:S(2)}) collective-permute-start(f32[64,16,256]{2,1,0:T(8,128)S(1)} %get-tuple-element.52), channel_id=1, source_target_pairs={{0,4},{4,0},{8,12},{12,8},{16,20},{20,16},{24,28},{28,24},{32,36},... | collective-permute-start | bytes 3145736 | tf_op jit(solution)/shard_map/ppermute | solution.py:38

commit v7 on v6

--- a/solution.py
+++ b/solution.py
@@ -120,6 +120,53 @@
     return list(results[: len(outs)]), list(results[len(outs) :])
 
 
+def head_kernel(core_ref, records_ref, own_ref, give_ref, raw, done, came, gone):
+    _, half, width = own_ref.shape
+    pieces, block = raw.shape[:2]
+    per_side = pieces // 2
+
+    def copy_in(n):
+        side, row = n // per_side, n % per_side * block
+        first = (core_ref[0] if side == 0 else 1 - core_ref[0]) * half + row
+        rows = pl.ds(pl.multiple_of(first, block), block)
+        return pltpu.make_async_copy(records_ref.at[rows, :, :width], raw.at[n], came.at[n])
+
+    def copy_out(n):
+        out_ref, row = (own_ref, give_ref)[n // per_side], n % per_side * block
+        return pltpu.make_async_copy(done.at[n], out_ref.at[:, row : row + block, :], gone.at[n])
+
+    for n in range(pieces):
+        copy_in(n).start()
+    for n in range(pieces):
+        copy_in(n).wait()
+        for s in range(0, block, SLAB):
+            done[n, :, s : s + SLAB, :] = jnp.swapaxes(raw[n, s : s + SLAB], 0, 1)
+        copy_out(n).start()
+    for n in range(pieces):
+        copy_out(n).wait()
+
+
+def head_planes(records, core, width):
+    half = records.shape[0] // 2
+    pieces, block = 8, half // 4
+    out = jax.ShapeDtypeStruct((2, half, width), jnp.bfloat16)
+    return pl.pallas_call(
+        head_kernel,
+        in_specs=[pl.BlockSpec(memory_space=pltpu.SMEM), pl.BlockSpec(memory_space=pl.ANY)],
+        out_specs=[pl.BlockSpec(memory_space=pl.ANY)] * 2,
+        out_shape=[out, out],
+        scratch_shapes=[
+            pltpu.VMEM((pieces, block, 2, width), jnp.bfloat16),
+            pltpu.VMEM((pieces, 2, block, width), jnp.bfloat16),
+            pltpu.SemaphoreType.DMA((pieces,)),
+            pltpu.SemaphoreType.DMA((pieces,)),
+        ],
+        compiler_params=params(),
+        cost_estimate=cost(),
+        name="head_planes",
+    )(core, records)
+
+
 def power_kernel(*refs):
     for planes_ref, power_ref in zip(refs[:2], refs[2:]):
         for s in range(0, planes_ref.shape[1], SLAB):
@@ -214,8 +261,11 @@
             pairs = slice(part * 4 * count, (part + 1) * 4 * count)
             sums = jnp.dot(onehot[:, pairs], prods[...], preferred_element_type=jnp.float32)
             stack = sums if stack is None else stack + sums
-        stack = stack.astype(jnp.bfloat16)
-        lagged = jnp.dot(stack, table[...], preferred_element_type=jnp.float32)
+        high = stack.astype(jnp.bfloat16)
+        lagged = jnp.dot(high, table[...], preferred_element_type=jnp.float32)
+        if first == 0:
+            low = (stack - high.astype(jnp.float32)).astype(jnp.bfloat16)
+            lagged += jnp.dot(low, table[...], preferred_element_type=jnp.float32)
 
         @pl.when(step == 0)
         def _():
@@ -287,7 +337,7 @@
     bins = bin_row.shape[0]
 
     core_ref = core.astype(jnp.int32)[None]
-    own, give = planes(records, core_ref, 0, CUTS[:1], False)
+    own, give = [[block] for block in head_planes(records, core_ref, CUTS[0])]
     own_power, give_power = powers(own[0], give[0])
     sib = [to_sibling(give[0])]
     moved = [to_chips(own[0], (-1, 1)), to_chips(sib[0], (1, -1))]

time: 135 us -> 133 us (0.985)
  waiting for transfers between devices: 24.4 us -> 20.1 us
  Pallas kernels: 38.7 us -> 40.5 us
    ppermute x6, waiting for transfers between devices: 20.5 us -> 16.5 us  [to_chips(): return lax.ppermute(block, 'chan', route)]
    pallas_call x2 -> x1, Pallas kernels: 9.41 us -> 5.5 us  [planes(): pl.pallas_call(functools.partial(planes_kernel, int(with_power)), grid_sp...]
    pallas_call x0 -> x1, Pallas kernels: none -> 3.44 us  [head_planes(): pl.pallas_call(head_kernel, in_specs=[pl.BlockSpec(memory_space=pltpu.SME...]
    pallas_call x3, Pallas kernels: 26.1 us -> 28.3 us  [add_pairs(): pl.pallas_call(functools.partial(pairs_kernel, first, is_last), grid=(cut...]
  transfers between devices with their start and end apart: 13 -> 13, of which waited for: 4 -> 3; matrix products, arithmetic and copies ran while one was open for 4% -> 4% of each run, Pallas kernels for 24% -> 26%
where the time goes in v7:
time: 133 us
  Pallas kernels  40.5 us (30%)
  blocking collectives  37.5 us (28%)
  starting transfers between devices  26.8 us (20%)
  waiting for transfers between devices  20.1 us (15%)
  other arithmetic  4.46 us (3%)
  between operations  2.22 us (2%)
  local copies, waits for them, and re-layouts  1.45 us (1%)
    pallas_call x3, Pallas kernels, add_pairs(): pl.pallas_call(functools.partial(pairs_kernel, first, is_last), grid=(cut...  28.3 us
    all_to_all x1, blocking collectives, shards(): lax.all_to_all(total, ('chan', 'freq'), 0, 0, axis_index_groups=ways, til...  26.9 us
    ppermute x6, starting transfers between devices, to_chips(): return lax.ppermute(block, 'chan', route)  20.6 us
    ppermute x6, waiting for transfers between devices, to_chips(): return lax.ppermute(block, 'chan', route)  16.5 us
    psum x1, blocking collectives, shards(): lax.psum(jnp.sum(jnp.stack([own_power, give_power]), axis=2), 'freq')  10.6 us
    ppermute x2, starting transfers between devices, to_chips(): return lax.ppermute(block, ('chan', 'freq'), route)  5.52 us
    pallas_call x1, Pallas kernels, planes(): pl.pallas_call(functools.partial(planes_kernel, int(with_power)), grid_sp...  5.5 us
    pallas_call x1, Pallas kernels, head_planes(): pl.pallas_call(head_kernel, in_specs=[pl.BlockSpec(memory_space=pltpu.SME...  3.44 us
  transfers between devices with their start and end apart: 13, of which 3 were waited for; matrix products, arithmetic and copies ran while one was open for 4% of the time, Pallas kernels for 26%

profile of v7, /device:TPU:0, one launch (start us, length us, event | category | flops | bytes accessed | tf_op | source)
XLA Modules:
  0.0 133.0 jit_solution(18323164628052698395)
XLA Ops:
  0.0 3.4 %head_planes.1 = (bf16[2,512,1024]{2,1,0:T(8,128)(2,1)}, bf16[2,512,1024]{2,1,0:T(8,128)(2,1)}) custom-call(s32[1]{0:T(128)} %bitcast.core_ref.core, bf16[1024,2,2048]{2,1,0:T(2,128)(2,1)} %refs_1_), custom_call_target="tpu_custom_call" | custom-call | flops 1 | bytes 1 | tf_op jit(solution)/shard_map/head_planes/pallas_call | solution.py:153
  3.5 0.1 collective-permute-start
  3.6 1.4 %collective-permute-start.7 = (bf16[2,512,1024]{2,1,0:T(8,128)(2,1)}, bf16[2,512,1024]{2,1,0:T(8,128)(2,1)}, u32[]{:S(2)}, u32[]{:S(2)}) collective-permute-start(bf16[2,512,1024]{2,1,0:T(8,128)(2,1)} %get-tuple-element.29.refs_0_.own), channel_id=1, source_target_pairs={{4,12},{8,0},{12,20},{16,8},{20,28},{24,16},{28,36},{32,24},{36,44... | collective-permute-start | bytes 6291464 | tf_op jit(solution)/shard_map/ppermute | solution.py:46
  5.0 3.3 %powers.1 = (f32[512,128]{1,0:T(8,128)}, f32[512,128]{1,0:T(8,128)}) custom-call(bf16[2,512,1024]{2,1,0:T(8,128)(2,1)} %get-tuple-element.29.refs_0_.own, bf16[2,512,1024]{2,1,0:T(8,128)(2,1)} %get-tuple-element.30.refs_1_), custom_call_target="tpu_custom_call" | custom-call | flops 1 | bytes 1 | tf_op jit(solution)/shard_map/powers/pallas_call | solution.py:180
  8.3 0.1 fusion.4
  8.4 5.9 %collective-permute-start.5 = (bf16[2,512,1024]{2,1,0:T(8,128)(2,1)}, bf16[2,512,1024]{2,1,0:T(8,128)(2,1)}, u32[]{:S(2)}, u32[]{:S(2)}) collective-permute-start(bf16[2,512,1024]{2,1,0:T(8,128)(2,1)} %collective-permute-done.sib), channel_id=1, source_target_pairs={{0,8},{8,16},{12,4},{16,24},{20,12},{24,32},{28,20},{32,40},{36,28... | collective-permute-start | bytes 6291464 | tf_op jit(solution)/shard_map/ppermute | solution.py:46
  14.3 0.1 fusion.5
  14.5 5.5 %planes.1 = (bf16[2,512,768]{2,1,0:T(8,128)(2,1)}, bf16[2,512,256]{2,1,0:T(8,128)(2,1)}, f32[512,128]{1,0:T(8,128)}, bf16[2,512,768]{2,1,0:T(8,128)(2,1)}, bf16[...) custom-call(s32[1]{0:T(128)} %bitcast.core_ref.core, bf16[1024,2,2048]{2,1,0:T(2,128)(2,1)} %refs_1_, bf16[1024,2,2048]{2,1,0:T(2,128)(2,1)} %refs_1_), custom_call_target="tpu_custom_call" | custom-call | flops 1 | bytes 1 | tf_op jit(solution)/shard_map/planes/pallas_call | solution.py:112
  20.2 0.7 negate_multiply_fusion
  20.9 1.1 add_bitcast_fusion
  22.0 0.2 maximum_reduce_fusion
  22.2 10.6 %psum.7 = f32[2,512]{1,0:T(2,128)S(1)} all-reduce(f32[2,512]{1,0:T(2,128)S(1)} %maximum_reduce_fusion), channel_id=1, replica_groups=mesh['chan'=32,'freq'=4] {'freq'}, use_global_device_ids=true, to_apply=%region_1.2 | all-reduce | flops 1024 | bytes 8192 | tf_op jit(solution)/shard_map/psum | solution.py:350
  32.9 1.3 collective-permute-start.2
  34.3 4.2 %collective-permute-start.4 = (f32[514]{0:T(1024)S(1)}, f32[514]{0:T(1024)S(1)}, u32[]{:S(2)}, u32[]{:S(2)}) collective-permute-start(f32[514]{0:T(1024)S(1)} %collective-permute-done.1), channel_id=1, source_target_pairs={{0,9},{1,10},{2,11},{3,8},{8,17},{9,18},{10,19},{11,16},{12,5},{13... | collective-permute-start | bytes 6176 | tf_op jit(solution)/shard_map/ppermute | solution.py:50
  38.5 1.0 select_reduce_fusion
  39.5 1.2 collective-permute-done.2
  40.7 1.3 collective-permute-start.10
  42.0 16.5 %collective-permute-done.5.from_sib = bf16[2,512,1024]{2,1,0:T(8,128)(2,1)} collective-permute-done((bf16[2,512,1024]{2,1,0:T(8,128)(2,1)}, bf16[2,512,1024]{2,1,0:T(8,128)(2,1)}, u32[]{:S(2)}, u32[]{:S(2)}) %collective-permute-start.5) | collective-permute-done | bytes 2097184 | tf_op jit(solution)/shard_map/ppermute | solution.py:46
  58.5 5.9 %collective-permute-start.11 = (bf16[2,512,768]{2,1,0:T(8,128)(2,1)}, bf16[2,512,768]{2,1,0:T(8,128)(2,1)}, u32[]{:S(2)}, u32[]{:S(2)}) collective-permute-start(bf16[2,512,768]{2,1,0:T(8,128)(2,1)} %collective-permute-done.3.sib), channel_id=1, source_target_pairs={{0,8},{8,16},{12,4},{16,24},{20,12},{24,32},{28,20},{32,40},{36,28... | collective-permute-start | bytes 4718600 | tf_op jit(solution)/shard_map/ppermute | solution.py:46
  64.5 0.6 fusion.6
  66.4 0.6 slice.34
  67.7 0.1 copy.16
  67.9 15.2 %add_pairs.3.refs_3_ = f32[512,1024]{1,0:T(8,128)S(1)} custom-call(s32[1]{0:T(128)} %bitcast.core_ref.core, s32[1,2048]{1,0:T(1,128)S(1)} %bitcast.32, bf16[2,512,1024]{2,1,0:T(8,128)(2,1)S(1)} %copy-done, bf16[2,512,1024]{2,1,0:T(8,128)(2,1)} %collective-permute-done.sib, bf16[2,512,1024]{2,1,0:T(8,128)(2,1)} %collective-permute-done.7.from_own, ...), custom_call_target="tpu_custom_call" | custom-call | flops 1 | bytes 1 | tf_op jit(solution)/shard_map/add_pairs/pallas_call | solution.py:317
  83.1 1.3 collective-permute-start.8
  84.4 4.8 %collective-permute-start.9 = (bf16[2,512,256]{2,1,0:T(8,128)(2,1)S(1)}, bf16[2,512,256]{2,1,0:T(8,128)(2,1)S(1)}, u32[]{:S(2)}, u32[]{:S(2)}) collective-permute-start(bf16[2,512,256]{2,1,0:T(8,128)(2,1)S(1)} %collective-permute-done.6.sib), channel_id=1, source_target_pairs={{0,8},{8,16},{12,4},{16,24},{20,12},{24,32},{28,20},{32,40},{36,28... | collective-permute-start | bytes 1572872 | tf_op jit(solution)/shard_map/ppermute | solution.py:46
  89.3 10.0 %add_pairs.4.refs_3_ = f32[512,1024]{1,0:T(8,128)S(1)} custom-call(s32[1]{0:T(128)} %bitcast.core_ref.core, s32[1,2048]{1,0:T(1,128)S(1)} %bitcast.33, bf16[2,512,768]{2,1,0:T(8,128)(2,1)S(1)} %copy-done.1, bf16[2,512,768]{2,1,0:T(8,128)(2,1)} %collective-permute-done.3.sib, bf16[2,512,768]{2,1,0:T(8,128)(2,1)} %collective-permute-done.10.from_own, ...), custom_call_target="tpu_custom_call" | custom-call | flops 1 | bytes 1 | tf_op jit(solution)/shard_map/add_pairs/pallas_call | solution.py:317
  99.3 3.1 %add_pairs.5 = (f32[64,16,256]{2,1,0:T(8,128)S(1)}, f32[64,16,256]{2,1,0:T(8,128)S(1)}) custom-call(s32[1]{0:T(128)} %bitcast.core_ref.core, s32[1,2048]{1,0:T(1,128)S(1)} %bitcast.34, bf16[2,512,256]{2,1,0:T(8,128)(2,1)S(1)} %copy-done.2, bf16[2,512,256]{2,1,0:T(8,128)(2,1)S(1)} %collective-permute-done.6.sib, ...), custom_call_target="tpu_custom_call" | custom-call | flops 1 | bytes 1 | tf_op jit(solution)/shard_map/add_pairs/pallas_call | solution.py:317
  102.4 0.4 collective-permute-start.12
  102.8 2.4 %collective-permute-done.12 = f32[64,16,256]{2,1,0:T(8,128)S(1)} collective-permute-done((f32[64,16,256]{2,1,0:T(8,128)S(1)}, f32[64,16,256]{2,1,0:T(8,128)S(1)}, u32[]{:S(2)}, u32[]{:S(2)}) %collective-permute-start.12) | collective-permute-done | bytes 1048608 | tf_op jit(solution)/shard_map/ppermute | solution.py:38
  105.1 0.3 add_convert_fusion
  105.4 26.9 %all_to_all.5 = bf16[64,16,256]{2,1,0:T(8,128)(2,1)S(1)} all-to-all(bf16[64,16,256]{2,1,0:T(8,128)(2,1)S(1)} %add_convert_fusion), channel_id=1, replica_groups={{0,1,2,3,8,9,10,11,16,17,18,19,24,25,26,27,32,33,34,35,40,41,42,43,48,4..., dimensions={0} | all-to-all | bytes 1048576 | tf_op jit(solution)/shard_map/all_to_all | solution.py:409
  132.3 0.7 convert_reduce_fusion
  (50 shorter events, 0.6 us)
Async XLA Ops:
  3.5 4.9 %collective-permute-start = (bf16[2,512,1024]{2,1,0:T(8,128)(2,1)}, bf16[2,512,1024]{2,1,0:T(8,128)(2,1)}, u32[]{:S(2)}, u32[]{:S(2)}) collective-permute-start(bf16[2,512,1024]{2,1,0:T(8,128)(2,1)} %get-tuple-element.30.refs_1_), channel_id=1, source_target_pairs={{0,4},{4,0},{8,12},{12,8},{16,20},{20,16},{24,28},{28,24},{32,36},... | collective-permute-start | bytes 6291464 | tf_op jit(solution)/shard_map/ppermute | solution.py:38
  3.5 4.7 %copy-start.5 = (s32[32768]{0:T(1024)S(1)}, s32[32768]{0:T(1024)}, u32[]{:S(2)}) copy-start(s32[32768]{0:T(1024)} %param.5) | copy-start | bytes 393220
  3.6 64.3 %collective-permute-start.7 = (bf16[2,512,1024]{2,1,0:T(8,128)(2,1)}, bf16[2,512,1024]{2,1,0:T(8,128)(2,1)}, u32[]{:S(2)}, u32[]{:S(2)}) collective-permute-start(bf16[2,512,1024]{2,1,0:T(8,128)(2,1)} %get-tuple-element.29.refs_0_.own), channel_id=1, source_target_pairs={{4,12},{8,0},{12,20},{16,8},{20,28},{24,16},{28,36},{32,24},{36,44... | collective-permute-start | bytes 6291464 | tf_op jit(solution)/shard_map/ppermute | solution.py:46
  8.4 50.1 %collective-permute-start.5 = (bf16[2,512,1024]{2,1,0:T(8,128)(2,1)}, bf16[2,512,1024]{2,1,0:T(8,128)(2,1)}, u32[]{:S(2)}, u32[]{:S(2)}) collective-permute-start(bf16[2,512,1024]{2,1,0:T(8,128)(2,1)} %collective-permute-done.sib), channel_id=1, source_target_pairs={{0,8},{8,16},{12,4},{16,24},{20,12},{24,32},{28,20},{32,40},{36,28... | collective-permute-start | bytes 6291464 | tf_op jit(solution)/shard_map/ppermute | solution.py:46
  14.4 5.7 %copy-start.7 = (s32[1,2]{1,0:T(1,128)S(1)}, s32[1,2]{1,0:T(1,128)}, u32[]{:S(2)}) copy-start(s32[1,2]{1,0:T(1,128)} %param.7) | copy-start | bytes 28
  14.4 6.5 %copy-start.3 = (f32[512,128]{1,0:T(8,128)S(1)}, f32[512,128]{1,0:T(8,128)}, u32[]{:S(2)}) copy-start(f32[512,128]{1,0:T(8,128)} %get-tuple-element.31) | copy-start | bytes 786436
  14.5 6.5 %copy-start.4 = (f32[512,128]{1,0:T(8,128)S(1)}, f32[512,128]{1,0:T(8,128)}, u32[]{:S(2)}) copy-start(f32[512,128]{1,0:T(8,128)} %get-tuple-element.34) | copy-start | bytes 786436
  20.0 18.5 %copy-start.6 = (s32[512]{0:T(512)S(1)}, s32[512]{0:T(512)}, u32[]{:S(2)}) copy-start(s32[512]{0:T(512)} %param.6) | copy-start | bytes 6148
  20.0 47.9 %copy-start = (bf16[2,512,1024]{2,1,0:T(8,128)(2,1)S(1)}, bf16[2,512,1024]{2,1,0:T(8,128)(2,1)}, u32[]{:S(2)}) copy-start(bf16[2,512,1024]{2,1,0:T(8,128)(2,1)} %get-tuple-element.29.refs_0_.own) | copy-start | bytes 6291460
  20.0 22.0 %collective-permute-start.3 = (bf16[2,512,768]{2,1,0:T(8,128)(2,1)}, bf16[2,512,768]{2,1,0:T(8,128)(2,1)}, u32[]{:S(2)}, u32[]{:S(2)}) collective-permute-start(bf16[2,512,768]{2,1,0:T(8,128)(2,1)} %get-tuple-element.38), channel_id=1, source_target_pairs={{0,4},{4,0},{8,12},{12,8},{16,20},{20,16},{24,28},{28,24},{32,36},... | collective-permute-start | bytes 4718600 | tf_op jit(solution)/shard_map/ppermute | solution.py:38
  32.8 1.4 %collective-permute-start.1 = (f32[514]{0:T(1024)S(1)}, f32[514]{0:T(1024)S(1)}, u32[]{:S(2)}, u32[]{:S(2)}) collective-permute-start(f32[514]{0:T(1024)S(1)} %get-tuple-element.70), channel_id=1, source_target_pairs={{0,4},{4,0},{8,12},{12,8},{16,20},{20,16},{24,28},{28,24},{32,36},... | collective-permute-start | bytes 6176 | tf_op jit(solution)/shard_map/ppermute | solution.py:38
  32.9 7.7 %collective-permute-start.2 = (f32[514]{0:T(1024)S(1)}, f32[514]{0:T(1024)S(1)}, u32[]{:S(2)}, u32[]{:S(2)}) collective-permute-start(f32[514]{0:T(1024)S(1)} %get-tuple-element.71), channel_id=1, source_target_pairs={{4,13},{5,14},{6,15},{7,12},{8,1},{9,2},{10,3},{11,0},{12,21},{13,... | collective-permute-start | bytes 6176 | tf_op jit(solution)/shard_map/ppermute | solution.py:50
  34.3 6.4 %collective-permute-start.4 = (f32[514]{0:T(1024)S(1)}, f32[514]{0:T(1024)S(1)}, u32[]{:S(2)}, u32[]{:S(2)}) collective-permute-start(f32[514]{0:T(1024)S(1)} %collective-permute-done.1), channel_id=1, source_target_pairs={{0,9},{1,10},{2,11},{3,8},{8,17},{9,18},{10,19},{11,16},{12,5},{13... | collective-permute-start | bytes 6176 | tf_op jit(solution)/shard_map/ppermute | solution.py:50
  40.7 42.4 %collective-permute-start.6 = (bf16[2,512,256]{2,1,0:T(8,128)(2,1)}, bf16[2,512,256]{2,1,0:T(8,128)(2,1)S(1)}, u32[]{:S(2)}, u32[]{:S(2)}) collective-permute-start(bf16[2,512,256]{2,1,0:T(8,128)(2,1)} %get-tuple-element.41), channel_id=1, source_target_pairs={{0,4},{4,0},{8,12},{12,8},{16,20},{20,16},{24,28},{28,24},{32,36},... | collective-permute-start | bytes 1572872 | tf_op jit(solution)/shard_map/ppermute | solution.py:38
  40.7 48.5 %collective-permute-start.10 = (bf16[2,512,768]{2,1,0:T(8,128)(2,1)}, bf16[2,512,768]{2,1,0:T(8,128)(2,1)}, u32[]{:S(2)}, u32[]{:S(2)}) collective-permute-start(bf16[2,512,768]{2,1,0:T(8,128)(2,1)} %get-tuple-element.48.own), channel_id=1, source_target_pairs={{4,12},{8,0},{12,20},{16,8},{20,28},{24,16},{28,36},{32,24},{36,44... | collective-permute-start | bytes 4718600 | tf_op jit(solution)/shard_map/ppermute | solution.py:46
  58.5 30.7 %collective-permute-start.11 = (bf16[2,512,768]{2,1,0:T(8,128)(2,1)}, bf16[2,512,768]{2,1,0:T(8,128)(2,1)}, u32[]{:S(2)}, u32[]{:S(2)}) collective-permute-start(bf16[2,512,768]{2,1,0:T(8,128)(2,1)} %collective-permute-done.3.sib), channel_id=1, source_target_pairs={{0,8},{8,16},{12,4},{16,24},{20,12},{24,32},{28,20},{32,40},{36,28... | collective-permute-start | bytes 4718600 | tf_op jit(solution)/shard_map/ppermute | solution.py:46
  67.9 15.2 %copy-start.2 = (bf16[2,512,256]{2,1,0:T(8,128)(2,1)S(1)}, bf16[2,512,256]{2,1,0:T(8,128)(2,1)}, u32[]{:S(2)}) copy-start(bf16[2,512,256]{2,1,0:T(8,128)(2,1)} %get-tuple-element.46.own) | copy-start | bytes 1572868
  67.9 21.4 %copy-start.1 = (bf16[2,512,768]{2,1,0:T(8,128)(2,1)S(1)}, bf16[2,512,768]{2,1,0:T(8,128)(2,1)}, u32[]{:S(2)}) copy-start(bf16[2,512,768]{2,1,0:T(8,128)(2,1)} %get-tuple-element.48.own) | copy-start | bytes 4718596
  83.1 16.2 %collective-permute-start.8 = (bf16[2,512,256]{2,1,0:T(8,128)(2,1)S(1)}, bf16[2,512,256]{2,1,0:T(8,128)(2,1)S(1)}, u32[]{:S(2)}, u32[]{:S(2)}) collective-permute-start(bf16[2,512,256]{2,1,0:T(8,128)(2,1)S(1)} %copy-done.2), channel_id=1, source_target_pairs={{4,12},{8,0},{12,20},{16,8},{20,28},{24,16},{28,36},{32,24},{36,44... | collective-permute-start | bytes 1572872 | tf_op jit(solution)/shard_map/ppermute | solution.py:46
  84.4 14.9 %collective-permute-start.9 = (bf16[2,512,256]{2,1,0:T(8,128)(2,1)S(1)}, bf16[2,512,256]{2,1,0:T(8,128)(2,1)S(1)}, u32[]{:S(2)}, u32[]{:S(2)}) collective-permute-start(bf16[2,512,256]{2,1,0:T(8,128)(2,1)S(1)} %collective-permute-done.6.sib), channel_id=1, source_target_pairs={{0,8},{8,16},{12,4},{16,24},{20,12},{24,32},{28,20},{32,40},{36,28... | collective-permute-start | bytes 1572872 | tf_op jit(solution)/shard_map/ppermute | solution.py:46
  102.4 2.7 %collective-permute-start.12 = (f32[64,16,256]{2,1,0:T(8,128)S(1)}, f32[64,16,256]{2,1,0:T(8,128)S(1)}, u32[]{:S(2)}, u32[]{:S(2)}) collective-permute-start(f32[64,16,256]{2,1,0:T(8,128)S(1)} %get-tuple-element.52), channel_id=1, source_target_pairs={{0,4},{4,0},{8,12},{12,8},{16,20},{20,16},{24,28},{28,24},{32,36},... | collective-permute-start | bytes 3145736 | tf_op jit(solution)/shard_map/ppermute | solution.py:38

commit v8 on v7

--- a/solution.py
+++ b/solution.py
@@ -212,13 +212,15 @@
     step = pl.program_id(0)
     count = own.shape[1] // len(refs)
 
-    @pl.when(step == 0)
-    def _():
-        bins, pairs = onehot.shape
-        for k in range(0, pairs, 256):
-            bin_row = lax.broadcasted_iota(jnp.int32, (bins, 256), 0)
+    def fill_onehot(start, stop):
+        for k in range(start, stop, 256):
+            bin_row = lax.broadcasted_iota(jnp.int32, (onehot.shape[0], 256), 0)
             hit = bin_row == row_ref[:, k : k + 256]
             onehot[:, k : k + 256] = jnp.where(hit, 1.0, 0.0).astype(jnp.bfloat16)
+
+    one_step = is_last and CUTS[-1] == TILE
+    if not one_step:
+        pl.when(step == 0)(lambda: fill_onehot(0, onehot.shape[1]))
 
     def fill_table():
         tiles = cos_ref.shape[0] - TILE // FINE - FINE
@@ -259,6 +261,8 @@
         for part, prods in enumerate(refs):
             products(prods, part * count, *blocks)
             pairs = slice(part * 4 * count, (part + 1) * 4 * count)
+            if one_step:
+                fill_onehot(pairs.start, pairs.stop)
             sums = jnp.dot(onehot[:, pairs], prods[...], preferred_element_type=jnp.float32)
             stack = sums if stack is None else stack + sums
         high = stack.astype(jnp.bfloat16)

time: 133 us -> 133 us (level)
  no operation moved by 1% of the time
where the time goes in v8:
time: 133 us
  Pallas kernels  40.3 us (30%)
  blocking collectives  37.5 us (28%)
  starting transfers between devices  26.8 us (20%)
  waiting for transfers between devices  20.1 us (15%)
  other arithmetic  4.46 us (3%)
  between operations  2.22 us (2%)
  local copies, waits for them, and re-layouts  1.45 us (1%)
    pallas_call x3, Pallas kernels, add_pairs(): pl.pallas_call(functools.partial(pairs_kernel, first, is_last), grid=(cut...  28.1 us
    all_to_all x1, blocking collectives, shards(): lax.all_to_all(total, ('chan', 'freq'), 0, 0, axis_index_groups=ways, til...  26.9 us
    ppermute x6, starting transfers between devices, to_chips(): return lax.ppermute(block, 'chan', route)  20.6 us
    ppermute x6, waiting for transfers between devices, to_chips(): return lax.ppermute(block, 'chan', route)  16.5 us
    psum x1, blocking collectives, shards(): lax.psum(jnp.sum(jnp.stack([own_power, give_power]), axis=2), 'freq')  10.6 us
    ppermute x2, starting transfers between devices, to_chips(): return lax.ppermute(block, ('chan', 'freq'), route)  5.52 us
    pallas_call x1, Pallas kernels, planes(): pl.pallas_call(functools.partial(planes_kernel, int(with_power)), grid_sp...  5.5 us
    pallas_call x1, Pallas kernels, head_planes(): pl.pallas_call(head_kernel, in_specs=[pl.BlockSpec(memory_space=pltpu.SME...  3.44 us
  transfers between devices with their start and end apart: 13, of which 3 were waited for; matrix products, arithmetic and copies ran while one was open for 4% of the time, Pallas kernels for 26%

profile of v8, /device:TPU:0, one launch (start us, length us, event | category | flops | bytes accessed | tf_op | source)
XLA Modules:
  0.0 132.9 jit_solution(1564213558142675959)
XLA Ops:
  0.0 3.4 %head_planes.1 = (bf16[2,512,1024]{2,1,0:T(8,128)(2,1)}, bf16[2,512,1024]{2,1,0:T(8,128)(2,1)}) custom-call(s32[1]{0:T(128)} %bitcast.core_ref.core, bf16[1024,2,2048]{2,1,0:T(2,128)(2,1)} %refs_1_), custom_call_target="tpu_custom_call" | custom-call | flops 1 | bytes 1 | tf_op jit(solution)/shard_map/head_planes/pallas_call | solution.py:153
  3.5 0.1 collective-permute-start
  3.6 1.4 %collective-permute-start.7 = (bf16[2,512,1024]{2,1,0:T(8,128)(2,1)}, bf16[2,512,1024]{2,1,0:T(8,128)(2,1)}, u32[]{:S(2)}, u32[]{:S(2)}) collective-permute-start(bf16[2,512,1024]{2,1,0:T(8,128)(2,1)} %get-tuple-element.29.refs_0_.own), channel_id=1, source_target_pairs={{4,12},{8,0},{12,20},{16,8},{20,28},{24,16},{28,36},{32,24},{36,44... | collective-permute-start | bytes 6291464 | tf_op jit(solution)/shard_map/ppermute | solution.py:46
  5.0 3.3 %powers.1 = (f32[512,128]{1,0:T(8,128)}, f32[512,128]{1,0:T(8,128)}) custom-call(bf16[2,512,1024]{2,1,0:T(8,128)(2,1)} %get-tuple-element.29.refs_0_.own, bf16[2,512,1024]{2,1,0:T(8,128)(2,1)} %get-tuple-element.30.refs_1_), custom_call_target="tpu_custom_call" | custom-call | flops 1 | bytes 1 | tf_op jit(solution)/shard_map/powers/pallas_call | solution.py:180
  8.3 0.1 fusion.4
  8.4 5.9 %collective-permute-start.5 = (bf16[2,512,1024]{2,1,0:T(8,128)(2,1)}, bf16[2,512,1024]{2,1,0:T(8,128)(2,1)}, u32[]{:S(2)}, u32[]{:S(2)}) collective-permute-start(bf16[2,512,1024]{2,1,0:T(8,128)(2,1)} %collective-permute-done.sib), channel_id=1, source_target_pairs={{0,8},{8,16},{12,4},{16,24},{20,12},{24,32},{28,20},{32,40},{36,28... | collective-permute-start | bytes 6291464 | tf_op jit(solution)/shard_map/ppermute | solution.py:46
  14.3 0.1 fusion.5
  14.5 5.5 %planes.1 = (bf16[2,512,768]{2,1,0:T(8,128)(2,1)}, bf16[2,512,256]{2,1,0:T(8,128)(2,1)}, f32[512,128]{1,0:T(8,128)}, bf16[2,512,768]{2,1,0:T(8,128)(2,1)}, bf16[...) custom-call(s32[1]{0:T(128)} %bitcast.core_ref.core, bf16[1024,2,2048]{2,1,0:T(2,128)(2,1)} %refs_1_, bf16[1024,2,2048]{2,1,0:T(2,128)(2,1)} %refs_1_), custom_call_target="tpu_custom_call" | custom-call | flops 1 | bytes 1 | tf_op jit(solution)/shard_map/planes/pallas_call | solution.py:112
  20.2 0.7 negate_multiply_fusion
  20.9 1.1 add_bitcast_fusion
  22.0 0.2 maximum_reduce_fusion
  22.2 10.6 %psum.7 = f32[2,512]{1,0:T(2,128)S(1)} all-reduce(f32[2,512]{1,0:T(2,128)S(1)} %maximum_reduce_fusion), channel_id=1, replica_groups=mesh['chan'=32,'freq'=4] {'freq'}, use_global_device_ids=true, to_apply=%region_1.2 | all-reduce | flops 1024 | bytes 8192 | tf_op jit(solution)/shard_map/psum | solution.py:354
  32.9 1.3 collective-permute-start.2
  34.3 4.2 %collective-permute-start.4 = (f32[514]{0:T(1024)S(1)}, f32[514]{0:T(1024)S(1)}, u32[]{:S(2)}, u32[]{:S(2)}) collective-permute-start(f32[514]{0:T(1024)S(1)} %collective-permute-done.1), channel_id=1, source_target_pairs={{0,9},{1,10},{2,11},{3,8},{8,17},{9,18},{10,19},{11,16},{12,5},{13... | collective-permute-start | bytes 6176 | tf_op jit(solution)/shard_map/ppermute | solution.py:50
  38.5 1.0 select_reduce_fusion
  39.5 1.2 collective-permute-done.2
  40.7 1.3 collective-permute-start.10
  42.0 16.5 %collective-permute-done.5.from_sib = bf16[2,512,1024]{2,1,0:T(8,128)(2,1)} collective-permute-done((bf16[2,512,1024]{2,1,0:T(8,128)(2,1)}, bf16[2,512,1024]{2,1,0:T(8,128)(2,1)}, u32[]{:S(2)}, u32[]{:S(2)}) %collective-permute-start.5) | collective-permute-done | bytes 2097184 | tf_op jit(solution)/shard_map/ppermute | solution.py:46
  58.5 5.9 %collective-permute-start.11 = (bf16[2,512,768]{2,1,0:T(8,128)(2,1)}, bf16[2,512,768]{2,1,0:T(8,128)(2,1)}, u32[]{:S(2)}, u32[]{:S(2)}) collective-permute-start(bf16[2,512,768]{2,1,0:T(8,128)(2,1)} %collective-permute-done.3.sib), channel_id=1, source_target_pairs={{0,8},{8,16},{12,4},{16,24},{20,12},{24,32},{28,20},{32,40},{36,28... | collective-permute-start | bytes 4718600 | tf_op jit(solution)/shard_map/ppermute | solution.py:46
  64.5 0.6 fusion.6
  66.4 0.6 slice.34
  67.7 0.1 copy.16
  67.9 15.2 %add_pairs.3.refs_3_ = f32[512,1024]{1,0:T(8,128)S(1)} custom-call(s32[1]{0:T(128)} %bitcast.core_ref.core, s32[1,2048]{1,0:T(1,128)S(1)} %bitcast.32, bf16[2,512,1024]{2,1,0:T(8,128)(2,1)S(1)} %copy-done, bf16[2,512,1024]{2,1,0:T(8,128)(2,1)} %collective-permute-done.sib, bf16[2,512,1024]{2,1,0:T(8,128)(2,1)} %collective-permute-done.7.from_own, ...), custom_call_target="tpu_custom_call" | custom-call | flops 1 | bytes 1 | tf_op jit(solution)/shard_map/add_pairs/pallas_call | solution.py:321
  83.1 1.3 collective-permute-start.8
  84.4 4.8 %collective-permute-start.9 = (bf16[2,512,256]{2,1,0:T(8,128)(2,1)S(1)}, bf16[2,512,256]{2,1,0:T(8,128)(2,1)S(1)}, u32[]{:S(2)}, u32[]{:S(2)}) collective-permute-start(bf16[2,512,256]{2,1,0:T(8,128)(2,1)S(1)} %collective-permute-done.6.sib), channel_id=1, source_target_pairs={{0,8},{8,16},{12,4},{16,24},{20,12},{24,32},{28,20},{32,40},{36,28... | collective-permute-start | bytes 1572872 | tf_op jit(solution)/shard_map/ppermute | solution.py:46
  89.3 10.0 %add_pairs.4.refs_3_ = f32[512,1024]{1,0:T(8,128)S(1)} custom-call(s32[1]{0:T(128)} %bitcast.core_ref.core, s32[1,2048]{1,0:T(1,128)S(1)} %bitcast.33, bf16[2,512,768]{2,1,0:T(8,128)(2,1)S(1)} %copy-done.1, bf16[2,512,768]{2,1,0:T(8,128)(2,1)} %collective-permute-done.3.sib, bf16[2,512,768]{2,1,0:T(8,128)(2,1)} %collective-permute-done.10.from_own, ...), custom_call_target="tpu_custom_call" | custom-call | flops 1 | bytes 1 | tf_op jit(solution)/shard_map/add_pairs/pallas_call | solution.py:321
  99.3 2.9 %add_pairs.5 = (f32[64,16,256]{2,1,0:T(8,128)S(1)}, f32[64,16,256]{2,1,0:T(8,128)S(1)}) custom-call(s32[1]{0:T(128)} %bitcast.core_ref.core, s32[1,2048]{1,0:T(1,128)S(1)} %bitcast.34, bf16[2,512,256]{2,1,0:T(8,128)(2,1)S(1)} %copy-done.2, bf16[2,512,256]{2,1,0:T(8,128)(2,1)S(1)} %collective-permute-done.6.sib, ...), custom_call_target="tpu_custom_call" | custom-call | flops 1 | bytes 1 | tf_op jit(solution)/shard_map/add_pairs/pallas_call | solution.py:321
  102.2 0.4 collective-permute-start.12
  102.6 2.4 %collective-permute-done.12 = f32[64,16,256]{2,1,0:T(8,128)S(1)} collective-permute-done((f32[64,16,256]{2,1,0:T(8,128)S(1)}, f32[64,16,256]{2,1,0:T(8,128)S(1)}, u32[]{:S(2)}, u32[]{:S(2)}) %collective-permute-start.12) | collective-permute-done | bytes 1048608 | tf_op jit(solution)/shard_map/ppermute | solution.py:38
  105.0 0.3 add_convert_fusion
  105.2 26.9 %all_to_all.5 = bf16[64,16,256]{2,1,0:T(8,128)(2,1)S(1)} all-to-all(bf16[64,16,256]{2,1,0:T(8,128)(2,1)S(1)} %add_convert_fusion), channel_id=1, replica_groups={{0,1,2,3,8,9,10,11,16,17,18,19,24,25,26,27,32,33,34,35,40,41,42,43,48,4..., dimensions={0} | all-to-all | bytes 1048576 | tf_op jit(solution)/shard_map/all_to_all | solution.py:413
  132.2 0.7 convert_reduce_fusion
  (50 shorter events, 0.6 us)
Async XLA Ops:
  3.5 4.9 %collective-permute-start = (bf16[2,512,1024]{2,1,0:T(8,128)(2,1)}, bf16[2,512,1024]{2,1,0:T(8,128)(2,1)}, u32[]{:S(2)}, u32[]{:S(2)}) collective-permute-start(bf16[2,512,1024]{2,1,0:T(8,128)(2,1)} %get-tuple-element.30.refs_1_), channel_id=1, source_target_pairs={{0,4},{4,0},{8,12},{12,8},{16,20},{20,16},{24,28},{28,24},{32,36},... | collective-permute-start | bytes 6291464 | tf_op jit(solution)/shard_map/ppermute | solution.py:38
  3.5 4.7 %copy-start.5 = (s32[32768]{0:T(1024)S(1)}, s32[32768]{0:T(1024)}, u32[]{:S(2)}) copy-start(s32[32768]{0:T(1024)} %param.5) | copy-start | bytes 393220
  3.6 64.3 %collective-permute-start.7 = (bf16[2,512,1024]{2,1,0:T(8,128)(2,1)}, bf16[2,512,1024]{2,1,0:T(8,128)(2,1)}, u32[]{:S(2)}, u32[]{:S(2)}) collective-permute-start(bf16[2,512,1024]{2,1,0:T(8,128)(2,1)} %get-tuple-element.29.refs_0_.own), channel_id=1, source_target_pairs={{4,12},{8,0},{12,20},{16,8},{20,28},{24,16},{28,36},{32,24},{36,44... | collective-permute-start | bytes 6291464 | tf_op jit(solution)/shard_map/ppermute | solution.py:46
  8.4 50.1 %collective-permute-start.5 = (bf16[2,512,1024]{2,1,0:T(8,128)(2,1)}, bf16[2,512,1024]{2,1,0:T(8,128)(2,1)}, u32[]{:S(2)}, u32[]{:S(2)}) collective-permute-start(bf16[2,512,1024]{2,1,0:T(8,128)(2,1)} %collective-permute-done.sib), channel_id=1, source_target_pairs={{0,8},{8,16},{12,4},{16,24},{20,12},{24,32},{28,20},{32,40},{36,28... | collective-permute-start | bytes 6291464 | tf_op jit(solution)/shard_map/ppermute | solution.py:46
  14.4 5.7 %copy-start.7 = (s32[1,2]{1,0:T(1,128)S(1)}, s32[1,2]{1,0:T(1,128)}, u32[]{:S(2)}) copy-start(s32[1,2]{1,0:T(1,128)} %param.7) | copy-start | bytes 28
  14.4 6.5 %copy-start.3 = (f32[512,128]{1,0:T(8,128)S(1)}, f32[512,128]{1,0:T(8,128)}, u32[]{:S(2)}) copy-start(f32[512,128]{1,0:T(8,128)} %get-tuple-element.31) | copy-start | bytes 786436
  14.5 6.5 %copy-start.4 = (f32[512,128]{1,0:T(8,128)S(1)}, f32[512,128]{1,0:T(8,128)}, u32[]{:S(2)}) copy-start(f32[512,128]{1,0:T(8,128)} %get-tuple-element.34) | copy-start | bytes 786436
  20.0 18.5 %copy-start.6 = (s32[512]{0:T(512)S(1)}, s32[512]{0:T(512)}, u32[]{:S(2)}) copy-start(s32[512]{0:T(512)} %param.6) | copy-start | bytes 6148
  20.0 47.9 %copy-start = (bf16[2,512,1024]{2,1,0:T(8,128)(2,1)S(1)}, bf16[2,512,1024]{2,1,0:T(8,128)(2,1)}, u32[]{:S(2)}) copy-start(bf16[2,512,1024]{2,1,0:T(8,128)(2,1)} %get-tuple-element.29.refs_0_.own) | copy-start | bytes 6291460
  20.0 22.0 %collective-permute-start.3 = (bf16[2,512,768]{2,1,0:T(8,128)(2,1)}, bf16[2,512,768]{2,1,0:T(8,128)(2,1)}, u32[]{:S(2)}, u32[]{:S(2)}) collective-permute-start(bf16[2,512,768]{2,1,0:T(8,128)(2,1)} %get-tuple-element.38), channel_id=1, source_target_pairs={{0,4},{4,0},{8,12},{12,8},{16,20},{20,16},{24,28},{28,24},{32,36},... | collective-permute-start | bytes 4718600 | tf_op jit(solution)/shard_map/ppermute | solution.py:38
  32.8 1.4 %collective-permute-start.1 = (f32[514]{0:T(1024)S(1)}, f32[514]{0:T(1024)S(1)}, u32[]{:S(2)}, u32[]{:S(2)}) collective-permute-start(f32[514]{0:T(1024)S(1)} %get-tuple-element.70), channel_id=1, source_target_pairs={{0,4},{4,0},{8,12},{12,8},{16,20},{20,16},{24,28},{28,24},{32,36},... | collective-permute-start | bytes 6176 | tf_op jit(solution)/shard_map/ppermute | solution.py:38
  32.9 7.7 %collective-permute-start.2 = (f32[514]{0:T(1024)S(1)}, f32[514]{0:T(1024)S(1)}, u32[]{:S(2)}, u32[]{:S(2)}) collective-permute-start(f32[514]{0:T(1024)S(1)} %get-tuple-element.71), channel_id=1, source_target_pairs={{4,13},{5,14},{6,15},{7,12},{8,1},{9,2},{10,3},{11,0},{12,21},{13,... | collective-permute-start | bytes 6176 | tf_op jit(solution)/shard_map/ppermute | solution.py:50
  34.3 6.4 %collective-permute-start.4 = (f32[514]{0:T(1024)S(1)}, f32[514]{0:T(1024)S(1)}, u32[]{:S(2)}, u32[]{:S(2)}) collective-permute-start(f32[514]{0:T(1024)S(1)} %collective-permute-done.1), channel_id=1, source_target_pairs={{0,9},{1,10},{2,11},{3,8},{8,17},{9,18},{10,19},{11,16},{12,5},{13... | collective-permute-start | bytes 6176 | tf_op jit(solution)/shard_map/ppermute | solution.py:50
  40.7 42.4 %collective-permute-start.6 = (bf16[2,512,256]{2,1,0:T(8,128)(2,1)}, bf16[2,512,256]{2,1,0:T(8,128)(2,1)S(1)}, u32[]{:S(2)}, u32[]{:S(2)}) collective-permute-start(bf16[2,512,256]{2,1,0:T(8,128)(2,1)} %get-tuple-element.41), channel_id=1, source_target_pairs={{0,4},{4,0},{8,12},{12,8},{16,20},{20,16},{24,28},{28,24},{32,36},... | collective-permute-start | bytes 1572872 | tf_op jit(solution)/shard_map/ppermute | solution.py:38
  40.7 48.5 %collective-permute-start.10 = (bf16[2,512,768]{2,1,0:T(8,128)(2,1)}, bf16[2,512,768]{2,1,0:T(8,128)(2,1)}, u32[]{:S(2)}, u32[]{:S(2)}) collective-permute-start(bf16[2,512,768]{2,1,0:T(8,128)(2,1)} %get-tuple-element.48.own), channel_id=1, source_target_pairs={{4,12},{8,0},{12,20},{16,8},{20,28},{24,16},{28,36},{32,24},{36,44... | collective-permute-start | bytes 4718600 | tf_op jit(solution)/shard_map/ppermute | solution.py:46
  58.5 30.7 %collective-permute-start.11 = (bf16[2,512,768]{2,1,0:T(8,128)(2,1)}, bf16[2,512,768]{2,1,0:T(8,128)(2,1)}, u32[]{:S(2)}, u32[]{:S(2)}) collective-permute-start(bf16[2,512,768]{2,1,0:T(8,128)(2,1)} %collective-permute-done.3.sib), channel_id=1, source_target_pairs={{0,8},{8,16},{12,4},{16,24},{20,12},{24,32},{28,20},{32,40},{36,28... | collective-permute-start | bytes 4718600 | tf_op jit(solution)/shard_map/ppermute | solution.py:46
  67.9 15.2 %copy-start.2 = (bf16[2,512,256]{2,1,0:T(8,128)(2,1)S(1)}, bf16[2,512,256]{2,1,0:T(8,128)(2,1)}, u32[]{:S(2)}) copy-start(bf16[2,512,256]{2,1,0:T(8,128)(2,1)} %get-tuple-element.46.own) | copy-start | bytes 1572868
  67.9 21.4 %copy-start.1 = (bf16[2,512,768]{2,1,0:T(8,128)(2,1)S(1)}, bf16[2,512,768]{2,1,0:T(8,128)(2,1)}, u32[]{:S(2)}) copy-start(bf16[2,512,768]{2,1,0:T(8,128)(2,1)} %get-tuple-element.48.own) | copy-start | bytes 4718596
  83.1 16.2 %collective-permute-start.8 = (bf16[2,512,256]{2,1,0:T(8,128)(2,1)S(1)}, bf16[2,512,256]{2,1,0:T(8,128)(2,1)S(1)}, u32[]{:S(2)}, u32[]{:S(2)}) collective-permute-start(bf16[2,512,256]{2,1,0:T(8,128)(2,1)S(1)} %copy-done.2), channel_id=1, source_target_pairs={{4,12},{8,0},{12,20},{16,8},{20,28},{24,16},{28,36},{32,24},{36,44... | collective-permute-start | bytes 1572872 | tf_op jit(solution)/shard_map/ppermute | solution.py:46
  84.4 14.9 %collective-permute-start.9 = (bf16[2,512,256]{2,1,0:T(8,128)(2,1)S(1)}, bf16[2,512,256]{2,1,0:T(8,128)(2,1)S(1)}, u32[]{:S(2)}, u32[]{:S(2)}) collective-permute-start(bf16[2,512,256]{2,1,0:T(8,128)(2,1)S(1)} %collective-permute-done.6.sib), channel_id=1, source_target_pairs={{0,8},{8,16},{12,4},{16,24},{20,12},{24,32},{28,20},{32,40},{36,28... | collective-permute-start | bytes 1572872 | tf_op jit(solution)/shard_map/ppermute | solution.py:46
  102.2 2.7 %collective-permute-start.12 = (f32[64,16,256]{2,1,0:T(8,128)S(1)}, f32[64,16,256]{2,1,0:T(8,128)S(1)}, u32[]{:S(2)}, u32[]{:S(2)}) collective-permute-start(f32[64,16,256]{2,1,0:T(8,128)S(1)} %get-tuple-element.52), channel_id=1, source_target_pairs={{0,4},{4,0},{8,12},{12,8},{16,20},{20,16},{24,28},{28,24},{32,36},... | collective-permute-start | bytes 3145736 | tf_op jit(solution)/shard_map/ppermute | solution.py:38
